TPU v7x, 32 devices: a whole 2x2x4 slice. The times are simulated.
32 devices in a mesh: lon: 4 (over z), lat: 8 (over y, x, core).
Axes of the slice: x: 2, y: 2, z: 4, core: 2. Of those that a mesh axis runs over, the one named last changes fastest.
Arguments:
- free_elevation: float32 [128, 1024], P('lat', 'lon'), may hold values from -3 to 3
- zonal_volume_carriage: float32 [128, 1024], P('lat', 'lon'), may hold values from -2 to 2
- meridional_volume_carriage: float32 [128, 1024], P('lat', 'lon'), may hold values from -2 to 2
- thermal_field: float32 [60, 128, 1024], P(None, 'lat', 'lon'), may hold values from -6 to 6
- flooded_strata_number: int32 [128, 1024], P('lat', 'lon'), may hold values from 0 to 60, as said below
- aerial_exchanges: float32 [5, 64, 512], P(None, 'lat', 'lon'), may hold values from -6 to 6
- aerial_terrain_flags: int32 [64, 512], P('lat', 'lon'), may hold values 0 or 1
- donor_tile_number: int32 [4, 128, 8], P(None, 'lat', 'lon'), may hold values from 0 to 23
- donor_point_number: int32 [4, 128, 1024], P(None, 'lat', 'lon'), may hold values from 0 to 127
- pairing_coefficients: float32 [4, 128, 1024], P(None, 'lat', 'lon'), may hold values from 0 to 0.5
Outputs:
- advanced_elevation: float32 [128, 1024], P('lat', 'lon')
- transport_x_next: float32 [128, 1024], P('lat', 'lon')
- transport_y_next: float32 [128, 1024], P('lat', 'lon')
- advanced_thermal_field: float32 [60, 128, 1024], P(None, 'lat', 'lon')
- marine_skin_condition: float32 [4, 64, 512], P(None, 'lat', 'lon')
Inputs may be any that keep to these rules, and one draw needn't show every extreme that they name: flooded_strata_number is 0 on land; wet columns hold 1 to 60 levels. donor_tile_number // 8 - 1 is the source tile's offset in latitude and donor_tile_number mod 8 the source block (row) within it; the longitude tile is the target's.
All inputs are finite; a program needn't handle non-finite values. No bound on the sum of `aerial_terrain_flags` on one device may be relied on, other than what follows from the above.
Results may differ from a plain program's by a relative error of at most 0.0003.
Values sent between devices are 32-bit elements; how exact they have to be, the bound alone decides.
No kernel may reach another device: no remote copies, remote signals or barrier semaphores. Data moves between devices by JAX's collectives and lax.ppermute only.
A program may use at most 64 MiB of HBM per device.

v0:
```python
import math

import jax
import jax.numpy as jnp
from jax import lax
from jax.sharding import PartitionSpec as P

SUBS = 3


grav_step = 0.6
height_step = 0.6
wind_step = 0.5
fresh_step = 0.5
mixing_fourth = 0.02
advect_coef = 0.1
diapycnal_diffusion = 0.2
heat_gain = 0.3
light_gain = 0.3
light_decay = 8.0
depth_floor = 0.25
area_floor = 1.0


def padded_2(block, sides, width, periodic):
    for axis, dim in sides:
        count = lax.axis_size(axis)
        forward = [(i, i + 1) for i in range(count - 1)]
        if periodic:
            forward.append((count - 1, 0))
        backward = [(target, source) for source, target in forward]
        low = lax.ppermute(
            lax.slice_in_dim(block, block.shape[dim] - width, None, axis=dim), axis, forward
        )
        high = lax.ppermute(lax.slice_in_dim(block, 0, width, axis=dim), axis, backward)
        block = jnp.concatenate([low, block, high], axis=dim)
    return block


def shifted(array, axis, by):
    length = lax.axis_size(axis)
    pairs = [(i, i + by) for i in range(length) if 0 <= i + by < length]
    return lax.ppermute(array, axis, pairs)


def column_depth(stratum_tally_sheet, stratum_entries):
    scale = 1.0 / (2.0 * stratum_entries)
    return stratum_tally_sheet * scale + stratum_tally_sheet * (stratum_tally_sheet - 1.0) * (
        scale / stratum_entries
    )


def barotropic_step(planes, stratum_entries):
    height = planes[0]
    zonal_velocity = planes[1]
    meridional_velocity = planes[2]
    stratum_tally_sheet = planes[3]
    wind_east = planes[4]
    wind_north = planes[5]
    fresh_water = planes[6]
    stratum_thicknesses = column_depth(stratum_tally_sheet, stratum_entries)
    lone_flooded_point = (stratum_tally_sheet > 0.5).astype(jnp.float32)
    east_face = lone_flooded_point[1:-1, :-1] * lone_flooded_point[1:-1, 1:]
    east_depth = jnp.minimum(stratum_thicknesses[1:-1, :-1], stratum_thicknesses[1:-1, 1:])
    east_flow = east_face * (
        zonal_velocity[1:-1, :-1]
        - grav_step * east_depth * (height[1:-1, 1:] - height[1:-1, :-1])
        + wind_step * wind_east[1:-1, :-1]
    )
    north_face = lone_flooded_point[:-1, 1:-1] * lone_flooded_point[1:, 1:-1]
    north_depth = jnp.minimum(stratum_thicknesses[:-1, 1:-1], stratum_thicknesses[1:, 1:-1])
    north_flow = north_face * (
        meridional_velocity[:-1, 1:-1]
        - grav_step * north_depth * (height[1:, 1:-1] - height[:-1, 1:-1])
        + wind_step * wind_north[:-1, 1:-1]
    )
    spread = east_flow[:, 1:] - east_flow[:, :-1] + north_flow[1:, :] - north_flow[:-1, :]
    inner_wet = lone_flooded_point[1:-1, 1:-1]
    new_height = height[1:-1, 1:-1] + inner_wet * (
        fresh_step * fresh_water[1:-1, 1:-1] - height_step * spread
    )
    return jnp.stack(
        [
            new_height,
            east_flow[:, 1:],
            north_flow[1:, :],
            stratum_tally_sheet[1:-1, 1:-1],
            wind_east[1:-1, 1:-1],
            wind_north[1:-1, 1:-1],
            fresh_water[1:-1, 1:-1],
        ]
    )


def face_masks(count_border, level_order):
    east_open = (level_order < jnp.minimum(count_border[:, :-1], count_border[:, 1:])).astype(
        jnp.float32
    )
    north_open = (level_order < jnp.minimum(count_border[:-1, :], count_border[1:, :])).astype(
        jnp.float32
    )
    return (east_open, north_open)


def laplace(field, count_border, level_order):
    east_open, north_open = face_masks(count_border, level_order)
    flux_east = east_open * (field[..., 1:] - field[..., :-1])
    flux_north = north_open * (field[..., 1:, :] - field[..., :-1, :])
    return (
        flux_east[..., 1:-1, 1:]
        - flux_east[..., 1:-1, :-1]
        + flux_north[..., 1:, 1:-1]
        - flux_north[..., :-1, 1:-1]
    )


def face_speeds(stratum_thicknesses, east_border, north_border):
    speed_east = east_border[:, :-1] / jnp.maximum(
        jnp.minimum(stratum_thicknesses[:, :-1], stratum_thicknesses[:, 1:]), depth_floor
    )
    speed_north = north_border[:-1, :] / jnp.maximum(
        jnp.minimum(stratum_thicknesses[:-1, :], stratum_thicknesses[1:, :]), depth_floor
    )
    return (speed_east, speed_north)


def horizontal_tendency(
    temp_border, lap_border, count_border, speed_east, speed_north, level_order
):
    mixing = laplace(lap_border, count_border, level_order)
    east_open, north_open = face_masks(count_border, level_order)
    carry_east = east_open * speed_east * 0.5 * (temp_border[..., 1:] + temp_border[..., :-1])
    carry_north = (
        north_open * speed_north * 0.5 * (temp_border[..., 1:, :] + temp_border[..., :-1, :])
    )
    advect = (
        carry_east[..., 1:-1, 1:]
        - carry_east[..., 1:-1, :-1]
        + carry_north[..., 1:, 1:-1]
        - carry_north[..., :-1, 1:-1]
    )
    return -advect_coef * advect - mixing_fourth * mixing


def profile_change_rate(
    thermal_field,
    lateral_contribution,
    stratum_tally_sheet,
    boundary_thermal_exchange,
    solar_radiation,
    stratum_entries,
):
    level_order = jnp.arange(stratum_entries, dtype=jnp.float32)[:, None, None]
    flooded_point_flags = (level_order < stratum_tally_sheet).astype(jnp.float32)
    beneath_stratum_flooded = (level_order + 1.0 < stratum_tally_sheet).astype(jnp.float32)
    sinking_exchange = beneath_stratum_flooded[:-1] * (thermal_field[1:] - thermal_field[:-1])
    blank_sheet = jnp.zeros_like(thermal_field[:1])
    radial_contribution = jnp.concatenate([sinking_exchange, blank_sheet]) - jnp.concatenate(
        [blank_sheet, sinking_exchange]
    )
    absorb = jnp.exp(-level_order / light_decay) * (1.0 - math.exp(-1.0 / light_decay))
    top_level = (level_order < 0.5).astype(jnp.float32)
    donor_entries = (
        light_gain * absorb * solar_radiation + heat_gain * boundary_thermal_exchange * top_level
    )
    return thermal_field + flooded_point_flags * (
        diapycnal_diffusion * radial_contribution + lateral_contribution + donor_entries
    )


def column_onehot(columns, rows, blocks, width):
    lanes = lax.broadcasted_iota(jnp.int32, (1, 1, 1, width), 3)
    return (columns.reshape(rows, blocks, width)[..., None] == lanes).astype(jnp.float32)


def regrid_forward(padded, donor_tile_number, donor_point_number, weight):
    nflux, table_rows, width = padded.shape
    links, rows, blocks = donor_tile_number.shape
    running = jnp.zeros((nflux, rows, blocks * width), jnp.float32)
    for link_index in range(links):
        picked = jnp.take(padded, donor_tile_number[link_index], axis=1)
        onehot = column_onehot(donor_point_number[link_index], rows, blocks, width)
        chosen = jnp.einsum("rbjc,frbc->frbj", onehot, picked, precision=lax.Precision.HIGHEST)
        running = running + chosen.reshape(nflux, rows, blocks * width) * weight[link_index][None]
    return running


def regrid_back(values, donor_tile_number, donor_point_number, weight, table_rows):
    planes = values.shape[0]
    links, rows, blocks = donor_tile_number.shape
    width = values.shape[2] // blocks
    targets = lax.broadcasted_iota(jnp.int32, (1, 1, table_rows), 2)
    table = jnp.zeros((planes, table_rows, width), jnp.float32)
    for link_index in range(links):
        shares = (values * weight[link_index][None]).reshape(planes, rows, blocks, width)
        onehot = column_onehot(donor_point_number[link_index], rows, blocks, width)
        by_cell = jnp.einsum("rbjc,srbj->srbc", onehot, shares, precision=lax.Precision.HIGHEST)
        row_hot = (donor_tile_number[link_index][..., None] == targets).astype(jnp.float32)
        table = table + jnp.einsum(
            "rbt,srbc->stc", row_hot, by_cell, precision=lax.Precision.HIGHEST
        )
    return table


def clear_poles(extended, plane_index, width):
    row_total = extended.shape[1]
    band_index = lax.axis_index("lat")
    band_total = lax.axis_size("lat")
    row_ids = lax.broadcasted_iota(jnp.int32, (row_total, 1), 0)
    south_rim = (band_index == 0) & (row_ids < width)
    north_rim = (band_index == band_total - 1) & (row_ids >= row_total - width)
    keep_rows = jnp.where(south_rim | north_rim, 0.0, 1.0)
    return extended.at[plane_index].multiply(keep_rows)


def shards(
    free_elevation,
    zonal_volume_carriage,
    meridional_volume_carriage,
    thermal_field,
    flooded_strata_number,
    aerial_exchanges,
    aerial_terrain_flags,
    donor_tile_number,
    donor_point_number,
    pairing_coefficients,
):
    stratum_entries = thermal_field.shape[0]
    band_rows = aerial_exchanges.shape[1]
    open_sea = (1 - aerial_terrain_flags).astype(jnp.float32)
    masked = aerial_exchanges * open_sea[None]
    padded = padded_2(masked, (("lat", 1),), band_rows, False)
    boundary_driving = regrid_forward(
        padded, donor_tile_number, donor_point_number, pairing_coefficients
    )
    stratum_tally_sheet = flooded_strata_number.astype(jnp.float32)
    planes = jnp.stack(
        [
            free_elevation,
            zonal_volume_carriage,
            meridional_volume_carriage,
            stratum_tally_sheet,
            boundary_driving[0],
            boundary_driving[1],
            boundary_driving[4],
        ]
    )
    present_scalar_field = planes
    for cycle_index in range(SUBS):
        extended = padded_2(present_scalar_field, (("lon", 2), ("lat", 1)), 1, True)
        present_scalar_field = barotropic_step(clear_poles(extended, 3, 1), stratum_entries)
    advanced_elevation = present_scalar_field[0]
    zonal_velocity = present_scalar_field[1]
    meridional_velocity = present_scalar_field[2]
    level_order = jnp.arange(stratum_entries, dtype=jnp.float32)[:, None, None]
    scalar_strata = jnp.concatenate(
        [thermal_field, present_scalar_field[3:4], present_scalar_field[1:3]]
    )
    extended = padded_2(scalar_strata, (("lon", 2), ("lat", 1)), 2, True)
    extended = clear_poles(extended, stratum_entries, 2)
    lap_border = laplace(extended[:stratum_entries], extended[stratum_entries], level_order)
    bordered = extended[:, 1:-1, 1:-1]
    count_border = bordered[stratum_entries]
    depth_border = column_depth(count_border, stratum_entries)
    speed_east, speed_north = face_speeds(
        depth_border, bordered[stratum_entries + 1], bordered[stratum_entries + 2]
    )
    lateral_contribution = horizontal_tendency(
        bordered[:stratum_entries], lap_border, count_border, speed_east, speed_north, level_order
    )
    advanced_thermal_field = profile_change_rate(
        thermal_field,
        lateral_contribution,
        stratum_tally_sheet,
        boundary_driving[2],
        boundary_driving[3],
        stratum_entries,
    )
    lone_flooded_point = (stratum_tally_sheet > 0.5).astype(jnp.float32)
    stratum_thicknesses = jnp.maximum(depth_border[1:-1, 1:-1], depth_floor)
    uppermost_stratum = (
        jnp.stack(
            [
                advanced_thermal_field[0],
                advanced_elevation,
                zonal_velocity / stratum_thicknesses,
                meridional_velocity / stratum_thicknesses,
            ]
        )
        * lone_flooded_point[None]
    )
    values = jnp.concatenate(
        [uppermost_stratum * lone_flooded_point[None], lone_flooded_point[None]]
    )
    table = regrid_back(
        values, donor_tile_number, donor_point_number, pairing_coefficients, 3 * band_rows
    )
    link_sums = table[:-1]
    link_area = table[-1]
    from_north = shifted((link_sums[:, :band_rows], link_area[:band_rows]), "lat", -1)
    from_south = shifted((link_sums[:, 2 * band_rows :], link_area[2 * band_rows :]), "lat", 1)
    merged_sums = link_sums[:, band_rows : 2 * band_rows] + from_north[0] + from_south[0]
    merged_area = link_area[band_rows : 2 * band_rows] + from_north[1] + from_south[1]
    marine_skin_condition = (
        open_sea[None] * merged_sums / jnp.maximum(merged_area, area_floor)[None]
    )
    return (
        advanced_elevation,
        zonal_velocity,
        meridional_velocity,
        advanced_thermal_field,
        marine_skin_condition,
    )


def solution(mesh):
    placed = (
        P("lat", "lon"),
        P("lat", "lon"),
        P("lat", "lon"),
        P(None, "lat", "lon"),
        P("lat", "lon"),
        P(None, "lat", "lon"),
        P("lat", "lon"),
        P(None, "lat", "lon"),
        P(None, "lat", "lon"),
        P(None, "lat", "lon"),
    )
    return jax.shard_map(
        shards,
        mesh=mesh,
        in_specs=placed,
        out_specs=(
            P("lat", "lon"),
            P("lat", "lon"),
            P("lat", "lon"),
            P(None, "lat", "lon"),
            P(None, "lat", "lon"),
        ),
        check_vma=False,
    )
```

profile of v0, /device:TPU:4, one launch (start us, length us, event | category | flops | bytes accessed | tf_op | source)
XLA Modules:
  0.0 138.9 jit_solution(14313356286278263328)
XLA Ops:
  0.6 0.7 subtract_convert_fusion
  1.3 0.7 copy_multiply_fusion
  2.1 1.9 %collective-permute-start = (f32[5,8,128]{2,0,1:T(8,128)S(1)}, f32[5,8,128]{2,0,1:T(8,128)S(1)}, u32[]{:S(2)}, u32[]{:S(2)}) collective-permute-start(f32[5,8,128]{2,0,1:T(8,128)S(1)} %copy_multiply_fusion), channel_id=1, source_target_pairs={{0,1},{1,2},{2,3},{3,4},{4,5},{5,6},{6,7},{8,9},{9,10},{10,11},{11... | collective-permute-start | bytes 61448 | tf_op jit(solution)/shard_map/ppermute | solution.py:32
  4.0 4.5 %collective-permute-start.1 = (f32[5,8,128]{2,0,1:T(8,128)S(1)}, f32[5,8,128]{2,0,1:T(8,128)S(1)}, u32[]{:S(2)}, u32[]{:S(2)}) collective-permute-start(f32[5,8,128]{2,0,1:T(8,128)S(1)} %copy_multiply_fusion), channel_id=1, source_target_pairs={{1,0},{2,1},{3,2},{4,3},{5,4},{6,5},{7,6},{9,8},{10,9},{11,10},{12... | collective-permute-start | bytes 61448 | tf_op jit(solution)/shard_map/ppermute | solution.py:35
  8.5 0.7 compare_select_fusion.3
  9.3 0.7 compare_and_fusion.3
  10.4 0.8 fusion.164
  11.5 0.8 fusion.163
  12.3 0.7 constant_dynamic-update-slice_fusion.5
  13.0 0.7 constant_dynamic-update-slice_fusion.4
  13.7 0.7 constant_dynamic-update-slice_fusion.3
  14.5 0.7 constant_dynamic-update-slice_fusion.2
  15.7 0.6 gather_fusion
  16.3 2.4 %fusion.15 = f32[5,16,2,128]{3,0,2,1:T(8,128)S(1)} fusion(s32[16,2,128]{2,1,0:T(2,128)S(1)} %eq.60, f32[16,2,5,128]{3,2,1,0:T(8,128)S(1)} %bitcast.247, pred[16,2]{1,0:T(8,128)(4,1)S(1)} %copy.27), kind=kOutput, calls=%fused_computation.48 | convolution fusion | flops 32002048 | bytes 180256 | tf_op jit(solution)/shard_map/rbjc,frbc->frbj/dot_general | solution.py:183
  19.4 2.4 %fusion.16 = f32[5,16,2,128]{3,0,2,1:T(8,128)S(1)} fusion(s32[16,2,128]{2,1,0:T(2,128)S(1)} %eq.64, f32[16,2,5,128]{3,2,1,0:T(8,128)S(1)} %bitcast.248, pred[16,2]{1,0:T(8,128)(4,1)S(1)} %copy.31), kind=kOutput, calls=%fused_computation.49 | convolution fusion | flops 32002048 | bytes 180256 | tf_op jit(solution)/shard_map/rbjc,frbc->frbj/dot_general | solution.py:183
  22.6 2.4 %fusion.17 = f32[5,16,2,128]{3,0,2,1:T(8,128)S(1)} fusion(s32[16,2,128]{2,1,0:T(2,128)S(1)} %eq.68, f32[16,2,5,128]{3,2,1,0:T(8,128)S(1)} %bitcast.249, pred[16,2]{1,0:T(8,128)(4,1)S(1)} %copy.34), kind=kOutput, calls=%fused_computation.50 | convolution fusion | flops 32002048 | bytes 180256 | tf_op jit(solution)/shard_map/rbjc,frbc->frbj/dot_general | solution.py:183
  25.7 2.4 %fusion.18 = f32[5,16,2,128]{3,0,2,1:T(8,128)S(1)} fusion(s32[16,2,128]{2,1,0:T(2,128)S(1)} %eq.72, f32[16,2,5,128]{3,2,1,0:T(8,128)S(1)} %bitcast.246, pred[16,2]{1,0:T(8,128)(4,1)S(1)} %copy.37), kind=kOutput, calls=%fused_computation.51 | convolution fusion | flops 32002048 | bytes 180256 | tf_op jit(solution)/shard_map/rbjc,frbc->frbj/dot_general | solution.py:183
  28.4 1.6 %collective-permute-start.2 = (f32[7,16,1]{2,1,0:T(8,128)S(1)}, f32[7,16,1]{2,1,0:T(8,128)S(1)}, u32[]{:S(2)}, u32[]{:S(2)}) collective-permute-start(f32[7,16,1]{2,1,0:T(8,128)S(1)} %get-tuple-element.95), channel_id=1, source_target_pairs={{0,8},{8,16},{16,24},{24,0},{1,9},{9,17},{17,25},{25,1},{2,10},{10... | collective-permute-start | bytes 1352 | tf_op jit(solution)/shard_map/ppermute | solution.py:32
  30.0 2.2 %collective-permute-start.3 = (f32[7,16,1]{2,1,0:T(8,128)S(1)}, f32[7,16,1]{2,1,0:T(8,128)S(1)}, u32[]{:S(2)}, u32[]{:S(2)}) collective-permute-start(f32[7,16,1]{2,1,0:T(8,128)S(1)} %get-tuple-element.96), channel_id=1, source_target_pairs={{8,0},{16,8},{24,16},{0,24},{9,1},{17,9},{25,17},{1,25},{10,2},{18... | collective-permute-start | bytes 1352 | tf_op jit(solution)/shard_map/ppermute | solution.py:35
  32.3 2.3 %collective-permute-done.2 = f32[7,16,1]{2,1,0:T(8,128)S(1)} collective-permute-done((f32[7,16,1]{2,1,0:T(8,128)S(1)}, f32[7,16,1]{2,1,0:T(8,128)S(1)}, u32[]{:S(2)}, u32[]{:S(2)}) %collective-permute-start.2) | collective-permute-done | bytes 480 | tf_op jit(solution)/shard_map/ppermute | solution.py:32
  35.0 2.6 %collective-permute-start.5 = (f32[7,1,258]{2,1,0:T(1,128)S(1)}, f32[7,1,258]{2,1,0:T(1,128)S(1)}, u32[]{:S(2)}, u32[]{:S(2)}) collective-permute-start(f32[7,1,258]{2,1,0:T(1,128)S(1)} %get-tuple-element.90), channel_id=1, source_target_pairs={{1,0},{2,1},{3,2},{4,3},{5,4},{6,5},{7,6},{0,7},{9,8},{10,9},{11,1... | collective-permute-start | bytes 21680 | tf_op jit(solution)/shard_map/ppermute | solution.py:35
  37.6 1.4 %collective-permute-done.4 = f32[7,1,258]{2,1,0:T(1,128)S(1)} collective-permute-done((f32[7,1,258]{2,1,0:T(1,128)S(1)}, f32[7,1,258]{2,1,0:T(1,128)S(1)}, u32[]{:S(2)}, u32[]{:S(2)}) %collective-permute-start.4) | collective-permute-done | bytes 7256 | tf_op jit(solution)/shard_map/ppermute | solution.py:32
  40.1 1.0 collective-permute-start.6
  41.1 2.8 %collective-permute-start.7 = (f32[7,16,1]{2,1,0:T(8,128)S(1)}, f32[7,16,1]{2,1,0:T(8,128)S(1)}, u32[]{:S(2)}, u32[]{:S(2)}) collective-permute-start(f32[7,16,1]{2,1,0:T(8,128)S(1)} %get-tuple-element.94), channel_id=1, source_target_pairs={{8,0},{16,8},{24,16},{0,24},{9,1},{17,9},{25,17},{1,25},{10,2},{18... | collective-permute-start | bytes 1352 | tf_op jit(solution)/shard_map/ppermute | solution.py:35
  43.9 2.4 %collective-permute-done.6 = f32[7,16,1]{2,1,0:T(8,128)S(1)} collective-permute-done((f32[7,16,1]{2,1,0:T(8,128)S(1)}, f32[7,16,1]{2,1,0:T(8,128)S(1)}, u32[]{:S(2)}, u32[]{:S(2)}) %collective-permute-start.6) | collective-permute-done | bytes 480 | tf_op jit(solution)/shard_map/ppermute | solution.py:32
  46.6 2.6 %collective-permute-start.9 = (f32[7,1,258]{2,1,0:T(1,128)S(1)}, f32[7,1,258]{2,1,0:T(1,128)S(1)}, u32[]{:S(2)}, u32[]{:S(2)}) collective-permute-start(f32[7,1,258]{2,1,0:T(1,128)S(1)} %get-tuple-element.88), channel_id=1, source_target_pairs={{1,0},{2,1},{3,2},{4,3},{5,4},{6,5},{7,6},{0,7},{9,8},{10,9},{11,1... | collective-permute-start | bytes 21680 | tf_op jit(solution)/shard_map/ppermute | solution.py:35
  49.4 1.2 collective-permute-done.8
  51.6 1.2 collective-permute-start.10
  52.8 2.6 %collective-permute-start.11 = (f32[7,16,1]{2,1,0:T(8,128)S(1)}, f32[7,16,1]{2,1,0:T(8,128)S(1)}, u32[]{:S(2)}, u32[]{:S(2)}) collective-permute-start(f32[7,16,1]{2,1,0:T(8,128)S(1)} %get-tuple-element.92), channel_id=1, source_target_pairs={{8,0},{16,8},{24,16},{0,24},{9,1},{17,9},{25,17},{1,25},{10,2},{18... | collective-permute-start | bytes 1352 | tf_op jit(solution)/shard_map/ppermute | solution.py:35
  55.5 2.2 %collective-permute-done.10 = f32[7,16,1]{2,1,0:T(8,128)S(1)} collective-permute-done((f32[7,16,1]{2,1,0:T(8,128)S(1)}, f32[7,16,1]{2,1,0:T(8,128)S(1)}, u32[]{:S(2)}, u32[]{:S(2)}) %collective-permute-start.10) | collective-permute-done | bytes 480 | tf_op jit(solution)/shard_map/ppermute | solution.py:32
  57.9 2.6 %collective-permute-start.13 = (f32[7,1,258]{2,1,0:T(1,128)S(1)}, f32[7,1,258]{2,1,0:T(1,128)S(1)}, u32[]{:S(2)}, u32[]{:S(2)}) collective-permute-start(f32[7,1,258]{2,1,0:T(1,128)S(1)} %get-tuple-element.86), channel_id=1, source_target_pairs={{1,0},{2,1},{3,2},{4,3},{5,4},{6,5},{7,6},{0,7},{9,8},{10,9},{11,1... | collective-permute-start | bytes 21680 | tf_op jit(solution)/shard_map/ppermute | solution.py:35
  60.5 0.6 slice_bitcast_fusion.31
  61.1 0.7 collective-permute-done.12
  62.5 0.7 fusion.121
  63.4 1.2 collective-permute-start.14
  64.6 2.7 %collective-permute-start.15 = (f32[63,16,2]{2,1,0:T(8,128)S(1)}, f32[63,16,2]{2,1,0:T(8,128)S(1)}, u32[]{:S(2)}, u32[]{:S(2)}) collective-permute-start(f32[63,16,2]{2,1,0:T(8,128)S(1)} %get-tuple-element.66), channel_id=1, source_target_pairs={{8,0},{16,8},{24,16},{0,24},{9,1},{17,9},{25,17},{1,25},{10,2},{18... | collective-permute-start | bytes 24200 | tf_op jit(solution)/shard_map/ppermute | solution.py:35
  67.9 12.1 %collective-permute-done.14 = f32[63,16,2]{2,1,0:T(8,128)S(1)} collective-permute-done((f32[63,16,2]{2,1,0:T(8,128)S(1)}, f32[63,16,2]{2,1,0:T(8,128)S(1)}, u32[]{:S(2)}, u32[]{:S(2)}) %collective-permute-start.14) | collective-permute-done | bytes 8096 | tf_op jit(solution)/shard_map/ppermute | solution.py:32
  80.0 7.9 %collective-permute-done.15 = f32[63,16,2]{2,1,0:T(8,128)S(1)} collective-permute-done((f32[63,16,2]{2,1,0:T(8,128)S(1)}, f32[63,16,2]{2,1,0:T(8,128)S(1)}, u32[]{:S(2)}, u32[]{:S(2)}) %collective-permute-start.15) | collective-permute-done | bytes 8096 | tf_op jit(solution)/shard_map/ppermute | solution.py:35
  87.8 1.4 pad_maximum_fusion.22
  89.2 2.6 %collective-permute-start.17 = (f32[63,2,260]{2,1,0:T(2,128)}, f32[63,2,260]{2,1,0:T(2,128)S(1)}, u32[]{:S(2)}, u32[]{:S(2)}) collective-permute-start(f32[63,2,260]{2,1,0:T(2,128)} %get-tuple-element.64), channel_id=1, source_target_pairs={{1,0},{2,1},{3,2},{4,3},{5,4},{6,5},{7,6},{0,7},{9,8},{10,9},{11,1... | collective-permute-start | bytes 393128 | tf_op jit(solution)/shard_map/ppermute | solution.py:35
  92.3 0.6 mul.515
  92.9 0.6 concatenate.75
  93.6 0.6 mul.519
  94.2 0.6 mul.522
  94.8 0.6 mul.525
  95.4 0.6 mul.528
  96.0 0.7 stack.112
  96.8 1.0 pad_maximum_fusion
  98.3 0.7 fusion.144
  99.1 0.6 fusion.3
  100.2 2.0 %slice_subtract_fusion.2 = f32[60,18,258]{2,1,0:T(8,128)S(1)} fusion(f32[60,19,260]{2,1,0:T(8,128)S(1)} %fusion.2, f32[60,20,259]{2,1,0:T(8,128)S(1)} %fusion.3), kind=kLoop, calls=%fused_computation.9 | loop fusion | flops 835920 | bytes 5572800 | tf_op jit(solution)/shard_map/sub | solution.py:110
  102.2 1.8 %fusion.6 = (f32[60,18,257]{2,1,0:T(8,128)S(1)}, f32[60,18,257]{2,1,0:T(8,128)S(1)}) fusion(f32[63,20,260]{2,1,0:T(8,128)S(1)} %pad_maximum_fusion, f32[18,257]{1,0:T(8,128)S(1)} %fusion.80, f32[18,257]{1,0:T(8,128)S(1)} %slice_minimum_fusion.5, f32[60,18,258]{2,1,0:T(8,128)S(1)} %slice_subtract_fusion.2), kind=kLoop, calls=%fused_computation.31 | loop fusion | flops 1942920 | bytes 6698448 | tf_op jit(solution)/shard_map/mul | solution.py:132
  104.2 7.4 %fusion.5 = (f32[60,17,258]{2,1,0:T(8,128)S(1)}, f32[60,17,258]{2,1,0:T(8,128)S(1)}) fusion(f32[63,2,260]{2,1,0:T(2,128)S(1)} %collective-permute-done.16, f32[63,16,2]{2,1,0:T(8,128)S(1)} %collective-permute-done.15, f32[63,16,2]{2,1,0:T(8,128)S(1)} %collective-permute-done.14, f32[1,16,256]{2,1,0:T(8,128)S(1)} %bitcast.245, ...), kind=kLoop, calls=%fused_computation.18 | loop fusion | flops 5000040 | bytes 5556048 | tf_op jit(solution)/shard_map/mul | solution.py:134
  111.8 1.9 %fusion.36 = f32[60,16,256]{2,1,0:T(8,128)S(1)} fusion(f32[60,16,256]{2,1,0:T(8,128)S(1)} %copy-done, f32[60,17,258]{2,1,0:T(8,128)S(1)} %get-tuple-element.125, f32[60,18,257]{2,1,0:T(8,128)S(1)} %get-tuple-element.123, f32[60,17,258]{2,1,0:T(8,128)S(1)} %get-tuple-element.124, f32[60,18,257]{2,1,0:T(8,128)S(1)} %get-tuple-element.122, ...), kind=kLoop, calls=%fused_computation.75 | loop fusion | flops 4669440 | bytes 10846688 | tf_op jit(solution)/shard_map/add | solution.py:166
  114.1 1.8 %fusion.11 = f32[16,2,5,128]{3,2,1,0:T(8,128)S(1)} fusion(s32[16,2,128]{2,1,0:T(2,128)S(1)} %copy-done.23, f32[5,16,2,128]{3,2,1,0:T(2,128)S(1)} %get-tuple-element.98), kind=kOutput, calls=%fused_computation.43 | convolution fusion | flops 31981568 | bytes 180224 | tf_op jit(solution)/shard_map/rbjc,srbj->srbc/dot_general | solution.py:197
  116.0 1.8 %fusion.13 = f32[16,2,5,128]{3,2,1,0:T(8,128)S(1)} fusion(s32[16,2,128]{2,1,0:T(2,128)S(1)} %copy-done.17, f32[5,16,2,128]{3,2,1,0:T(2,128)S(1)} %get-tuple-element.100), kind=kOutput, calls=%fused_computation.46 | convolution fusion | flops 31981568 | bytes 180224 | tf_op jit(solution)/shard_map/rbjc,srbj->srbc/dot_general | solution.py:197
  117.8 1.8 %fusion.9 = f32[16,2,5,128]{3,2,1,0:T(8,128)S(1)} fusion(s32[16,2,128]{2,1,0:T(2,128)S(1)} %copy-done.19, f32[5,16,2,128]{3,2,1,0:T(2,128)S(1)} %get-tuple-element.99), kind=kOutput, calls=%fused_computation.40 | convolution fusion | flops 31981568 | bytes 180224 | tf_op jit(solution)/shard_map/rbjc,srbj->srbc/dot_general | solution.py:197
  119.7 1.8 %fusion.7 = f32[16,2,5,128]{3,2,1,0:T(8,128)S(1)} fusion(s32[16,2,128]{2,1,0:T(2,128)S(1)} %copy-done.21, f32[5,16,2,128]{3,2,1,0:T(2,128)S(1)} %get-tuple-element.97), kind=kOutput, calls=%fused_computation.37 | convolution fusion | flops 31981568 | bytes 180224 | tf_op jit(solution)/shard_map/rbjc,srbj->srbc/dot_general | solution.py:197
  122.8 3.1 %collective-permute-start.20 = (f32[8,128]{1,0:T(8,128)S(1)}, f32[8,128]{1,0:T(8,128)S(1)}, u32[]{:S(2)}, u32[]{:S(2)}) collective-permute-start(f32[8,128]{1,0:T(8,128)S(1)} %get-tuple-element.116), channel_id=1, source_target_pairs={{1,0},{2,1},{3,2},{4,3},{5,4},{6,5},{7,6},{9,8},{10,9},{11,10},{12... | collective-permute-start | bytes 12296 | tf_op jit(solution)/shard_map/ppermute | solution.py:43
  125.9 1.9 %collective-permute-start.21 = (f32[8,128]{1,0:T(8,128)S(1)}, f32[8,128]{1,0:T(8,128)S(1)}, u32[]{:S(2)}, u32[]{:S(2)}) collective-permute-start(f32[8,128]{1,0:T(8,128)S(1)} %get-tuple-element.117), channel_id=1, source_target_pairs={{0,1},{1,2},{2,3},{3,4},{4,5},{5,6},{6,7},{8,9},{9,10},{10,11},{11... | collective-permute-start | bytes 12296 | tf_op jit(solution)/shard_map/ppermute | solution.py:43
  127.8 4.5 %collective-permute-start.18 = (f32[4,8,128]{2,1,0:T(8,128)S(1)}, f32[4,8,128]{2,1,0:T(8,128)S(1)}, u32[]{:S(2)}, u32[]{:S(2)}) collective-permute-start(f32[4,8,128]{2,1,0:T(8,128)S(1)} %get-tuple-element.118), channel_id=1, source_target_pairs={{1,0},{2,1},{3,2},{4,3},{5,4},{6,5},{7,6},{9,8},{10,9},{11,10},{12... | collective-permute-start | bytes 49160 | tf_op jit(solution)/shard_map/ppermute | solution.py:43
  132.4 1.9 %collective-permute-start.19 = (f32[4,8,128]{2,1,0:T(8,128)S(1)}, f32[4,8,128]{2,1,0:T(8,128)S(1)}, u32[]{:S(2)}, u32[]{:S(2)}) collective-permute-start(f32[4,8,128]{2,1,0:T(8,128)S(1)} %get-tuple-element.119), channel_id=1, source_target_pairs={{0,1},{1,2},{2,3},{3,4},{4,5},{5,6},{6,7},{8,9},{9,10},{10,11},{11... | collective-permute-start | bytes 49160 | tf_op jit(solution)/shard_map/ppermute | solution.py:43
  134.3 4.0 %collective-permute-done.19 = f32[4,8,128]{2,1,0:T(8,128)S(1)} collective-permute-done((f32[4,8,128]{2,1,0:T(8,128)S(1)}, f32[4,8,128]{2,1,0:T(8,128)S(1)}, u32[]{:S(2)}, u32[]{:S(2)}) %collective-permute-start.19) | collective-permute-done | bytes 16416 | tf_op jit(solution)/shard_map/ppermute | solution.py:43
  138.3 0.6 fusion.116
  (184 shorter events, 11.3 us)
Async XLA Ops:
  1.3 10.1 %copy-start.13 = (f32[8,128]{1,0:T(8,128)}, f32[8,128]{1,0:T(8,128)S(1)}, u32[]{:S(2)}) copy-start(f32[8,128]{1,0:T(8,128)S(1)} %subtract_convert_fusion) | copy-start | bytes 12292
  2.1 13.6 %collective-permute-start = (f32[5,8,128]{2,0,1:T(8,128)S(1)}, f32[5,8,128]{2,0,1:T(8,128)S(1)}, u32[]{:S(2)}, u32[]{:S(2)}) collective-permute-start(f32[5,8,128]{2,0,1:T(8,128)S(1)} %copy_multiply_fusion), channel_id=1, source_target_pairs={{0,1},{1,2},{2,3},{3,4},{4,5},{5,6},{6,7},{8,9},{9,10},{10,11},{11... | collective-permute-start | bytes 61448 | tf_op jit(solution)/shard_map/ppermute | solution.py:32
  4.0 11.7 %collective-permute-start.1 = (f32[5,8,128]{2,0,1:T(8,128)S(1)}, f32[5,8,128]{2,0,1:T(8,128)S(1)}, u32[]{:S(2)}, u32[]{:S(2)}) collective-permute-start(f32[5,8,128]{2,0,1:T(8,128)S(1)} %copy_multiply_fusion), channel_id=1, source_target_pairs={{1,0},{2,1},{3,2},{4,3},{5,4},{6,5},{7,6},{9,8},{10,9},{11,10},{12... | collective-permute-start | bytes 61448 | tf_op jit(solution)/shard_map/ppermute | solution.py:35
  15.2 3.6 %copy-start.16 = (s32[16,2,128]{2,1,0:T(2,128)}, s32[16,2,128]{2,1,0:T(2,128)S(1)}, u32[]{:S(2)}) copy-start(s32[16,2,128]{2,1,0:T(2,128)S(1)} %eq.60) | copy-start | bytes 49156
  15.3 9.7 %copy-start.22 = (s32[16,2,128]{2,1,0:T(2,128)}, s32[16,2,128]{2,1,0:T(2,128)S(1)}, u32[]{:S(2)}) copy-start(s32[16,2,128]{2,1,0:T(2,128)S(1)} %eq.64) | copy-start | bytes 49156
  15.4 9.5 %copy-start.18 = (s32[16,2,128]{2,1,0:T(2,128)}, s32[16,2,128]{2,1,0:T(2,128)S(1)}, u32[]{:S(2)}) copy-start(s32[16,2,128]{2,1,0:T(2,128)S(1)} %eq.68) | copy-start | bytes 49156
  15.6 10.2 %copy-start.20 = (s32[16,2,128]{2,1,0:T(2,128)}, s32[16,2,128]{2,1,0:T(2,128)S(1)}, u32[]{:S(2)}) copy-start(s32[16,2,128]{2,1,0:T(2,128)S(1)} %eq.72) | copy-start | bytes 49156
  25.7 18.2 %copy-start.4 = (s32[16,256]{1,0:T(8,128)S(1)}, s32[16,256]{1,0:T(8,128)}, u32[]{:S(2)}) copy-start(s32[16,256]{1,0:T(8,128)} %param.24) | copy-start | bytes 49156
  28.1 21.1 %copy-start = (f32[60,16,256]{2,1,0:T(8,128)S(1)}, f32[60,16,256]{2,1,0:T(8,128)}, u32[]{:S(2)}) copy-start(f32[60,16,256]{2,1,0:T(8,128)} %param.23) | copy-start | bytes 2949124
  28.4 6.2 %collective-permute-start.2 = (f32[7,16,1]{2,1,0:T(8,128)S(1)}, f32[7,16,1]{2,1,0:T(8,128)S(1)}, u32[]{:S(2)}, u32[]{:S(2)}) collective-permute-start(f32[7,16,1]{2,1,0:T(8,128)S(1)} %get-tuple-element.95), channel_id=1, source_target_pairs={{0,8},{8,16},{16,24},{24,0},{1,9},{9,17},{17,25},{25,1},{2,10},{10... | collective-permute-start | bytes 1352 | tf_op jit(solution)/shard_map/ppermute | solution.py:32
  30.0 4.8 %collective-permute-start.3 = (f32[7,16,1]{2,1,0:T(8,128)S(1)}, f32[7,16,1]{2,1,0:T(8,128)S(1)}, u32[]{:S(2)}, u32[]{:S(2)}) collective-permute-start(f32[7,16,1]{2,1,0:T(8,128)S(1)} %get-tuple-element.96), channel_id=1, source_target_pairs={{8,0},{16,8},{24,16},{0,24},{9,1},{17,9},{25,17},{1,25},{10,2},{18... | collective-permute-start | bytes 1352 | tf_op jit(solution)/shard_map/ppermute | solution.py:35
  34.9 4.1 %collective-permute-start.4 = (f32[7,1,258]{2,1,0:T(1,128)S(1)}, f32[7,1,258]{2,1,0:T(1,128)S(1)}, u32[]{:S(2)}, u32[]{:S(2)}) collective-permute-start(f32[7,1,258]{2,1,0:T(1,128)S(1)} %get-tuple-element.89), channel_id=1, source_target_pairs={{0,1},{1,2},{2,3},{3,4},{4,5},{5,6},{6,7},{7,0},{8,9},{9,10},{10,1... | collective-permute-start | bytes 21680 | tf_op jit(solution)/shard_map/ppermute | solution.py:32
  35.0 4.0 %collective-permute-start.5 = (f32[7,1,258]{2,1,0:T(1,128)S(1)}, f32[7,1,258]{2,1,0:T(1,128)S(1)}, u32[]{:S(2)}, u32[]{:S(2)}) collective-permute-start(f32[7,1,258]{2,1,0:T(1,128)S(1)} %get-tuple-element.90), channel_id=1, source_target_pairs={{1,0},{2,1},{3,2},{4,3},{5,4},{6,5},{7,6},{0,7},{9,8},{10,9},{11,1... | collective-permute-start | bytes 21680 | tf_op jit(solution)/shard_map/ppermute | solution.py:35
  40.1 6.2 %collective-permute-start.6 = (f32[7,16,1]{2,1,0:T(8,128)S(1)}, f32[7,16,1]{2,1,0:T(8,128)S(1)}, u32[]{:S(2)}, u32[]{:S(2)}) collective-permute-start(f32[7,16,1]{2,1,0:T(8,128)S(1)} %get-tuple-element.93), channel_id=1, source_target_pairs={{0,8},{8,16},{16,24},{24,0},{1,9},{9,17},{17,25},{25,1},{2,10},{10... | collective-permute-start | bytes 1352 | tf_op jit(solution)/shard_map/ppermute | solution.py:32
  41.1 5.3 %collective-permute-start.7 = (f32[7,16,1]{2,1,0:T(8,128)S(1)}, f32[7,16,1]{2,1,0:T(8,128)S(1)}, u32[]{:S(2)}, u32[]{:S(2)}) collective-permute-start(f32[7,16,1]{2,1,0:T(8,128)S(1)} %get-tuple-element.94), channel_id=1, source_target_pairs={{8,0},{16,8},{24,16},{0,24},{9,1},{17,9},{25,17},{1,25},{10,2},{18... | collective-permute-start | bytes 1352 | tf_op jit(solution)/shard_map/ppermute | solution.py:35
  46.5 4.1 %collective-permute-start.8 = (f32[7,1,258]{2,1,0:T(1,128)S(1)}, f32[7,1,258]{2,1,0:T(1,128)S(1)}, u32[]{:S(2)}, u32[]{:S(2)}) collective-permute-start(f32[7,1,258]{2,1,0:T(1,128)S(1)} %get-tuple-element.87), channel_id=1, source_target_pairs={{0,1},{1,2},{2,3},{3,4},{4,5},{5,6},{6,7},{7,0},{8,9},{9,10},{10,1... | collective-permute-start | bytes 21680 | tf_op jit(solution)/shard_map/ppermute | solution.py:32
  46.6 4.0 %collective-permute-start.9 = (f32[7,1,258]{2,1,0:T(1,128)S(1)}, f32[7,1,258]{2,1,0:T(1,128)S(1)}, u32[]{:S(2)}, u32[]{:S(2)}) collective-permute-start(f32[7,1,258]{2,1,0:T(1,128)S(1)} %get-tuple-element.88), channel_id=1, source_target_pairs={{1,0},{2,1},{3,2},{4,3},{5,4},{6,5},{7,6},{0,7},{9,8},{10,9},{11,1... | collective-permute-start | bytes 21680 | tf_op jit(solution)/shard_map/ppermute | solution.py:35
  49.2 11.3 %copy-start.15 = (s32[4,16,2]{1,2,0:T(2,128)S(1)}, s32[4,16,2]{1,2,0:T(2,128)}, u32[]{:S(2)}) copy-start(s32[4,16,2]{1,2,0:T(2,128)} %param.27) | copy-start | bytes 1540
  51.6 6.0 %collective-permute-start.10 = (f32[7,16,1]{2,1,0:T(8,128)S(1)}, f32[7,16,1]{2,1,0:T(8,128)S(1)}, u32[]{:S(2)}, u32[]{:S(2)}) collective-permute-start(f32[7,16,1]{2,1,0:T(8,128)S(1)} %get-tuple-element.91), channel_id=1, source_target_pairs={{0,8},{8,16},{16,24},{24,0},{1,9},{9,17},{17,25},{25,1},{2,10},{10... | collective-permute-start | bytes 1352 | tf_op jit(solution)/shard_map/ppermute | solution.py:32
  52.8 4.8 %collective-permute-start.11 = (f32[7,16,1]{2,1,0:T(8,128)S(1)}, f32[7,16,1]{2,1,0:T(8,128)S(1)}, u32[]{:S(2)}, u32[]{:S(2)}) collective-permute-start(f32[7,16,1]{2,1,0:T(8,128)S(1)} %get-tuple-element.92), channel_id=1, source_target_pairs={{8,0},{16,8},{24,16},{0,24},{9,1},{17,9},{25,17},{1,25},{10,2},{18... | collective-permute-start | bytes 1352 | tf_op jit(solution)/shard_map/ppermute | solution.py:35
  57.8 4.1 %collective-permute-start.12 = (f32[7,1,258]{2,1,0:T(1,128)S(1)}, f32[7,1,258]{2,1,0:T(1,128)S(1)}, u32[]{:S(2)}, u32[]{:S(2)}) collective-permute-start(f32[7,1,258]{2,1,0:T(1,128)S(1)} %get-tuple-element.85), channel_id=1, source_target_pairs={{0,1},{1,2},{2,3},{3,4},{4,5},{5,6},{6,7},{7,0},{8,9},{9,10},{10,1... | collective-permute-start | bytes 21680 | tf_op jit(solution)/shard_map/ppermute | solution.py:32
  57.9 4.0 %collective-permute-start.13 = (f32[7,1,258]{2,1,0:T(1,128)S(1)}, f32[7,1,258]{2,1,0:T(1,128)S(1)}, u32[]{:S(2)}, u32[]{:S(2)}) collective-permute-start(f32[7,1,258]{2,1,0:T(1,128)S(1)} %get-tuple-element.86), channel_id=1, source_target_pairs={{1,0},{2,1},{3,2},{4,3},{5,4},{6,5},{7,6},{0,7},{9,8},{10,9},{11,1... | collective-permute-start | bytes 21680 | tf_op jit(solution)/shard_map/ppermute | solution.py:35
  63.2 41.0 %copy-start.2 = (f32[16,256]{1,0:T(8,128)}, f32[16,256]{1,0:T(8,128)S(1)}, u32[]{:S(2)}) copy-start(f32[16,256]{1,0:T(8,128)S(1)} %get-tuple-element.55) | copy-start | bytes 49156
  63.2 41.0 %copy-start.3 = (f32[16,256]{1,0:T(8,128)}, f32[16,256]{1,0:T(8,128)S(1)}, u32[]{:S(2)}) copy-start(f32[16,256]{1,0:T(8,128)S(1)} %get-tuple-element.56) | copy-start | bytes 49156
  63.4 16.5 %collective-permute-start.14 = (f32[63,16,2]{2,1,0:T(8,128)S(1)}, f32[63,16,2]{2,1,0:T(8,128)S(1)}, u32[]{:S(2)}, u32[]{:S(2)}) collective-permute-start(f32[63,16,2]{2,1,0:T(8,128)S(1)} %get-tuple-element.65), channel_id=1, source_target_pairs={{0,8},{8,16},{16,24},{24,0},{1,9},{9,17},{17,25},{25,1},{2,10},{10... | collective-permute-start | bytes 24200 | tf_op jit(solution)/shard_map/ppermute | solution.py:32
  64.6 23.2 %collective-permute-start.15 = (f32[63,16,2]{2,1,0:T(8,128)S(1)}, f32[63,16,2]{2,1,0:T(8,128)S(1)}, u32[]{:S(2)}, u32[]{:S(2)}) collective-permute-start(f32[63,16,2]{2,1,0:T(8,128)S(1)} %get-tuple-element.66), channel_id=1, source_target_pairs={{8,0},{16,8},{24,16},{0,24},{9,1},{17,9},{25,17},{1,25},{10,2},{18... | collective-permute-start | bytes 24200 | tf_op jit(solution)/shard_map/ppermute | solution.py:35
  89.2 7.6 %collective-permute-start.16 = (f32[63,2,260]{2,1,0:T(2,128)}, f32[63,2,260]{2,1,0:T(2,128)S(1)}, u32[]{:S(2)}, u32[]{:S(2)}) collective-permute-start(f32[63,2,260]{2,1,0:T(2,128)} %get-tuple-element.63), channel_id=1, source_target_pairs={{0,1},{1,2},{2,3},{3,4},{4,5},{5,6},{6,7},{7,0},{8,9},{9,10},{10,1... | collective-permute-start | bytes 393128 | tf_op jit(solution)/shard_map/ppermute | solution.py:32
  89.2 7.6 %collective-permute-start.17 = (f32[63,2,260]{2,1,0:T(2,128)}, f32[63,2,260]{2,1,0:T(2,128)S(1)}, u32[]{:S(2)}, u32[]{:S(2)}) collective-permute-start(f32[63,2,260]{2,1,0:T(2,128)} %get-tuple-element.64), channel_id=1, source_target_pairs={{1,0},{2,1},{3,2},{4,3},{5,4},{6,5},{7,6},{0,7},{9,8},{10,9},{11,1... | collective-permute-start | bytes 393128 | tf_op jit(solution)/shard_map/ppermute | solution.py:35
  96.7 1.1 copy-start.28
  104.2 7.5 %copy-start.29 = (f32[60]{0:T(128)S(1)}, f32[60]{0:T(128)}, u32[]{:S(2)}) copy-start(f32[60]{0:T(128)} %compare_convert_fusion.4) | copy-start | bytes 724
  111.7 2.1 %copy-start.7 = (f32[16,256]{1,0:T(8,128)S(1)}, f32[16,256]{1,0:T(8,128)}, u32[]{:S(2)}) copy-start(f32[16,256]{1,0:T(8,128)} %get-tuple-element.120) | copy-start | bytes 49156
  111.7 2.1 %copy-start.6 = (f32[16,256]{1,0:T(8,128)S(1)}, f32[16,256]{1,0:T(8,128)}, u32[]{:S(2)}) copy-start(f32[16,256]{1,0:T(8,128)} %get-tuple-element.121) | copy-start | bytes 49156
  111.7 2.1 %copy-start.5 = (f32[16,2,128]{2,1,0:T(2,128)S(1)}, f32[16,2,128]{2,1,0:T(2,128)}, u32[]{:S(2)}) copy-start(f32[16,2,128]{2,1,0:T(2,128)} %mul.515) | copy-start | bytes 49156
  111.7 2.2 %copy-start.8 = (f32[1,16,2,128]{3,2,1,0:T(2,128)S(1)}, f32[1,16,2,128]{3,2,1,0:T(2,128)}, u32[]{:S(2)}) copy-start(f32[1,16,2,128]{3,2,1,0:T(2,128)} %concatenate.75) | copy-start | bytes 49156
  111.7 2.2 %copy-start.9 = (f32[16,2,128]{2,1,0:T(2,128)S(1)}, f32[16,2,128]{2,1,0:T(2,128)}, u32[]{:S(2)}) copy-start(f32[16,2,128]{2,1,0:T(2,128)} %mul.519) | copy-start | bytes 49156
  111.7 2.2 %copy-start.10 = (f32[16,2,128]{2,1,0:T(2,128)S(1)}, f32[16,2,128]{2,1,0:T(2,128)}, u32[]{:S(2)}) copy-start(f32[16,2,128]{2,1,0:T(2,128)} %mul.522) | copy-start | bytes 49156
  111.7 2.2 %copy-start.11 = (f32[16,2,128]{2,1,0:T(2,128)S(1)}, f32[16,2,128]{2,1,0:T(2,128)}, u32[]{:S(2)}) copy-start(f32[16,2,128]{2,1,0:T(2,128)} %mul.525) | copy-start | bytes 49156
  111.7 2.2 %copy-start.12 = (f32[16,2,128]{2,1,0:T(2,128)S(1)}, f32[16,2,128]{2,1,0:T(2,128)}, u32[]{:S(2)}) copy-start(f32[16,2,128]{2,1,0:T(2,128)} %mul.528) | copy-start | bytes 49156
  111.7 2.4 %copy-start.23 = (s32[16,2,128]{2,1,0:T(2,128)S(1)}, s32[16,2,128]{2,1,0:T(2,128)}, u32[]{:S(2)}) copy-start(s32[16,2,128]{2,1,0:T(2,128)} %copy-done.22) | copy-start | bytes 49156
  111.8 4.2 %copy-start.17 = (s32[16,2,128]{2,1,0:T(2,128)S(1)}, s32[16,2,128]{2,1,0:T(2,128)}, u32[]{:S(2)}) copy-start(s32[16,2,128]{2,1,0:T(2,128)} %copy-done.16) | copy-start | bytes 49156
  113.7 7.8 %copy-start.1 = (f32[60,16,256]{2,1,0:T(8,128)}, f32[60,16,256]{2,1,0:T(8,128)S(1)}, u32[]{:S(2)}) copy-start(f32[60,16,256]{2,1,0:T(8,128)S(1)} %fusion.36) | copy-start | bytes 2949124
  113.7 4.1 %copy-start.19 = (s32[16,2,128]{2,1,0:T(2,128)S(1)}, s32[16,2,128]{2,1,0:T(2,128)}, u32[]{:S(2)}) copy-start(s32[16,2,128]{2,1,0:T(2,128)} %copy-done.18) | copy-start | bytes 49156
  113.7 5.9 %copy-start.21 = (s32[16,2,128]{2,1,0:T(2,128)S(1)}, s32[16,2,128]{2,1,0:T(2,128)}, u32[]{:S(2)}) copy-start(s32[16,2,128]{2,1,0:T(2,128)} %copy-done.20) | copy-start | bytes 49156
  113.9 7.6 %copy-start.27 = (s32[16,2]{0,1:T(2,128)S(1)}, s32[16,2]{0,1:T(2,128)}, u32[]{:S(2)}) copy-start(s32[16,2]{0,1:T(2,128)} %get-tuple-element.128) | copy-start | bytes 388
  113.9 7.9 %copy-start.26 = (s32[16,2]{0,1:T(2,128)S(1)}, s32[16,2]{0,1:T(2,128)}, u32[]{:S(2)}) copy-start(s32[16,2]{0,1:T(2,128)} %get-tuple-element.127) | copy-start | bytes 388
  114.1 8.0 %copy-start.25 = (s32[16,2]{0,1:T(2,128)S(1)}, s32[16,2]{0,1:T(2,128)}, u32[]{:S(2)}) copy-start(s32[16,2]{0,1:T(2,128)} %get-tuple-element.129) | copy-start | bytes 388
  114.1 8.3 %copy-start.24 = (s32[16,2]{0,1:T(2,128)S(1)}, s32[16,2]{0,1:T(2,128)}, u32[]{:S(2)}) copy-start(s32[16,2]{0,1:T(2,128)} %get-tuple-element.126) | copy-start | bytes 388
  114.1 24.2 %copy-start.14 = (f32[8,128]{1,0:T(8,128)S(1)}, f32[8,128]{1,0:T(8,128)}, u32[]{:S(2)}) copy-start(f32[8,128]{1,0:T(8,128)} %copy-done.13) | copy-start | bytes 12292
  122.8 11.5 %collective-permute-start.20 = (f32[8,128]{1,0:T(8,128)S(1)}, f32[8,128]{1,0:T(8,128)S(1)}, u32[]{:S(2)}, u32[]{:S(2)}) collective-permute-start(f32[8,128]{1,0:T(8,128)S(1)} %get-tuple-element.116), channel_id=1, source_target_pairs={{1,0},{2,1},{3,2},{4,3},{5,4},{6,5},{7,6},{9,8},{10,9},{11,10},{12... | collective-permute-start | bytes 12296 | tf_op jit(solution)/shard_map/ppermute | solution.py:43
  125.9 8.4 %collective-permute-start.21 = (f32[8,128]{1,0:T(8,128)S(1)}, f32[8,128]{1,0:T(8,128)S(1)}, u32[]{:S(2)}, u32[]{:S(2)}) collective-permute-start(f32[8,128]{1,0:T(8,128)S(1)} %get-tuple-element.117), channel_id=1, source_target_pairs={{0,1},{1,2},{2,3},{3,4},{4,5},{5,6},{6,7},{8,9},{9,10},{10,11},{11... | collective-permute-start | bytes 12296 | tf_op jit(solution)/shard_map/ppermute | solution.py:43
  127.8 6.5 %collective-permute-start.18 = (f32[4,8,128]{2,1,0:T(8,128)S(1)}, f32[4,8,128]{2,1,0:T(8,128)S(1)}, u32[]{:S(2)}, u32[]{:S(2)}) collective-permute-start(f32[4,8,128]{2,1,0:T(8,128)S(1)} %get-tuple-element.118), channel_id=1, source_target_pairs={{1,0},{2,1},{3,2},{4,3},{5,4},{6,5},{7,6},{9,8},{10,9},{11,10},{12... | collective-permute-start | bytes 49160 | tf_op jit(solution)/shard_map/ppermute | solution.py:43
  132.4 6.0 %collective-permute-start.19 = (f32[4,8,128]{2,1,0:T(8,128)S(1)}, f32[4,8,128]{2,1,0:T(8,128)S(1)}, u32[]{:S(2)}, u32[]{:S(2)}) collective-permute-start(f32[4,8,128]{2,1,0:T(8,128)S(1)} %get-tuple-element.119), channel_id=1, source_target_pairs={{0,1},{1,2},{2,3},{3,4},{4,5},{5,6},{6,7},{8,9},{9,10},{10,11},{11... | collective-permute-start | bytes 49160 | tf_op jit(solution)/shard_map/ppermute | solution.py:43
where the time goes:
time: 140 us; the launch traced here: 139 us
  starting transfers between devices  44.1 us (32%)
  waiting for transfers between devices  34.6 us (25%)
  other arithmetic  26.2 us (19%)
  matrix products  18.1 us (13%)
  local copies, waits for them, and re-layouts  14.3 us (10%)
  between operations  1.58 us (1%)
    ppermute x9, starting transfers between devices, padded_2(): lax.ppermute(lax.slice_in_dim(block, 0, width, axis=dim), axis, backward)  25.5 us
    ppermute x9, waiting for transfers between devices, padded_2(): lax.ppermute(lax.slice_in_dim(block, block.shape[dim] - width, None, axis...  22.4 us
    ppermute x4, starting transfers between devices, shifted(): return lax.ppermute(array, axis, pairs)  11.5 us
    dot_general x4, matrix products, regrid_forward(): jnp.einsum('rbjc,frbc->frbj', onehot, picked, precision=lax.Precision.HIG...  9.61 us
    ppermute x9, waiting for transfers between devices, padded_2(): lax.ppermute(lax.slice_in_dim(block, 0, width, axis=dim), axis, backward)  8.2 us
    mul x1, other arithmetic, horizontal_tendency(): north_open * speed_north * 0.5  7.43 us
    dot_general x4, matrix products, regrid_back(): jnp.einsum('rbjc,srbj->srbc', onehot, shares, precision=lax.Precision.HIG...  7.33 us
    ppermute x9, starting transfers between devices, padded_2(): lax.ppermute(lax.slice_in_dim(block, block.shape[dim] - width, None, axis...  7.07 us
  transfers between devices with their start and end apart: 22, of which 11 were waited for; matrix products, arithmetic and copies ran while one was open for 10% of the time, Pallas kernels for 0%

commit v1 on v0

v1 whole, which is shorter than its diff:
```python
import functools
import math

import jax
import jax.numpy as jnp
from jax import lax
from jax.experimental import pallas as pl
from jax.experimental.pallas import tpu as pltpu
from jax.sharding import PartitionSpec as P

SUBS = 3

grav_step = 0.6
height_step = 0.6
wind_step = 0.5
fresh_step = 0.5
mixing_fourth = 0.02
advect_coef = 0.1
diapycnal_diffusion = 0.2
heat_gain = 0.3
light_gain = 0.3
light_decay = 8.0
depth_floor = 0.25
area_floor = 1.0

TILE = 8
LANES = 128
HALF = TILE // 2

f32 = jnp.float32
i32 = jnp.int32


def swap_pairs(count, first, periodic):
    pairs = []
    for low in range(first, count, 2):
        high = low + 1
        if high == count:
            if not periodic:
                continue
            high = 0
        pairs += [(low, high), (high, low)]
    return pairs


def swap(array, axis, first, periodic):
    return lax.ppermute(array, axis, swap_pairs(lax.axis_size(axis), first, periodic))


def lane_ids(rows, width=LANES):
    return lax.broadcasted_iota(i32, (rows, width), 1)


def row_ids(rows, width=LANES):
    return lax.broadcasted_iota(i32, (rows, width), 0)


def roll_rows(array, by):
    by = by % array.shape[0]
    return pltpu.roll(array, by, 0) if by else array


def roll_lanes(array, by):
    by = by % array.shape[1]
    return pltpu.roll(array, by, 1) if by else array


def call(body, outs, ins, name, flops, aliases=None, scratch=(), hbm=()):
    specs = [
        pl.BlockSpec(memory_space=pltpu.HBM if place in hbm else pltpu.VMEM)
        for place in range(len(ins))
    ]
    ins = [
        pltpu.with_memory_space_constraint(leaf, pltpu.HBM) if place in hbm else leaf
        for place, leaf in enumerate(ins)
    ]
    moved = 4 * sum(math.prod(leaf.shape) for leaf in list(ins) + list(outs))
    return pl.pallas_call(
        body,
        out_shape=outs,
        in_specs=specs,
        out_specs=[pl.BlockSpec(memory_space=pltpu.VMEM)] * len(outs),
        scratch_shapes=list(scratch),
        input_output_aliases=aliases or {},
        compiler_params=pltpu.CompilerParams(vmem_limit_bytes=24 * 1024 * 1024),
        cost_estimate=pl.CostEstimate(flops=flops, bytes_accessed=moved, transcendentals=0),
        name=name,
    )(*ins)


def shape(*dims, dtype=f32):
    return jax.ShapeDtypeStruct(dims, dtype)


def write_edge(top, fields, tiles, masked, out_ref):
    sub = row_ids(TILE, out_ref.shape[2])
    mine = (sub >= HALF) == top
    for place in range(len(fields) // 2):
        first = jnp.where(top, fields[2 * place][TILE:], fields[2 * place][:TILE])
        second = jnp.where(top, fields[2 * place + 1][TILE:], fields[2 * place + 1][:TILE])
        out_ref[place] = jnp.where(mine, first, roll_rows(second, HALF))
    at = len(fields) // 2
    numbers = jnp.where(top, tiles[TILE:], tiles[:TILE])
    planes = [numbers] + masked
    for place in range(len(planes) // 2):
        out_ref[at + place] = jnp.concatenate(planes[2 * place : 2 * place + 2], axis=1)


def write_temp_edge(top, temp_ref, out_ref, at):
    levels, _, width = temp_ref.shape
    sub = row_ids(TILE, width)
    for group in range(pl.cdiv(levels, 4)):
        packed = jnp.zeros((TILE, width), f32)
        for spot in range(min(4, levels - 4 * group)):
            level = 4 * group + spot
            low = roll_rows(temp_ref[level, :TILE, :], 2 * spot)
            high = roll_rows(temp_ref[level, TILE:, :], 2 * spot + 2)
            packed = jnp.where(sub // 2 == spot, jnp.where(top, high, low), packed)
        out_ref[at + group] = packed


def goes_north(first):
    return (lax.rem(lax.axis_index("lat"), 2) == 0) == (first == 0)


def edge_fields(state, points, weights):
    links = points.shape[0]
    fields = [state[place] for place in range(4)]
    fields += [points[k].astype(f32) for k in range(links)]
    fields += [weights[k] for k in range(links)]
    return fields


def load_body(
    height,
    zonal,
    merid,
    counts,
    points,
    tile,
    weights,
    flux,
    flags,
    temp,
    edge,
    own,
    state_out,
    points_out,
    weights_out,
    flags_out,
    temp_out,
    counts_in,
    tile_in,
    flux_in,
    sems,
):
    pairs = [
        (flux, flux_in),
        (flags, flags_out),
        (tile, tile_in),
        (counts, counts_in),
        (height, state_out.at[0]),
        (zonal, state_out.at[1]),
        (merid, state_out.at[2]),
        (points, points_out),
        (weights, weights_out),
        (temp, temp_out),
    ]
    copies = [
        pltpu.make_async_copy(source, target, sems.at[place])
        for place, (source, target) in enumerate(pairs)
    ]
    for copy in copies:
        copy.start()
    for copy in copies[:-1]:
        copy.wait()
    state_out[3] = counts_in[...].astype(f32)
    links, blocks, rows = tile.shape
    open_sea = (1 - flags_out[...]).astype(f32)
    masked = [flux_in[plane] * open_sea for plane in range(flux.shape[0])]
    lane = lane_ids(rows)
    diagonal = row_ids(rows, rows) == lane_ids(rows, rows)
    tiles = jnp.zeros((rows, LANES), f32)
    for k in range(links):
        for b in range(blocks):
            line = jnp.broadcast_to(tile_in[k, b : b + 1, :].astype(f32), (rows, rows))
            upright = jnp.sum(jnp.where(diagonal, line, 0.0), axis=1, keepdims=True)
            tiles = jnp.where(lane == k * blocks + b, upright, tiles)
    for plane, values in enumerate(masked):
        own[plane] = values
    own[len(masked)] = tiles[:TILE]
    own[len(masked) + 1] = tiles[TILE:]
    top = goes_north(0)
    fields = edge_fields(state_out, points_out, weights_out)
    write_edge(top, fields, tiles, masked, edge)
    copies[-1].wait()
    write_temp_edge(top, temp_out, edge, len(fields) // 2 + (len(masked) + 1) // 2)


def pack_second_body(own, state, points, weights, temp, draft, temp_edge, edges):
    top = goes_north(1)
    nflux = own.shape[0] - 2
    tiles = jnp.concatenate([own[nflux], own[nflux + 1]], axis=0)
    masked = [own[plane] for plane in range(nflux)]
    write_edge(top, edge_fields(state, points, weights), tiles, masked, draft)
    write_temp_edge(top, temp, temp_edge, 0)
    rows = temp.shape[1]
    for place, columns in enumerate(
        edge_columns([temp[level] for level in range(temp.shape[0])], rows)
    ):
        edges[place] = columns


def edge_columns(fields, rows):
    lane = lane_ids(rows)
    high = jnp.zeros((rows, LANES), f32)
    low = jnp.zeros((rows, LANES), f32)
    for level, field in enumerate(fields):
        ends = jnp.where(lane < HALF, field[:, :LANES], field[:, -LANES:])
        turned = roll_lanes(ends, 2 * level + 2)
        high = jnp.where(lane // 2 == level, turned, high)
        low = jnp.where(lane // 2 == (level + 1) % (LANES // 2), turned, low)
    return roll_lanes(low, -2), high


HALO_FLUXES = (0, 1, 4)


def pack_flux_body(flux_at, draft, received, out):
    last = out.shape[0] - 2
    planes = []
    for plane in HALO_FLUXES:
        spot = flux_at * 2 + 1 + plane
        planes.append(received[spot // 2, :, (spot % 2) * LANES : (spot % 2 + 1) * LANES])
    out[last] = jnp.concatenate(planes[:2], axis=1)
    out[last + 1] = jnp.concatenate([planes[2], planes[2]], axis=1)


def pack_third_body(flux_at, received, out):
    for place, plane in enumerate(HALO_FLUXES):
        spot = flux_at * 2 + 1 + plane
        out[place] = received[spot // 2, :, (spot % 2) * LANES : (spot % 2 + 1) * LANES]


def unpack_temp_body(temp_at, got_a, got_b, halo, edges):
    even = lax.rem(lax.axis_index("lat"), 2) == 0
    levels, _, width = halo.shape
    sub = row_ids(TILE, width)
    fields = []
    for group in range(pl.cdiv(levels, 4)):
        one, two = got_a[temp_at + group], got_b[group]
        north = jnp.where(even, one, two)
        south = jnp.where(even, two, one)
        for spot in range(min(4, levels - 4 * group)):
            level = 4 * group + spot
            rows = jnp.where(
                sub < HALF, roll_rows(north, -2 * spot), roll_rows(south, 6 - 2 * spot)
            )
            halo[level] = rows
            fields.append(rows)
    for place, columns in enumerate(edge_columns(fields, TILE)):
        edges[place] = columns


def pick(array, rows):
    return jnp.take_along_axis(array, rows, axis=0, mode="promise_in_bounds")


def pick_lane(array, lanes):
    return jnp.take_along_axis(array, lanes, axis=1, mode="promise_in_bounds")


def spot_of(array, flux_at, place):
    return array[flux_at + place // 2, :, (place % 2) * LANES : (place % 2 + 1) * LANES]


def by_side(even, one, two):
    return jnp.where(even, one, two), jnp.where(even, two, one)


def row_numbers(numbers, column):
    number = jnp.broadcast_to(numbers[:, column : column + 1].astype(i32), (TILE, LANES))
    return number & (TILE - 1), lax.shift_right_logical(number, 3)


FORCING_AT = {0: 4, 1: 5, 4: 6}


def forcing_body(flux_at, got_a, got_b, own, state, points, weights, ext, light):
    even = lax.rem(lax.axis_index("lat"), 2) == 0
    links, rows, width = points.shape
    blocks = width // LANES
    nflux = own.shape[0] - 2
    ext[:4, :rows, :] = state[...]
    north, south = [], []
    for plane in range(nflux):
        one, two = spot_of(got_a, flux_at, 1 + plane), spot_of(got_b, flux_at, 1 + plane)
        high, low = by_side(even, one, two)
        north.append(high)
        south.append(low)
    mid = [own[plane] for plane in range(nflux)]
    for row_tile in range(rows // TILE):
        here = slice(row_tile * TILE, (row_tile + 1) * TILE)
        for b in range(blocks):
            cols = slice(b * LANES, (b + 1) * LANES)
            totals = [jnp.zeros((TILE, LANES), f32) for _ in range(nflux)]
            for k in range(links):
                within, band = row_numbers(own[nflux + row_tile], k * blocks + b)
                lanes = points[k, here, cols]
                weight = weights[k, here, cols]
                for plane in range(nflux):
                    value = jnp.where(
                        band == 0,
                        pick(south[plane], within),
                        jnp.where(band == 1, pick(mid[plane], within), pick(north[plane], within)),
                    )
                    totals[plane] = totals[plane] + weight * pick_lane(value, lanes)
            for plane in range(nflux):
                if plane in FORCING_AT:
                    ext[FORCING_AT[plane], here, cols] = totals[plane]
                else:
                    light[plane - 2, here, cols] = totals[plane]


def forcing_halo_body(
    flux_at, draft, got_a, got_b, got_c, own, edges, edges_halo, ext, send_a, send_b
):
    even = lax.rem(lax.axis_index("lat"), 2) == 0
    rows, width = 2 * TILE, ext.shape[2]
    blocks = width // LANES
    links = flux_at - 2
    sub = row_ids(TILE, width)
    halos = []
    for place in range(flux_at):
        north, south = by_side(even, got_a[place], got_b[place])
        halos.append(jnp.where(sub < HALF, north, south))
        halos.append(roll_rows(jnp.where(sub < HALF, south, north), HALF))
    for place in range(4):
        ext[place, rows:, :] = halos[place]
    last = got_b.shape[0] - 2
    far_b = [got_b[last, :, :LANES], got_b[last, :, LANES:], got_b[last + 1, :, :LANES]]
    tables = {}
    for place, plane in enumerate(HALO_FLUXES):
        one, two = spot_of(got_a, flux_at, 1 + plane), spot_of(got_b, flux_at, 1 + plane)
        north, south = by_side(even, one, two)
        far_north, far_south = by_side(even, got_c[place], far_b[place])
        tables[plane] = [far_south, south, own[plane], north, far_north]
    sub_one = row_ids(TILE)
    north, south = by_side(even, spot_of(got_a, flux_at, 0), spot_of(got_b, flux_at, 0))
    numbers = jnp.where(sub_one < HALF, north, south)
    for b in range(blocks):
        cols = slice(b * LANES, (b + 1) * LANES)
        totals = {plane: jnp.zeros((TILE, LANES), f32) for plane in HALO_FLUXES}
        for k in range(links):
            within, band = row_numbers(numbers, k * blocks + b)
            band = band + jnp.where(sub_one < HALF, 2, 0)
            lanes = halos[4 + k][:, cols].astype(i32)
            weight = halos[4 + links + k][:, cols]
            for plane in HALO_FLUXES:
                value = pick(tables[plane][0], within)
                for at in range(1, 5):
                    value = jnp.where(band == at, pick(tables[plane][at], within), value)
                totals[plane] = totals[plane] + weight * pick_lane(value, lanes)
        for plane in HALO_FLUXES:
            ext[FORCING_AT[plane], rows:, cols] = totals[plane]

    lane = lane_ids(3 * TILE)
    to_west = jnp.zeros((3 * TILE, LANES), f32)
    to_east = jnp.zeros((3 * TILE, LANES), f32)
    for place in range(ext.shape[0]):
        low = roll_lanes(ext[place, :, :LANES], 3 * place)
        high = roll_lanes(ext[place, :, width - LANES :], -3 * place)
        to_west = jnp.where((lane >= 3 * place) & (lane < 3 * place + 3), low, to_west)
        edge = LANES - 3 * place
        to_east = jnp.where((lane >= edge - 3) & (lane < edge), high, to_east)
    lon_even = lax.rem(lax.axis_index("lon"), 2) == 0
    send_a[0] = jnp.where(lon_even, to_east, to_west)
    send_b[0] = jnp.where(lon_even, to_west, to_east)
    for part, columns in ((slice(0, rows), edges), (slice(rows, rows + TILE), edges_halo)):
        send_a[1, part, :] = jnp.where(lon_even, columns[1], columns[0])
        send_b[1, part, :] = jnp.where(lon_even, columns[0], columns[1])


def column_depth(counts, levels):
    scale = 1.0 / (2.0 * levels)
    return counts * scale + counts * (counts - 1.0) * (scale / levels)


def level_tendency(level, temp_level, halo_level, ends_temp, ends_lap, limits, speeds):
    width = temp_level.shape[1]
    rows = temp_level.shape[0]
    whole = jnp.concatenate([temp_level, halo_level], axis=0)
    lane = lane_ids(3 * TILE, width)
    turn = lax.rem(2 * LANES - 2 * level, LANES)
    level_f = level.astype(f32)

    def beside(array, ends):
        turned = pltpu.roll(ends, turn, 1)
        turned = jnp.concatenate([turned] * (width // LANES), axis=1)
        spots = lane[: array.shape[0]]
        east = roll_lanes(jnp.where(spots == 0, turned, array), -1)
        west = roll_lanes(jnp.where(spots == width - 1, turned, array), 1)
        return east, west

    east, west = beside(whole, ends_temp)
    north, south = roll_rows(whole, -1), roll_rows(whole, 1)
    opens = [level_f < limit for limit in limits]
    lap = -4.0 * whole
    for around, is_open in zip((east, west, north, south), opens):
        lap = lap + jnp.where(is_open, around, whole)
    own = whole[:rows]
    own_lap = lap[:rows]
    lap_east, lap_west = beside(own_lap, ends_lap)
    lap_north, lap_south = roll_rows(lap, -1)[:rows], roll_rows(lap, 1)[:rows]
    opens = [is_open[:rows] for is_open in opens]
    mixing = -4.0 * own_lap
    for around, is_open in zip((lap_east, lap_west, lap_north, lap_south), opens):
        mixing = mixing + jnp.where(is_open, around, own_lap)
    carried = [
        jnp.where(is_open, speed * (around[:rows] + own), 0.0)
        for around, is_open, speed in zip((east, west, north, south), opens, speeds)
    ]
    advect = carried[0] - carried[1] + carried[2] - carried[3]
    return -advect_coef * advect - mixing_fourth * mixing


def level_update(level, own, lateral, down, down_before, counts, solar, heat):
    level_f = level.astype(f32)
    absorb = jnp.exp(jnp.full(own.shape, -1.0 / light_decay, f32) * level_f)
    absorb = absorb * (light_gain * (1.0 - math.exp(-1.0 / light_decay)))
    source = absorb * solar + jnp.where(level == 0, heat_gain, 0.0) * heat
    change = diapycnal_diffusion * (down - down_before) + lateral + source
    return own + jnp.where(level_f < counts, change, 0.0)


def subcycle_body(
    levels,
    ext,
    light,
    edges_own,
    edges_halo,
    got_a,
    got_b,
    temp,
    halo,
    points,
    weights,
    tile_hbm,
    out_height,
    out_zonal,
    out_merid,
    limits_out,
    speeds_out,
    ends_out,
    sums_a,
    sums_b,
    sums_mid,
    values,
    table,
    tile,
    tile_sem,
):
    tile_copy = pltpu.make_async_copy(tile_hbm, tile, tile_sem)
    tile_copy.start()
    edges = [
        jnp.concatenate([edges_own[place], edges_halo[place]], axis=0) for place in range(2)
    ]
    width = ext.shape[2]
    rows = temp.shape[1]
    lon_even = lax.rem(lax.axis_index("lon"), 2) == 0
    even = lax.rem(lax.axis_index("lat"), 2) == 0
    lane = lane_ids(3 * TILE)
    from_east = [jnp.where(lon_even, got_a[place], got_b[place]) for place in range(2)]
    from_west = [jnp.where(lon_even, got_b[place], got_a[place]) for place in range(2)]
    planes = []
    for place in range(ext.shape[0]):
        third = jnp.where(
            lane < 3,
            roll_lanes(from_east[0], -3 * place),
            jnp.where(lane >= LANES - 3, roll_lanes(from_west[0], 3 * place), 0.0),
        )
        planes.append(jnp.concatenate([ext[place], third], axis=1))
    height, zonal, merid, counts, wind_east, wind_north, fresh = planes

    def east_of(array):
        return roll_lanes(array, -1)

    def west_of(array):
        return roll_lanes(array, 1)

    def north_of(array):
        return roll_rows(array, -1)

    def south_of(array):
        return roll_rows(array, 1)

    depth = column_depth(counts, levels)
    wet = (counts > 0.5).astype(f32)
    east_wet = wet * east_of(wet)
    north_wet = wet * north_of(wet)
    east_depth = jnp.minimum(depth, east_of(depth))
    north_depth = jnp.minimum(depth, north_of(depth))
    east_pull = grav_step * east_depth
    north_pull = grav_step * north_depth
    wind_east = wind_step * wind_east
    wind_north = wind_step * wind_north
    fresh = fresh_step * fresh
    for _ in range(SUBS):
        zonal = east_wet * (zonal - east_pull * (east_of(height) - height) + wind_east)
        merid = north_wet * (merid - north_pull * (north_of(height) - height) + wind_north)
        spread = zonal - west_of(zonal) + merid - south_of(merid)
        height = height + wet * (fresh - height_step * spread)
    out_height[...] = height[:rows, :width]
    out_zonal[...] = zonal[:rows, :width]
    out_merid[...] = merid[:rows, :width]

    limit_east = jnp.minimum(counts, east_of(counts))
    limit_north = jnp.minimum(counts, north_of(counts))
    limit_west, limit_south = west_of(limit_east), south_of(limit_north)
    limits = [
        limit[:, :width] for limit in (limit_east, limit_west, limit_north, limit_south)
    ]
    speed_east = 0.5 * zonal / jnp.maximum(east_depth, depth_floor)
    speed_north = 0.5 * merid / jnp.maximum(north_depth, depth_floor)
    speeds = [
        speed[:rows, :width]
        for speed in (speed_east, west_of(speed_east), speed_north, south_of(speed_north))
    ]
    for place in range(4):
        limits_out[place] = limits[place]
        speeds_out[place] = speeds[place]

    lane_level = (lane // 2).astype(f32)
    odd_lane = (lane & 1) == 1
    far_east, far_west = from_east[1], from_west[1]

    def column(limit, at):
        return jnp.broadcast_to(limit[:, at : at + 1], (3 * TILE, LANES))

    def edge_lap(center, toward_east, toward_west, at, at_west):
        total = -4.0 * center
        for around, limit in (
            (toward_east, column(limit_east, at)),
            (toward_west, column(limit_east, at_west)),
            (north_of(center), column(limit_north, at)),
            (south_of(center), column(limit_south, at)),
        ):
            total = total + jnp.where(lane_level < limit, around, center)
        return total

    total_lanes = width + LANES
    lap_west = edge_lap(
        far_west,
        roll_lanes(edges[0], 1),
        roll_lanes(far_west, 1),
        total_lanes - 1,
        total_lanes - 2,
    )
    lap_east = edge_lap(
        far_east, roll_lanes(far_east, -1), roll_lanes(edges[1], -1), width, width - 1
    )
    ends_temp = jnp.where(odd_lane, roll_lanes(far_west, -2), far_east)
    ends_lap = jnp.where(odd_lane, roll_lanes(lap_west, -2), lap_east)
    ends_out[0] = ends_temp
    ends_out[1] = ends_lap

    own_counts = counts[:rows, :width]
    zero = jnp.zeros((), i32)
    lateral = level_tendency(
        zero, temp[0], halo[0], ends_temp, ends_lap[:rows], limits, speeds
    )
    if levels > 1:
        down = jnp.where(own_counts > 1.0, temp[1] - temp[0], 0.0)
    else:
        down = jnp.zeros((rows, width), f32)
    top = level_update(
        zero, temp[0], lateral, down, jnp.zeros_like(down), own_counts, light[1], light[0]
    )
    own_wet = wet[:rows, :width]
    thick = jnp.maximum(depth[:rows, :width], depth_floor)
    surface = [
        top * own_wet,
        height[:rows, :width] * own_wet,
        zonal[:rows, :width] / thick * own_wet,
        merid[:rows, :width] / thick * own_wet,
        own_wet,
    ]
    nsums = len(surface)
    values[...] = jnp.zeros(values.shape, f32)
    for place in range(nsums):
        values[:, place, :] = surface[place]
    table[...] = jnp.zeros(table.shape, f32)
    links = points.shape[0]
    blocks = width // LANES
    cells = lax.broadcasted_iota(i32, (LANES, LANES), 0)
    tile_copy.wait()

    for row in range(rows):
        held = values[row]
        for k in range(links):
            shares = held * weights[k, row : row + 1, :]
            upper = shares.astype(jnp.bfloat16)
            lower = (shares - upper.astype(f32)).astype(jnp.bfloat16)
            both = jnp.concatenate([upper, lower], axis=0)
            for b in range(blocks):
                cols = slice(b * LANES, (b + 1) * LANES)
                hot = (cells == points[k, row : row + 1, cols]).astype(f32).astype(jnp.bfloat16)
                found = lax.dot_general(
                    both[:, cols], hot, (((1,), (1,)), ((), ())), preferred_element_type=f32
                )
                target = tile[k, b, row]
                table[target] = table[target] + found
    for place in range(nsums):
        total = table[:, place, :] + table[:, TILE + place, :]
        south, middle, north = total[:TILE], total[TILE : 2 * TILE], total[2 * TILE :]
        sums_mid[place] = middle
        sums_a[place] = jnp.where(even, north, south)
        sums_b[place] = jnp.where(even, south, north)


LEVELS_AT_ONCE = 4


def tracer_body(temp, halo, limits, speeds, ends, light, state, out):
    levels, rows, width = temp.shape
    own_counts = state[3]

    def one_level(level, down_before):
        own = temp[level]
        lateral = level_tendency(
            level,
            own,
            halo[level],
            ends[0],
            ends[1, :rows],
            [limits[place] for place in range(4)],
            [speeds[place] for place in range(4)],
        )
        beneath = temp[jnp.minimum(level + 1, levels - 1)]
        down = jnp.where((level + 1).astype(f32) < own_counts, beneath - own, 0.0)
        out[level] = level_update(
            level, own, lateral, down, down_before, own_counts, light[1], light[0]
        )
        return down

    lax.fori_loop(
        0, levels, one_level, jnp.zeros((rows, width), f32), unroll=math.gcd(levels, LEVELS_AT_ONCE)
    )


def merge_body(mid, got_a, got_b, flags, out):
    open_sea = (1 - flags[...]).astype(f32)
    nsurf = out.shape[0]
    area = mid[nsurf] + got_a[nsurf] + got_b[nsurf]
    scale = open_sea / jnp.maximum(area, area_floor)
    for place in range(nsurf):
        out[place] = (mid[place] + got_a[place] + got_b[place]) * scale


def shards(
    free_elevation,
    zonal_volume_carriage,
    meridional_volume_carriage,
    thermal_field,
    flooded_strata_number,
    aerial_exchanges,
    aerial_terrain_flags,
    donor_tile_number,
    donor_point_number,
    pairing_coefficients,
):
    levels, rows, width = thermal_field.shape
    nflux, band_rows, lanes = aerial_exchanges.shape
    links, _, blocks = donor_tile_number.shape
    assert rows == 2 * TILE and band_rows == TILE and lanes == LANES
    assert 2 * levels <= LANES and lax.axis_size("lon") % 2 == 0
    nsums = 5
    fields = 4 + 2 * links
    flux_at = fields // 2
    temp_at = flux_at + (nflux + 1) // 2
    groups = pl.cdiv(levels, 4)
    tile_lines = jnp.swapaxes(donor_tile_number, 1, 2)
    edge_a, own, state, points, weights, flags, temp = call(
        load_body,
        [
            shape(temp_at + groups, TILE, width),
            shape(nflux + 2, TILE, LANES),
            shape(4, rows, width),
            shape(links, rows, width, dtype=i32),
            shape(links, rows, width),
            shape(band_rows, lanes, dtype=i32),
            shape(levels, rows, width),
        ],
        (
            free_elevation,
            zonal_volume_carriage,
            meridional_volume_carriage,
            flooded_strata_number,
            donor_point_number,
            tile_lines,
            pairing_coefficients,
            aerial_exchanges,
            aerial_terrain_flags,
            thermal_field,
        ),
        "load",
        1000000,
        scratch=[
            pltpu.VMEM((rows, width), i32),
            pltpu.VMEM((links, blocks, rows), i32),
            pltpu.VMEM((nflux, band_rows, lanes), f32),
            pltpu.SemaphoreType.DMA((10,)),
        ],
        hbm=range(10),
    )
    got_a = swap(edge_a, "lat", 0, False)
    draft_b, temp_b, edges = call(
        pack_second_body,
        [
            shape(temp_at + 2, TILE, width),
            shape(groups, TILE, width),
            shape(2, rows, LANES),
        ],
        (own, state, points, weights, temp),
        "pack_b",
        1000000,
    )
    (edge_b,) = call(
        functools.partial(pack_flux_body, flux_at),
        [shape(temp_at + 2, TILE, width)],
        (draft_b, got_a),
        "pack_b_flux",
        1000,
        aliases={0: 0},
    )
    got_b = swap(edge_b, "lat", 1, False)
    got_temp_b = swap(temp_b, "lat", 1, False)
    (edge_c,) = call(
        functools.partial(pack_third_body, flux_at),
        [shape(len(HALO_FLUXES), TILE, LANES)],
        (got_b,),
        "pack_c",
        1000,
    )
    got_c = swap(edge_c, "lat", 0, False)
    draft_ext, light = call(
        functools.partial(forcing_body, flux_at),
        [shape(7, 3 * TILE, width), shape(2, rows, width)],
        (got_a, got_b, own, state, points, weights),
        "forcing",
        1000000,
    )
    halo, edges_halo = call(
        functools.partial(unpack_temp_body, temp_at),
        [shape(levels, TILE, width), shape(2, TILE, LANES)],
        (got_a, got_temp_b),
        "unpack_temp",
        1000000,
    )
    ext, send_a, send_b = call(
        functools.partial(forcing_halo_body, flux_at),
        [
            shape(7, 3 * TILE, width),
            shape(2, 3 * TILE, LANES),
            shape(2, 3 * TILE, LANES),
        ],
        (draft_ext, got_a, got_b, got_c, own, edges, edges_halo),
        "forcing_halo",
        1000000,
        aliases={0: 0},
    )
    lon_a = swap(send_a, "lon", 0, True)
    lon_b = swap(send_b, "lon", 1, True)
    (
        advanced_elevation,
        transport_x_next,
        transport_y_next,
        limits,
        speeds,
        ends,
        sums_a,
        sums_b,
        sums_mid,
    ) = call(
        functools.partial(subcycle_body, levels),
        [shape(rows, width)] * 3
        + [shape(4, 3 * TILE, width), shape(4, rows, width), shape(2, 3 * TILE, LANES)]
        + [shape(nsums, TILE, LANES)] * 3,
        (
            ext,
            light,
            edges,
            edges_halo,
            lon_a,
            lon_b,
            temp,
            halo,
            points,
            weights,
            tile_lines,
        ),
        "subcycles",
        100000000,
        scratch=[
            pltpu.VMEM((rows, TILE, width), f32),
            pltpu.VMEM((3 * TILE, 2 * TILE, LANES), f32),
            pltpu.SMEM((links, blocks, rows), i32),
            pltpu.SemaphoreType.DMA(()),
        ],
        hbm=(10,),
    )
    back_a = swap(sums_a, "lat", 0, False)
    back_b = swap(sums_b, "lat", 1, False)
    (advanced_thermal_field,) = call(
        tracer_body,
        [shape(levels, rows, width)],
        (temp, halo, limits, speeds, ends, light, state),
        "tracer",
        20000000,
    )
    (marine_skin_condition,) = call(
        merge_body,
        [shape(nsums - 1, TILE, LANES)],
        (sums_mid, back_a, back_b, flags),
        "merge",
        1000,
    )
    return (
        advanced_elevation,
        transport_x_next,
        transport_y_next,
        advanced_thermal_field,
        marine_skin_condition,
    )


def solution(mesh):
    flat = P("lat", "lon")
    deep = P(None, "lat", "lon")
    return jax.shard_map(
        shards,
        mesh=mesh,
        in_specs=(flat, flat, flat, deep, flat, deep, flat, deep, deep, deep),
        out_specs=(flat, flat, flat, deep, deep),
        check_vma=False,
    )
```

time: 140 us -> 36.4 us (0.26)
  the two profiles are of different devices: /device:TPU:4 before, /device:TPU:1 now
where the time goes in v1:
time: 36.4 us; the launch traced here: 36.2 us
  starting transfers between devices  15.3 us (42%)
  Pallas kernels  13.1 us (36%)
  waiting for transfers between devices  7.08 us (19%)
  between operations  0.71 us (2%)
    ppermute x8, starting transfers between devices, swap(): lax.ppermute(array, axis, swap_pairs(lax.axis_size(axis), first, periodic))  15.3 us
    pallas_call x10, Pallas kernels, call(): pl.pallas_call(body, out_shape=outs, in_specs=specs, out_specs=[pl.BlockS...  13.1 us
    ppermute x8, waiting for transfers between devices, swap(): lax.ppermute(array, axis, swap_pairs(lax.axis_size(axis), first, periodic))  7.08 us
  transfers between devices with their start and end apart: 8, of which 3 were waited for; matrix products, arithmetic and copies ran while one was open for 0% of the time, Pallas kernels for 18%

profile of v1, /device:TPU:1, one launch (start us, length us, event | category | flops | bytes accessed | tf_op | source)
XLA Modules:
  0.0 36.2 jit_solution(8072134715998028663)
XLA Ops:
  0.6 1.5 %load.1 = (f32[24,8,256]{2,1,0:T(8,128)S(1)}, f32[7,8,128]{2,1,0:T(8,128)S(1)}, f32[4,16,256]{2,1,0:T(8,128)S(1)}, s32[4,16,256]{2,1,0:T(8,128)S(1)}, f32[4,16,2...) custom-call(f32[16,256]{1,0:T(8,128)} %height.1, f32[16,256]{1,0:T(8,128)} %zonal.1, ...), custom_call_target="tpu_custom_call" | custom-call | flops 1000000 | bytes 2613760 | tf_op jit(solution)/shard_map/load/pallas_call | solution.py:78
  2.2 0.1 collective-permute-start
  2.3 0.3 pack_b.1
  2.6 4.5 %collective-permute-start.3 = (f32[15,8,256]{2,1,0:T(8,128)S(1)}, f32[15,8,256]{2,1,0:T(8,128)S(1)}, u32[]{:S(2)}, u32[]{:S(2)}) collective-permute-start(f32[15,8,256]{2,1,0:T(8,128)S(1)} %get-tuple-element.40), channel_id=1, source_target_pairs={{1,2},{2,1},{3,4},{4,3},{5,6},{6,5},{9,10},{10,9},{11,12},{12,11},... | collective-permute-start | bytes 368648 | tf_op jit(solution)/shard_map/ppermute | solution.py:47
  7.1 0.0 collective-permute-done.received.got_a
  7.1 1.9 %collective-permute-start.1 = (f32[11,8,256]{2,1,0:T(8,128)S(1)}, f32[11,8,256]{2,1,0:T(8,128)S(1)}, u32[]{:S(2)}, u32[]{:S(2)}) collective-permute-start(f32[11,8,256]{2,1,0:T(8,128)S(1)} %pack_b_flux.1), channel_id=1, source_target_pairs={{1,2},{2,1},{3,4},{4,3},{5,6},{6,5},{9,10},{10,9},{11,12},{12,11},... | collective-permute-start | bytes 270344 | tf_op jit(solution)/shard_map/ppermute | solution.py:47
  9.1 4.2 %collective-permute-done.1.got_b.received = f32[11,8,256]{2,1,0:T(8,128)S(1)} collective-permute-done((f32[11,8,256]{2,1,0:T(8,128)S(1)}, f32[11,8,256]{2,1,0:T(8,128)S(1)}, u32[]{:S(2)}, u32[]{:S(2)}) %collective-permute-start.1) | collective-permute-done | bytes 90144 | tf_op jit(solution)/shard_map/ppermute | solution.py:47
  13.3 0.0 collective-permute-start.2
  13.3 0.0 collective-permute-done.3.got_b
  13.3 0.2 unpack_temp.1
  13.5 0.4 %forcing.1 = (f32[7,24,256]{2,1,0:T(8,128)S(1)}, f32[2,16,256]{2,1,0:T(8,128)S(1)}) custom-call(f32[24,8,256]{2,1,0:T(8,128)S(1)} %collective-permute-done.received.got_a, f32[11,8,256]{2,1,0:T(8,128)S(1)} %collective-permute-done.1.got_b.received, f32[7,8,128]{2,1,0:T(8,128)S(1)} %get-tuple-element.32.own, f32[4,16,256]{2,1,0:T(8,128)S(1)} %get-tuple-element.33.state, ...), custom_call_target="tpu_custom_call" | custom-call | flops 1000000 | bytes 716800 | tf_op jit(solution)/shard_map/forcing/pallas_call | solution.py:78
  13.9 0.6 %collective-permute-done.2.got_c = f32[3,8,128]{2,1,0:T(8,128)S(1)} collective-permute-done((f32[3,8,128]{2,1,0:T(8,128)S(1)}, f32[3,8,128]{2,1,0:T(8,128)S(1)}, u32[]{:S(2)}, u32[]{:S(2)}) %collective-permute-start.2) | collective-permute-done | bytes 12320 | tf_op jit(solution)/shard_map/ppermute | solution.py:47
  14.5 0.3 forcing_halo.1
  14.7 1.4 %collective-permute-start.4 = (f32[2,24,128]{2,1,0:T(8,128)S(1)}, f32[2,24,128]{2,1,0:T(8,128)S(1)}, u32[]{:S(2)}, u32[]{:S(2)}) collective-permute-start(f32[2,24,128]{2,1,0:T(8,128)S(1)} %get-tuple-element.44), channel_id=1, source_target_pairs={{0,8},{8,0},{16,24},{24,16},{1,9},{9,1},{17,25},{25,17},{2,10},{10... | collective-permute-start | bytes 73736 | tf_op jit(solution)/shard_map/ppermute | solution.py:47
  16.1 2.2 %collective-permute-start.5 = (f32[2,24,128]{2,1,0:T(8,128)S(1)}, f32[2,24,128]{2,1,0:T(8,128)S(1)}, u32[]{:S(2)}, u32[]{:S(2)}) collective-permute-start(f32[2,24,128]{2,1,0:T(8,128)S(1)} %get-tuple-element.45), channel_id=1, source_target_pairs={{8,16},{16,8},{24,0},{0,24},{9,17},{17,9},{25,1},{1,25},{10,18},{1... | collective-permute-start | bytes 73736 | tf_op jit(solution)/shard_map/ppermute | solution.py:47
  18.3 0.0 collective-permute-done.4.got_a
  18.3 2.3 %collective-permute-done.5.got_b = f32[2,24,128]{2,1,0:T(8,128)S(1)} collective-permute-done((f32[2,24,128]{2,1,0:T(8,128)S(1)}, f32[2,24,128]{2,1,0:T(8,128)S(1)}, u32[]{:S(2)}, u32[]{:S(2)}) %collective-permute-start.5) | collective-permute-done | bytes 24608 | tf_op jit(solution)/shard_map/ppermute | solution.py:47
  20.6 4.1 %subcycles.1 = (f32[16,256]{1,0:T(8,128)}, f32[16,256]{1,0:T(8,128)}, f32[16,256]{1,0:T(8,128)}, f32[4,24,256]{2,1,0:T(8,128)S(1)}, f32[4,16,256]{2,1,0:T(8,128)...) custom-call(f32[7,24,256]{2,1,0:T(8,128)S(1)} %get-tuple-element.42., ...), custom_call_target="tpu_custom_call" | custom-call | flops 100000000 | bytes 2183680 | tf_op jit(solution)/shard_map/subcycles/pallas_call | solution.py:78
  24.7 1.7 %collective-permute-start.6 = (f32[5,8,128]{2,1,0:T(8,128)S(1)}, f32[5,8,128]{2,1,0:T(8,128)S(1)}, u32[]{:S(2)}, u32[]{:S(2)}) collective-permute-start(f32[5,8,128]{2,1,0:T(8,128)S(1)} %get-tuple-element.54), channel_id=1, source_target_pairs={{0,1},{1,0},{2,3},{3,2},{4,5},{5,4},{6,7},{7,6},{8,9},{9,8},{10,11... | collective-permute-start | bytes 61448 | tf_op jit(solution)/shard_map/ppermute | solution.py:47
  26.3 3.6 %collective-permute-start.7 = (f32[5,8,128]{2,1,0:T(8,128)S(1)}, f32[5,8,128]{2,1,0:T(8,128)S(1)}, u32[]{:S(2)}, u32[]{:S(2)}) collective-permute-start(f32[5,8,128]{2,1,0:T(8,128)S(1)} %get-tuple-element.55), channel_id=1, source_target_pairs={{1,2},{2,1},{3,4},{4,3},{5,6},{6,5},{9,10},{10,9},{11,12},{12,11},... | collective-permute-start | bytes 61448 | tf_op jit(solution)/shard_map/ppermute | solution.py:47
  30.0 5.6 %tracer.1 = f32[60,16,256]{2,1,0:T(8,128)} custom-call(f32[60,16,256]{2,1,0:T(8,128)S(1)} %get-tuple-element.36.temp, f32[60,8,256]{2,1,0:T(8,128)S(1)} %get-tuple-element.46.halo, f32[4,24,256]{2,1,0:T(8,128)S(1)} %get-tuple-element.50.limits, f32[4,16,256]{2,1,0:T(8,128)S(1)} %get-tuple-element.51.speeds, f32[2,24,128]{2,1,0:T(8,128)S(1)} %get-tuple-element.52.ends, ...), custom_call_target="tpu_custom_call" | custom-call | flops 20000000 | bytes 2744320 | tf_op jit(solution)/shard_map/tracer/pallas_call | solution.py:78
  35.6 0.0 collective-permute-done.6.got_a
  35.6 0.0 collective-permute-done.7.got_b
  35.6 0.6 %merge.1 = f32[4,8,128]{2,1,0:T(8,128)} custom-call(f32[5,8,128]{2,1,0:T(8,128)S(1)} %get-tuple-element.53.mid, f32[5,8,128]{2,1,0:T(8,128)S(1)} %collective-permute-done.6.got_a, f32[5,8,128]{2,1,0:T(8,128)S(1)} %collective-permute-done.7.got_b, s32[8,128]{1,0:T(8,128)S(1)} %get-tuple-element.56.flags), custom_call_target="tpu_custom_call" | custom-call | flops 1000 | bytes 81920 | tf_op jit(solution)/shard_map/merge/pallas_call | solution.py:78
  (2 shorter events, 0.0 us)
Async XLA Ops:
  2.2 4.9 %collective-permute-start = (f32[24,8,256]{2,1,0:T(8,128)S(1)}, f32[24,8,256]{2,1,0:T(8,128)S(1)}, u32[]{:S(2)}, u32[]{:S(2)}) collective-permute-start(f32[24,8,256]{2,1,0:T(8,128)S(1)} %get-tuple-element.31), channel_id=1, source_target_pairs={{0,1},{1,0},{2,3},{3,2},{4,5},{5,4},{6,7},{7,6},{8,9},{9,8},{10,11... | collective-permute-start | bytes 589832 | tf_op jit(solution)/shard_map/ppermute | solution.py:47
  2.6 10.6 %collective-permute-start.3 = (f32[15,8,256]{2,1,0:T(8,128)S(1)}, f32[15,8,256]{2,1,0:T(8,128)S(1)}, u32[]{:S(2)}, u32[]{:S(2)}) collective-permute-start(f32[15,8,256]{2,1,0:T(8,128)S(1)} %get-tuple-element.40), channel_id=1, source_target_pairs={{1,2},{2,1},{3,4},{4,3},{5,6},{6,5},{9,10},{10,9},{11,12},{12,11},... | collective-permute-start | bytes 368648 | tf_op jit(solution)/shard_map/ppermute | solution.py:47
  7.1 6.1 %collective-permute-start.1 = (f32[11,8,256]{2,1,0:T(8,128)S(1)}, f32[11,8,256]{2,1,0:T(8,128)S(1)}, u32[]{:S(2)}, u32[]{:S(2)}) collective-permute-start(f32[11,8,256]{2,1,0:T(8,128)S(1)} %pack_b_flux.1), channel_id=1, source_target_pairs={{1,2},{2,1},{3,4},{4,3},{5,6},{6,5},{9,10},{10,9},{11,12},{12,11},... | collective-permute-start | bytes 270344 | tf_op jit(solution)/shard_map/ppermute | solution.py:47
  13.3 1.2 %collective-permute-start.2 = (f32[3,8,128]{2,1,0:T(8,128)S(1)}, f32[3,8,128]{2,1,0:T(8,128)S(1)}, u32[]{:S(2)}, u32[]{:S(2)}) collective-permute-start(f32[3,8,128]{2,1,0:T(8,128)S(1)} %pack_c.1), channel_id=1, source_target_pairs={{0,1},{1,0},{2,3},{3,2},{4,5},{5,4},{6,7},{7,6},{8,9},{9,8},{10,11... | collective-permute-start | bytes 36872 | tf_op jit(solution)/shard_map/ppermute | solution.py:47
  14.7 3.6 %collective-permute-start.4 = (f32[2,24,128]{2,1,0:T(8,128)S(1)}, f32[2,24,128]{2,1,0:T(8,128)S(1)}, u32[]{:S(2)}, u32[]{:S(2)}) collective-permute-start(f32[2,24,128]{2,1,0:T(8,128)S(1)} %get-tuple-element.44), channel_id=1, source_target_pairs={{0,8},{8,0},{16,24},{24,16},{1,9},{9,1},{17,25},{25,17},{2,10},{10... | collective-permute-start | bytes 73736 | tf_op jit(solution)/shard_map/ppermute | solution.py:47
  16.1 4.5 %collective-permute-start.5 = (f32[2,24,128]{2,1,0:T(8,128)S(1)}, f32[2,24,128]{2,1,0:T(8,128)S(1)}, u32[]{:S(2)}, u32[]{:S(2)}) collective-permute-start(f32[2,24,128]{2,1,0:T(8,128)S(1)} %get-tuple-element.45), channel_id=1, source_target_pairs={{8,16},{16,8},{24,0},{0,24},{9,17},{17,9},{25,1},{1,25},{10,18},{1... | collective-permute-start | bytes 73736 | tf_op jit(solution)/shard_map/ppermute | solution.py:47
  24.7 10.9 %collective-permute-start.6 = (f32[5,8,128]{2,1,0:T(8,128)S(1)}, f32[5,8,128]{2,1,0:T(8,128)S(1)}, u32[]{:S(2)}, u32[]{:S(2)}) collective-permute-start(f32[5,8,128]{2,1,0:T(8,128)S(1)} %get-tuple-element.54), channel_id=1, source_target_pairs={{0,1},{1,0},{2,3},{3,2},{4,5},{5,4},{6,7},{7,6},{8,9},{9,8},{10,11... | collective-permute-start | bytes 61448 | tf_op jit(solution)/shard_map/ppermute | solution.py:47
  26.3 9.2 %collective-permute-start.7 = (f32[5,8,128]{2,1,0:T(8,128)S(1)}, f32[5,8,128]{2,1,0:T(8,128)S(1)}, u32[]{:S(2)}, u32[]{:S(2)}) collective-permute-start(f32[5,8,128]{2,1,0:T(8,128)S(1)} %get-tuple-element.55), channel_id=1, source_target_pairs={{1,2},{2,1},{3,4},{4,3},{5,6},{6,5},{9,10},{10,9},{11,12},{12,11},... | collective-permute-start | bytes 61448 | tf_op jit(solution)/shard_map/ppermute | solution.py:47

commit v2 on v1

--- a/solution.py
+++ b/solution.py
@@ -30,6 +30,9 @@
 f32 = jnp.float32
 i32 = jnp.int32
 
+LATE = 4.0
+FLOPS_PER_US = 1150000000
+
 
 def swap_pairs(count, first, periodic):
     pairs = []
@@ -65,7 +68,7 @@
     return pltpu.roll(array, by, 1) if by else array
 
 
-def call(body, outs, ins, name, flops, aliases=None, scratch=(), hbm=()):
+def call(body, outs, ins, name, took, aliases=None, scratch=(), hbm=()):
     specs = [
         pl.BlockSpec(memory_space=pltpu.HBM if place in hbm else pltpu.VMEM)
         for place in range(len(ins))
@@ -74,22 +77,24 @@
         pltpu.with_memory_space_constraint(leaf, pltpu.HBM) if place in hbm else leaf
         for place, leaf in enumerate(ins)
     ]
-    moved = 4 * sum(math.prod(leaf.shape) for leaf in list(ins) + list(outs))
+    moved = 4 * sum(math.prod(leaf.shape) for leaf in outs)
     return pl.pallas_call(
         body,
         out_shape=outs,
         in_specs=specs,
-        out_specs=[pl.BlockSpec(memory_space=pltpu.VMEM)] * len(outs),
+        out_specs=[pl.BlockSpec(memory_space=leaf.memory_space) for leaf in outs],
         scratch_shapes=list(scratch),
         input_output_aliases=aliases or {},
         compiler_params=pltpu.CompilerParams(vmem_limit_bytes=24 * 1024 * 1024),
-        cost_estimate=pl.CostEstimate(flops=flops, bytes_accessed=moved, transcendentals=0),
+        cost_estimate=pl.CostEstimate(
+            flops=int(took * FLOPS_PER_US), bytes_accessed=moved, transcendentals=0
+        ),
         name=name,
     )(*ins)
 
 
 def shape(*dims, dtype=f32):
-    return jax.ShapeDtypeStruct(dims, dtype)
+    return pltpu.VMEM(dims, dtype)
 
 
 def write_edge(top, fields, tiles, masked, out_ref):
@@ -202,13 +207,17 @@
     nflux = own.shape[0] - 2
     tiles = jnp.concatenate([own[nflux], own[nflux + 1]], axis=0)
     masked = [own[plane] for plane in range(nflux)]
-    write_edge(top, edge_fields(state, points, weights), tiles, masked, draft)
+    fields = edge_fields(state, points, weights)
+    write_edge(top, fields, tiles, masked, draft)
     write_temp_edge(top, temp, temp_edge, 0)
     rows = temp.shape[1]
-    for place, columns in enumerate(
-        edge_columns([temp[level] for level in range(temp.shape[0])], rows)
-    ):
-        edges[place] = columns
+    columns = edge_columns([temp[level] for level in range(temp.shape[0])], rows)
+    for place in range(2):
+        edges[place] = columns[place]
+    at = draft.shape[0] - 4
+    both = jnp.concatenate(columns, axis=1)
+    draft[at] = jnp.where(top, both[TILE:], both[:TILE])
+    draft[at + 1] = jnp.where(top, temp[0, TILE:, :], temp[0, :TILE, :])
 
 
 def edge_columns(fields, rows):
@@ -236,28 +245,34 @@
     out[last + 1] = jnp.concatenate([planes[2], planes[2]], axis=1)
 
 
+def pass_body(first, second, out):
+    out[0] = first[0]
+
+
 def pack_third_body(flux_at, received, out):
     for place, plane in enumerate(HALO_FLUXES):
         spot = flux_at * 2 + 1 + plane
         out[place] = received[spot // 2, :, (spot % 2) * LANES : (spot % 2 + 1) * LANES]
 
 
-def unpack_temp_body(temp_at, got_a, got_b, halo, edges):
+def unpack_rows(top, packed, level):
+    spot = level % 4
+    return jnp.where(top, roll_rows(packed, -2 * spot), roll_rows(packed, 6 - 2 * spot))
+
+
+def near_lanes(width):
+    north = lax.rem(lax.axis_index("lat"), 2) == 0
+    return (row_ids(TILE, width) < HALF) == north
+
+
+def unpack_first_body(temp_at, got_a, halo, edges):
+    levels, _, width = halo.shape
     even = lax.rem(lax.axis_index("lat"), 2) == 0
-    levels, _, width = halo.shape
-    sub = row_ids(TILE, width)
     fields = []
-    for group in range(pl.cdiv(levels, 4)):
-        one, two = got_a[temp_at + group], got_b[group]
-        north = jnp.where(even, one, two)
-        south = jnp.where(even, two, one)
-        for spot in range(min(4, levels - 4 * group)):
-            level = 4 * group + spot
-            rows = jnp.where(
-                sub < HALF, roll_rows(north, -2 * spot), roll_rows(south, 6 - 2 * spot)
-            )
-            halo[level] = rows
-            fields.append(rows)
+    for level in range(levels):
+        rows = unpack_rows(even, got_a[temp_at + level // 4], level)
+        halo[level] = rows
+        fields.append(rows)
     for place, columns in enumerate(edge_columns(fields, TILE)):
         edges[place] = columns
 
@@ -323,7 +338,7 @@
 
 
 def forcing_halo_body(
-    flux_at, draft, got_a, got_b, got_c, own, edges, edges_halo, ext, send_a, send_b
+    flux_at, draft, got_a, got_b, got_c, own, edges, edges_near, ext, send_a, send_b, edges_halo
 ):
     even = lax.rem(lax.axis_index("lat"), 2) == 0
     rows, width = 2 * TILE, ext.shape[2]
@@ -373,6 +388,11 @@
         to_west = jnp.where((lane >= 3 * place) & (lane < 3 * place + 3), low, to_west)
         edge = LANES - 3 * place
         to_east = jnp.where((lane >= edge - 3) & (lane < edge), high, to_east)
+    near = near_lanes(LANES)
+    at = got_b.shape[0] - 4
+    for place in range(2):
+        far = got_b[at, :, place * LANES : (place + 1) * LANES]
+        edges_halo[place] = jnp.where(near, edges_near[place], far)
     lon_even = lax.rem(lax.axis_index("lon"), 2) == 0
     send_a[0] = jnp.where(lon_even, to_east, to_west)
     send_b[0] = jnp.where(lon_even, to_west, to_east)
@@ -387,20 +407,21 @@
 
 
 def level_tendency(level, temp_level, halo_level, ends_temp, ends_lap, limits, speeds):
-    width = temp_level.shape[1]
-    rows = temp_level.shape[0]
+    rows, width = temp_level.shape
     whole = jnp.concatenate([temp_level, halo_level], axis=0)
-    lane = lane_ids(3 * TILE, width)
+    lane = lane_ids(3 * TILE)
     turn = lax.rem(2 * LANES - 2 * level, LANES)
     level_f = level.astype(f32)
 
     def beside(array, ends):
-        turned = pltpu.roll(ends, turn, 1)
-        turned = jnp.concatenate([turned] * (width // LANES), axis=1)
-        spots = lane[: array.shape[0]]
-        east = roll_lanes(jnp.where(spots == 0, turned, array), -1)
-        west = roll_lanes(jnp.where(spots == width - 1, turned, array), 1)
-        return east, west
+        ends = pltpu.roll(ends, turn, 1)
+        lanes = lane[: array.shape[0]]
+        parts = [array[:, at : at + LANES] for at in range(0, width, LANES)]
+        right = [roll_lanes(part, -1) for part in parts] + [ends]
+        left = [ends] + [roll_lanes(part, 1) for part in parts]
+        east = [jnp.where(lanes == LANES - 1, b, a) for a, b in zip(right, right[1:])]
+        west = [jnp.where(lanes == 0, a, b) for a, b in zip(left, left[1:])]
+        return jnp.concatenate(east, axis=1), jnp.concatenate(west, axis=1)
 
     east, west = beside(whole, ends_temp)
     north, south = roll_rows(whole, -1), roll_rows(whole, 1)
@@ -433,6 +454,22 @@
     return own + jnp.where(level_f < counts, change, 0.0)
 
 
+def hot_body(points, hot):
+    links, rows, width = points.shape
+    blocks = width // LANES
+    lane = lane_ids(LANES)
+    lines = [
+        points[k, :, b * LANES : (b + 1) * LANES] for k in range(links) for b in range(blocks)
+    ]
+    held = []
+    for at in range(0, len(lines) * rows, LANES):
+        group = lines[at // rows : (at + LANES) // rows]
+        held.append(jnp.transpose(jnp.concatenate(group, axis=0).astype(f32)).astype(i32))
+    for at in range(links * blocks * rows):
+        column = held[at // LANES][:, at % LANES : at % LANES + 1]
+        hot[at] = (column == lane).astype(f32).astype(jnp.bfloat16)
+
+
 def subcycle_body(
     levels,
     ext,
@@ -442,8 +479,9 @@
     got_a,
     got_b,
     temp,
-    halo,
-    points,
+    halo_near,
+    lat_b,
+    hot,
     weights,
     tile_hbm,
     out_height,
@@ -559,15 +597,16 @@
     lap_east = edge_lap(
         far_east, roll_lanes(far_east, -1), roll_lanes(edges[1], -1), width, width - 1
     )
-    ends_temp = jnp.where(odd_lane, roll_lanes(far_west, -2), far_east)
-    ends_lap = jnp.where(odd_lane, roll_lanes(lap_west, -2), lap_east)
+    ends_temp = roll_lanes(jnp.where(odd_lane, far_west, far_east), -1)
+    ends_lap = roll_lanes(jnp.where(odd_lane, lap_west, lap_east), -1)
     ends_out[0] = ends_temp
     ends_out[1] = ends_lap
 
     own_counts = counts[:rows, :width]
     zero = jnp.zeros((), i32)
+    top_halo = jnp.where(near_lanes(width), halo_near[0], lat_b[lat_b.shape[0] - 3])
     lateral = level_tendency(
-        zero, temp[0], halo[0], ends_temp, ends_lap[:rows], limits, speeds
+        zero, temp[0], top_halo, ends_temp, ends_lap[:rows], limits, speeds
     )
     if levels > 1:
         down = jnp.where(own_counts > 1.0, temp[1] - temp[0], 0.0)
@@ -590,9 +629,8 @@
     for place in range(nsums):
         values[:, place, :] = surface[place]
     table[...] = jnp.zeros(table.shape, f32)
-    links = points.shape[0]
+    links = weights.shape[0]
     blocks = width // LANES
-    cells = lax.broadcasted_iota(i32, (LANES, LANES), 0)
     tile_copy.wait()
 
     for row in range(rows):
@@ -604,9 +642,10 @@
             both = jnp.concatenate([upper, lower], axis=0)
             for b in range(blocks):
                 cols = slice(b * LANES, (b + 1) * LANES)
-                hot = (cells == points[k, row : row + 1, cols]).astype(f32).astype(jnp.bfloat16)
-                found = lax.dot_general(
-                    both[:, cols], hot, (((1,), (1,)), ((), ())), preferred_element_type=f32
+                found = jnp.dot(
+                    both[:, cols],
+                    hot[(k * blocks + b) * rows + row],
+                    preferred_element_type=f32,
                 )
                 target = tile[k, b, row]
                 table[target] = table[target] + found
@@ -618,43 +657,126 @@
         sums_b[place] = jnp.where(even, south, north)
 
 
-LEVELS_AT_ONCE = 4
-
-
-def tracer_body(temp, halo, limits, speeds, ends, light, state, out):
+LEVELS_AT_ONCE = 6
+
+
+def run_levels(first, count, temp, halo, limits, speeds, ends, light, state, out, done=None):
     levels, rows, width = temp.shape
     own_counts = state[3]
-
-    def one_level(level, down_before):
-        own = temp[level]
-        lateral = level_tendency(
-            level,
-            own,
-            halo[level],
-            ends[0],
-            ends[1, :rows],
-            [limits[place] for place in range(4)],
-            [speeds[place] for place in range(4)],
-        )
+    step = math.gcd(count, LEVELS_AT_ONCE)
+
+    def falls(level):
         beneath = temp[jnp.minimum(level + 1, levels - 1)]
-        down = jnp.where((level + 1).astype(f32) < own_counts, beneath - own, 0.0)
-        out[level] = level_update(
-            level, own, lateral, down, down_before, own_counts, light[1], light[0]
-        )
-        return down
-
-    lax.fori_loop(
-        0, levels, one_level, jnp.zeros((rows, width), f32), unroll=math.gcd(levels, LEVELS_AT_ONCE)
-    )
-
-
-def merge_body(mid, got_a, got_b, flags, out):
+        return jnp.where((level + 1).astype(f32) < own_counts, beneath - temp[level], 0.0)
+
+    def group(at, down_before):
+        for inner in range(step):
+            level = first + at * step + inner
+            own = temp[level]
+            lateral = level_tendency(
+                level,
+                own,
+                halo[level],
+                ends[0],
+                ends[1, :rows],
+                [limits[place] for place in range(4)],
+                [speeds[place] for place in range(4)],
+            )
+            down = falls(level)
+            out[at * step + inner] = level_update(
+                level, own, lateral, down, down_before, own_counts, light[1], light[0]
+            )
+            down_before = down
+        if done is not None:
+            done(at, step)
+        return down_before
+
+    start = falls(jnp.int32(first - 1)) if first else jnp.zeros((rows, width), f32)
+    lax.fori_loop(0, count // step, group, start)
+
+
+def upper_body(count, temp, halo_near, limits, speeds, ends, light, state, got_b, out, halo):
+    even = lax.rem(lax.axis_index("lat"), 2) == 0
+    near = near_lanes(temp.shape[2])
+    for level in range(temp.shape[0]):
+        rows = unpack_rows(jnp.logical_not(even), got_b[level // 4], level)
+        halo[level] = jnp.where(near, halo_near[level], rows)
+    run_levels(0, count, temp, halo, limits, speeds, ends, light, state, out)
+
+
+def lower_body(
+    first,
+    temp,
+    halo,
+    limits,
+    speeds,
+    ends,
+    light,
+    state,
+    upper,
+    height,
+    zonal,
+    merid,
+    mid,
+    got_a,
+    got_b,
+    flags,
+    out_height,
+    out_zonal,
+    out_merid,
+    out,
+    out_surface,
+    lower,
+    surface,
+    sems,
+    level_sems,
+):
     open_sea = (1 - flags[...]).astype(f32)
-    nsurf = out.shape[0]
+    nsurf = surface.shape[0]
     area = mid[nsurf] + got_a[nsurf] + got_b[nsurf]
     scale = open_sea / jnp.maximum(area, area_floor)
     for place in range(nsurf):
-        out[place] = (mid[place] + got_a[place] + got_b[place]) * scale
+        surface[place] = (mid[place] + got_a[place] + got_b[place]) * scale
+    pairs = [
+        (surface, out_surface),
+        (upper, out.at[pl.ds(0, first)]),
+        (height, out_height),
+        (zonal, out_zonal),
+        (merid, out_merid),
+    ]
+    copies = [
+        pltpu.make_async_copy(source, target, sems.at[place])
+        for place, (source, target) in enumerate(pairs)
+    ]
+    for copy in copies:
+        copy.start()
+    count = temp.shape[0] - first
+
+    def level_copy(at, step):
+        return pltpu.make_async_copy(
+            lower.at[pl.ds(at * step, step)],
+            out.at[pl.ds(first + at * step, step)],
+            level_sems.at[at],
+        )
+
+    run_levels(
+        first,
+        count,
+        temp,
+        halo,
+        limits,
+        speeds,
+        ends,
+        light,
+        state,
+        lower,
+        lambda at, step: level_copy(at, step).start(),
+    )
+    step = math.gcd(count, LEVELS_AT_ONCE)
+    for at in range(count // step):
+        level_copy(at, step).wait()
+    for copy in copies:
+        copy.wait()
 
 
 def shards(
@@ -704,7 +826,7 @@
             thermal_field,
         ),
         "load",
-        1000000,
+        1.5,
         scratch=[
             pltpu.VMEM((rows, width), i32),
             pltpu.VMEM((links, blocks, rows), i32),
@@ -717,30 +839,33 @@
     draft_b, temp_b, edges = call(
         pack_second_body,
         [
-            shape(temp_at + 2, TILE, width),
+            shape(temp_at + 4, TILE, width),
             shape(groups, TILE, width),
             shape(2, rows, LANES),
         ],
         (own, state, points, weights, temp),
         "pack_b",
-        1000000,
+        0.3,
     )
     (edge_b,) = call(
         functools.partial(pack_flux_body, flux_at),
-        [shape(temp_at + 2, TILE, width)],
+        [shape(temp_at + 4, TILE, width)],
         (draft_b, got_a),
         "pack_b_flux",
-        1000,
+        0.02,
         aliases={0: 0},
     )
     got_b = swap(edge_b, "lat", 1, False)
+    (temp_b,) = call(
+        pass_body, [shape(groups, TILE, width)], (temp_b, edge_b), "pass_temp", LATE, aliases={0: 0}
+    )
     got_temp_b = swap(temp_b, "lat", 1, False)
     (edge_c,) = call(
         functools.partial(pack_third_body, flux_at),
         [shape(len(HALO_FLUXES), TILE, LANES)],
         (got_b,),
         "pack_c",
-        1000,
+        0.02,
     )
     got_c = swap(edge_c, "lat", 0, False)
     draft_ext, light = call(
@@ -748,29 +873,40 @@
         [shape(7, 3 * TILE, width), shape(2, rows, width)],
         (got_a, got_b, own, state, points, weights),
         "forcing",
-        1000000,
-    )
-    halo, edges_halo = call(
-        functools.partial(unpack_temp_body, temp_at),
+        0.4,
+    )
+    halo_near, edges_near = call(
+        functools.partial(unpack_first_body, temp_at),
         [shape(levels, TILE, width), shape(2, TILE, LANES)],
-        (got_a, got_temp_b),
-        "unpack_temp",
-        1000000,
-    )
-    ext, send_a, send_b = call(
+        (got_a,),
+        "unpack_a",
+        0.2,
+    )
+    ext, send_a, send_b, edges_halo = call(
         functools.partial(forcing_halo_body, flux_at),
         [
             shape(7, 3 * TILE, width),
             shape(2, 3 * TILE, LANES),
             shape(2, 3 * TILE, LANES),
+            shape(2, TILE, LANES),
         ],
-        (draft_ext, got_a, got_b, got_c, own, edges, edges_halo),
+        (draft_ext, got_a, got_b, got_c, own, edges, edges_near),
         "forcing_halo",
-        1000000,
+        0.3,
         aliases={0: 0},
     )
+    lon_b = swap(send_b, "lon", 1, True)
+    (send_a,) = call(
+        pass_body, [shape(2, 3 * TILE, LANES)], (send_a, send_b), "pass_lon", LATE, aliases={0: 0}
+    )
     lon_a = swap(send_a, "lon", 0, True)
-    lon_b = swap(send_b, "lon", 1, True)
+    (hot,) = call(
+        hot_body,
+        [shape(links * blocks * rows, LANES, LANES, dtype=jnp.bfloat16)],
+        (points,),
+        "hot",
+        2.5,
+    )
     (
         advanced_elevation,
         transport_x_next,
@@ -794,43 +930,66 @@
             lon_a,
             lon_b,
             temp,
-            halo,
-            points,
+            halo_near,
+            got_b,
+            hot,
             weights,
             tile_lines,
         ),
         "subcycles",
-        100000000,
+        2.6,
         scratch=[
             pltpu.VMEM((rows, TILE, width), f32),
             pltpu.VMEM((3 * TILE, 2 * TILE, LANES), f32),
             pltpu.SMEM((links, blocks, rows), i32),
             pltpu.SemaphoreType.DMA(()),
         ],
-        hbm=(10,),
+        hbm=(11,),
+    )
+    back_b = swap(sums_b, "lat", 1, False)
+    (sums_a,) = call(
+        pass_body, [shape(nsums, TILE, LANES)], (sums_a, sums_b), "pass_sums", LATE, aliases={0: 0}
     )
     back_a = swap(sums_a, "lat", 0, False)
-    back_b = swap(sums_b, "lat", 1, False)
-    (advanced_thermal_field,) = call(
-        tracer_body,
-        [shape(levels, rows, width)],
-        (temp, halo, limits, speeds, ends, light, state),
-        "tracer",
-        20000000,
-    )
-    (marine_skin_condition,) = call(
-        merge_body,
-        [shape(nsums - 1, TILE, LANES)],
-        (sums_mid, back_a, back_b, flags),
-        "merge",
-        1000,
-    )
-    return (
-        advanced_elevation,
-        transport_x_next,
-        transport_y_next,
-        advanced_thermal_field,
-        marine_skin_condition,
+    first = levels // 10 * 6
+    tracer = (temp, halo_near, limits, speeds, ends, light, state)
+    upper, halo = call(
+        functools.partial(upper_body, first),
+        [shape(first, rows, width), shape(levels, TILE, width)],
+        tracer + (got_temp_b,),
+        "tracer_upper",
+        2.3,
+        aliases={1: 1},
+    )
+    tracer = (temp, halo, limits, speeds, ends, light, state)
+    return call(
+        functools.partial(lower_body, first),
+        [
+            pltpu.HBM((rows, width), f32),
+            pltpu.HBM((rows, width), f32),
+            pltpu.HBM((rows, width), f32),
+            pltpu.HBM((levels, rows, width), f32),
+            pltpu.HBM((nsums - 1, band_rows, lanes), f32),
+        ],
+        tracer
+        + (
+            upper,
+            advanced_elevation,
+            transport_x_next,
+            transport_y_next,
+            sums_mid,
+            back_a,
+            back_b,
+            flags,
+        ),
+        "tracer_lower",
+        2.4,
+        scratch=[
+            pltpu.VMEM((levels - first, rows, width), f32),
+            pltpu.VMEM((nsums - 1, band_rows, lanes), f32),
+            pltpu.SemaphoreType.DMA((5,)),
+            pltpu.SemaphoreType.DMA((levels - first,)),
+        ],
     )
 
 

time: 36.4 us -> 32.9 us (0.904); the launches traced: 36.2 us -> 32.2 us
  waiting for transfers between devices: 7.08 us -> 1.9 us
  starting transfers between devices: 15.3 us -> 17 us
  Pallas kernels: 13.1 us -> 12.6 us
    ppermute x8, waiting for transfers between devices: 7.08 us -> 1.9 us  [swap(): lax.ppermute(array, axis, swap_pairs(lax.axis_size(axis), first, periodic))]
    ppermute x8, starting transfers between devices: 15.3 us -> 17 us  [swap(): lax.ppermute(array, axis, swap_pairs(lax.axis_size(axis), first, periodic))]
    pallas_call x10 -> x14, Pallas kernels: 13.1 us -> 12.6 us  [call(): pl.pallas_call(body, out_shape=outs, in_specs=specs, out_specs=[pl.BlockS...]
  transfers between devices with their start and end apart: 8 -> 8, of which waited for: 3 -> 2; matrix products, arithmetic and copies ran while one was open for 0% -> 0% of each run, Pallas kernels for 18% -> 26%
where the time goes in v2:
time: 32.9 us; the launch traced here: 32.2 us
  starting transfers between devices  17 us (52%)
  Pallas kernels  12.6 us (38%)
  waiting for transfers between devices  1.9 us (6%)
  between operations  0.76 us (2%)
    ppermute x8, starting transfers between devices, swap(): lax.ppermute(array, axis, swap_pairs(lax.axis_size(axis), first, periodic))  17 us
    pallas_call x14, Pallas kernels, call(): pl.pallas_call(body, out_shape=outs, in_specs=specs, out_specs=[pl.BlockS...  12.6 us
    ppermute x8, waiting for transfers between devices, swap(): lax.ppermute(array, axis, swap_pairs(lax.axis_size(axis), first, periodic))  1.9 us
  transfers between devices with their start and end apart: 8, of which 2 were waited for; matrix products, arithmetic and copies ran while one was open for 0% of the time, Pallas kernels for 26%

profile of v2, /device:TPU:1, one launch (start us, length us, event | category | flops | bytes accessed | tf_op | source)
XLA Modules:
  0.0 32.2 jit_solution(2229952632747649679)
XLA Ops:
  0.6 1.5 %load.1 = (f32[24,8,256]{2,1,0:T(8,128)S(1)}, f32[7,8,128]{2,1,0:T(8,128)S(1)}, f32[4,16,256]{2,1,0:T(8,128)S(1)}, s32[4,16,256]{2,1,0:T(8,128)S(1)}, f32[4,16,2...) custom-call(f32[16,256]{1,0:T(8,128)} %height.1, f32[16,256]{1,0:T(8,128)} %zonal.1, ...), custom_call_target="tpu_custom_call" | custom-call | flops 1724999936 | bytes 1409024 | tf_op jit(solution)/shard_map/load/pallas_call | solution.py:81
  2.2 0.1 collective-permute-start
  2.3 0.3 pack_b.1
  2.6 1.1 %collective-permute-done.got_a.received = f32[24,8,256]{2,1,0:T(8,128)S(1)} collective-permute-done((f32[24,8,256]{2,1,0:T(8,128)S(1)}, f32[24,8,256]{2,1,0:T(8,128)S(1)}, u32[]{:S(2)}, u32[]{:S(2)}) %collective-permute-start) | collective-permute-done | bytes 196640 | tf_op jit(solution)/shard_map/ppermute | solution.py:50
  3.7 4.5 %collective-permute-start.1 = (f32[13,8,256]{2,1,0:T(8,128)S(1)}, f32[13,8,256]{2,1,0:T(8,128)S(1)}, u32[]{:S(2)}, u32[]{:S(2)}) collective-permute-start(f32[13,8,256]{2,1,0:T(8,128)S(1)} %pack_b_flux.1.second), channel_id=1, source_target_pairs={{1,2},{2,1},{3,4},{4,3},{5,6},{6,5},{9,10},{10,9},{11,12},{12,11},... | collective-permute-start | bytes 319496 | tf_op jit(solution)/shard_map/ppermute | solution.py:50
  8.2 2.5 %hot.1 = bf16[128,128,128]{2,1,0:T(8,128)(2,1)S(1)} custom-call(s32[4,16,256]{2,1,0:T(8,128)S(1)} %get-tuple-element.39.points), custom_call_target="tpu_custom_call" | custom-call | flops 2875000064 | bytes 8388608 | tf_op jit(solution)/shard_map/hot/pallas_call | solution.py:81
  10.7 0.2 unpack_a.1
  11.0 0.0 collective-permute-done.1.got_b.received.lat_b
  11.0 0.0 collective-permute-start.2
  11.0 0.4 %forcing.1 = (f32[7,24,256]{2,1,0:T(8,128)S(1)}, f32[2,16,256]{2,1,0:T(8,128)S(1)}) custom-call(f32[24,8,256]{2,1,0:T(8,128)S(1)} %collective-permute-done.got_a.received, f32[13,8,256]{2,1,0:T(8,128)S(1)} %collective-permute-done.1.got_b.received.lat_b, f32[7,8,128]{2,1,0:T(8,128)S(1)} %get-tuple-element.37.own, f32[4,16,256]{2,1,0:T(8,128)S(1)} %get-tuple-element.38.state, ...), custom_call_target="tpu_custom_call" | custom-call | flops 460000000 | bytes 204800 | tf_op jit(solution)/shard_map/forcing/pallas_call | solution.py:81
  11.4 0.8 %collective-permute-done.2.got_c = f32[3,8,128]{2,1,0:T(8,128)S(1)} collective-permute-done((f32[3,8,128]{2,1,0:T(8,128)S(1)}, f32[3,8,128]{2,1,0:T(8,128)S(1)}, u32[]{:S(2)}, u32[]{:S(2)}) %collective-permute-start.2) | collective-permute-done | bytes 12320 | tf_op jit(solution)/shard_map/ppermute | solution.py:50
  12.2 0.3 forcing_halo.1
  12.4 3.8 %collective-permute-start.4 = (f32[2,24,128]{2,1,0:T(8,128)S(1)}, f32[2,24,128]{2,1,0:T(8,128)S(1)}, u32[]{:S(2)}, u32[]{:S(2)}) collective-permute-start(f32[2,24,128]{2,1,0:T(8,128)S(1)} %get-tuple-element.49.second), channel_id=1, source_target_pairs={{8,16},{16,8},{24,0},{0,24},{9,17},{17,9},{25,1},{1,25},{10,18},{1... | collective-permute-start | bytes 73736 | tf_op jit(solution)/shard_map/ppermute | solution.py:50
  16.2 0.0 collective-permute-start.3
  16.2 4.7 %collective-permute-start.5 = (f32[15,8,256]{2,1,0:T(8,128)S(1)}, f32[15,8,256]{2,1,0:T(8,128)S(1)}, u32[]{:S(2)}, u32[]{:S(2)}) collective-permute-start(f32[15,8,256]{2,1,0:T(8,128)S(1)} %pass_temp.1), channel_id=1, source_target_pairs={{1,2},{2,1},{3,4},{4,3},{5,6},{6,5},{9,10},{10,9},{11,12},{12,11},... | collective-permute-start | bytes 368648 | tf_op jit(solution)/shard_map/ppermute | solution.py:50
  20.9 0.0 collective-permute-done.3.got_a
  20.9 0.0 collective-permute-done.4.got_b
  20.9 2.6 %subcycles.1 = (f32[16,256]{1,0:T(8,128)S(1)}, f32[16,256]{1,0:T(8,128)S(1)}, f32[16,256]{1,0:T(8,128)S(1)}, f32[4,24,256]{2,1,0:T(8,128)S(1)}, f32[4,16,256]{2,...) custom-call(f32[7,24,256]{2,1,0:T(8,128)S(1)} %get-tuple-element.45., ...), custom_call_target="tpu_custom_call" | custom-call | flops 2990000128 | bytes 299008 | tf_op jit(solution)/shard_map/subcycles/pallas_call | solution.py:81
  23.5 3.8 %collective-permute-start.7 = (f32[5,8,128]{2,1,0:T(8,128)S(1)}, f32[5,8,128]{2,1,0:T(8,128)S(1)}, u32[]{:S(2)}, u32[]{:S(2)}) collective-permute-start(f32[5,8,128]{2,1,0:T(8,128)S(1)} %get-tuple-element.61.second), channel_id=1, source_target_pairs={{1,2},{2,1},{3,4},{4,3},{5,6},{6,5},{9,10},{10,9},{11,12},{12,11},... | collective-permute-start | bytes 61448 | tf_op jit(solution)/shard_map/ppermute | solution.py:50
  27.3 0.1 collective-permute-start.6
  27.4 0.0 collective-permute-done.5.got_b
  27.4 2.4 %tracer_upper.1 = (f32[36,16,256]{2,1,0:T(8,128)S(1)}, f32[60,8,256]{2,1,0:T(8,128)S(1)}) custom-call(f32[60,16,256]{2,1,0:T(8,128)S(1)} %get-tuple-element.34.temp, f32[60,8,256]{2,1,0:T(8,128)S(1)} %get-tuple-element.36.halo_near, f32[4,24,256]{2,1,0:T(8,128)S(1)} %get-tuple-element.50.limits, ...), custom_call_target="tpu_custom_call", output_to_operand_aliasing={{1}: (1, {})} | custom-call | flops 2644999936 | bytes 1081344 | tf_op jit(solution)/shard_map/tracer_upper/pallas_call | solution.py:81
  29.8 0.0 collective-permute-done.6.got_a
  29.8 0.0 collective-permute-done.7.got_b
  29.8 2.4 %tracer_lower.1 = (f32[16,256]{1,0:T(8,128)}, f32[16,256]{1,0:T(8,128)}, f32[16,256]{1,0:T(8,128)}, f32[60,16,256]{2,1,0:T(8,128)}, f32[4,8,128]{2,1,0:T(8,128)}) custom-call(f32[60,16,256]{2,1,0:T(8,128)S(1)} %get-tuple-element.34.temp, f32[60,8,256]{2,1,0:T(8,128)S(1)} %get-tuple-element.54.halo, f32[4,24,256]{2,1,0:T(8,128)S(1)} %get-tuple-element.50.limits, ...), custom_call_target="tpu_custom_call" | custom-call | flops 2760000000 | bytes 1048576 | tf_op jit(solution)/shard_map/tracer_lower/pallas_call | solution.py:81
  (5 shorter events, 0.0 us)
Async XLA Ops:
  2.2 1.5 %collective-permute-start = (f32[24,8,256]{2,1,0:T(8,128)S(1)}, f32[24,8,256]{2,1,0:T(8,128)S(1)}, u32[]{:S(2)}, u32[]{:S(2)}) collective-permute-start(f32[24,8,256]{2,1,0:T(8,128)S(1)} %get-tuple-element.35), channel_id=1, source_target_pairs={{0,1},{1,0},{2,3},{3,2},{4,5},{5,4},{6,7},{7,6},{8,9},{9,8},{10,11... | collective-permute-start | bytes 589832 | tf_op jit(solution)/shard_map/ppermute | solution.py:50
  3.7 7.3 %collective-permute-start.1 = (f32[13,8,256]{2,1,0:T(8,128)S(1)}, f32[13,8,256]{2,1,0:T(8,128)S(1)}, u32[]{:S(2)}, u32[]{:S(2)}) collective-permute-start(f32[13,8,256]{2,1,0:T(8,128)S(1)} %pack_b_flux.1.second), channel_id=1, source_target_pairs={{1,2},{2,1},{3,4},{4,3},{5,6},{6,5},{9,10},{10,9},{11,12},{12,11},... | collective-permute-start | bytes 319496 | tf_op jit(solution)/shard_map/ppermute | solution.py:50
  11.0 1.2 %collective-permute-start.2 = (f32[3,8,128]{2,1,0:T(8,128)S(1)}, f32[3,8,128]{2,1,0:T(8,128)S(1)}, u32[]{:S(2)}, u32[]{:S(2)}) collective-permute-start(f32[3,8,128]{2,1,0:T(8,128)S(1)} %pack_c.1), channel_id=1, source_target_pairs={{0,1},{1,0},{2,3},{3,2},{4,5},{5,4},{6,7},{7,6},{8,9},{9,8},{10,11... | collective-permute-start | bytes 36872 | tf_op jit(solution)/shard_map/ppermute | solution.py:50
  12.4 8.5 %collective-permute-start.4 = (f32[2,24,128]{2,1,0:T(8,128)S(1)}, f32[2,24,128]{2,1,0:T(8,128)S(1)}, u32[]{:S(2)}, u32[]{:S(2)}) collective-permute-start(f32[2,24,128]{2,1,0:T(8,128)S(1)} %get-tuple-element.49.second), channel_id=1, source_target_pairs={{8,16},{16,8},{24,0},{0,24},{9,17},{17,9},{25,1},{1,25},{10,18},{1... | collective-permute-start | bytes 73736 | tf_op jit(solution)/shard_map/ppermute | solution.py:50
  16.2 4.7 %collective-permute-start.3 = (f32[2,24,128]{2,1,0:T(8,128)S(1)}, f32[2,24,128]{2,1,0:T(8,128)S(1)}, u32[]{:S(2)}, u32[]{:S(2)}) collective-permute-start(f32[2,24,128]{2,1,0:T(8,128)S(1)} %pass_lon.1), channel_id=1, source_target_pairs={{0,8},{8,0},{16,24},{24,16},{1,9},{9,1},{17,25},{25,17},{2,10},{10... | collective-permute-start | bytes 73736 | tf_op jit(solution)/shard_map/ppermute | solution.py:50
  16.2 11.2 %collective-permute-start.5 = (f32[15,8,256]{2,1,0:T(8,128)S(1)}, f32[15,8,256]{2,1,0:T(8,128)S(1)}, u32[]{:S(2)}, u32[]{:S(2)}) collective-permute-start(f32[15,8,256]{2,1,0:T(8,128)S(1)} %pass_temp.1), channel_id=1, source_target_pairs={{1,2},{2,1},{3,4},{4,3},{5,6},{6,5},{9,10},{10,9},{11,12},{12,11},... | collective-permute-start | bytes 368648 | tf_op jit(solution)/shard_map/ppermute | solution.py:50
  23.5 6.3 %collective-permute-start.7 = (f32[5,8,128]{2,1,0:T(8,128)S(1)}, f32[5,8,128]{2,1,0:T(8,128)S(1)}, u32[]{:S(2)}, u32[]{:S(2)}) collective-permute-start(f32[5,8,128]{2,1,0:T(8,128)S(1)} %get-tuple-element.61.second), channel_id=1, source_target_pairs={{1,2},{2,1},{3,4},{4,3},{5,6},{6,5},{9,10},{10,9},{11,12},{12,11},... | collective-permute-start | bytes 61448 | tf_op jit(solution)/shard_map/ppermute | solution.py:50
  27.3 2.5 %collective-permute-start.6 = (f32[5,8,128]{2,1,0:T(8,128)S(1)}, f32[5,8,128]{2,1,0:T(8,128)S(1)}, u32[]{:S(2)}, u32[]{:S(2)}) collective-permute-start(f32[5,8,128]{2,1,0:T(8,128)S(1)} %pass_sums.1), channel_id=1, source_target_pairs={{0,1},{1,0},{2,3},{3,2},{4,5},{5,4},{6,7},{7,6},{8,9},{9,8},{10,11... | collective-permute-start | bytes 61448 | tf_op jit(solution)/shard_map/ppermute | solution.py:50

commit v3 on v2

--- a/solution.py
+++ b/solution.py
@@ -77,7 +77,6 @@
         pltpu.with_memory_space_constraint(leaf, pltpu.HBM) if place in hbm else leaf
         for place, leaf in enumerate(ins)
     ]
-    moved = 4 * sum(math.prod(leaf.shape) for leaf in outs)
     return pl.pallas_call(
         body,
         out_shape=outs,
@@ -87,7 +86,7 @@
         input_output_aliases=aliases or {},
         compiler_params=pltpu.CompilerParams(vmem_limit_bytes=24 * 1024 * 1024),
         cost_estimate=pl.CostEstimate(
-            flops=int(took * FLOPS_PER_US), bytes_accessed=moved, transcendentals=0
+            flops=int(took * FLOPS_PER_US), bytes_accessed=1024, transcendentals=0
         ),
         name=name,
     )(*ins)
@@ -97,18 +96,24 @@
     return pltpu.VMEM(dims, dtype)
 
 
-def write_edge(top, fields, tiles, masked, out_ref):
+def write_edge(top, fields, out_ref):
     sub = row_ids(TILE, out_ref.shape[2])
     mine = (sub >= HALF) == top
     for place in range(len(fields) // 2):
         first = jnp.where(top, fields[2 * place][TILE:], fields[2 * place][:TILE])
         second = jnp.where(top, fields[2 * place + 1][TILE:], fields[2 * place + 1][:TILE])
         out_ref[place] = jnp.where(mine, first, roll_rows(second, HALF))
-    at = len(fields) // 2
-    numbers = jnp.where(top, tiles[TILE:], tiles[:TILE])
-    planes = [numbers] + masked
+
+
+def write_planes(planes, out_ref, at):
+    planes = planes + [planes[-1]] * (len(planes) % 2)
     for place in range(len(planes) // 2):
         out_ref[at + place] = jnp.concatenate(planes[2 * place : 2 * place + 2], axis=1)
+
+
+def flux_planes(top, own):
+    nflux = own.shape[0] - 2
+    return [jnp.where(top, own[nflux + 1], own[nflux])] + [own[plane] for plane in range(nflux)]
 
 
 def write_temp_edge(top, temp_ref, out_ref, at):
@@ -197,27 +202,33 @@
     own[len(masked) + 1] = tiles[TILE:]
     top = goes_north(0)
     fields = edge_fields(state_out, points_out, weights_out)
-    write_edge(top, fields, tiles, masked, edge)
+    write_edge(top, fields, edge)
+    planes = flux_planes(top, own)
+    at = len(fields) // 2
+    write_planes(planes, edge, at)
     copies[-1].wait()
-    write_temp_edge(top, temp_out, edge, len(fields) // 2 + (len(masked) + 1) // 2)
+    write_temp_edge(top, temp_out, edge, at + (len(planes) + 1) // 2)
 
 
 def pack_second_body(own, state, points, weights, temp, draft, temp_edge, edges):
     top = goes_north(1)
-    nflux = own.shape[0] - 2
-    tiles = jnp.concatenate([own[nflux], own[nflux + 1]], axis=0)
-    masked = [own[plane] for plane in range(nflux)]
     fields = edge_fields(state, points, weights)
-    write_edge(top, fields, tiles, masked, draft)
-    write_temp_edge(top, temp, temp_edge, 0)
-    rows = temp.shape[1]
-    columns = edge_columns([temp[level] for level in range(temp.shape[0])], rows)
+    write_edge(top, fields, draft)
+    planes = flux_planes(top, own)
+    at = len(fields) // 2
+    write_planes(planes, draft, at)
+    levels, rows, _ = temp.shape
+    columns = edge_columns([temp[level] for level in range(levels)], rows)
     for place in range(2):
         edges[place] = columns[place]
-    at = draft.shape[0] - 4
     both = jnp.concatenate(columns, axis=1)
-    draft[at] = jnp.where(top, both[TILE:], both[:TILE])
-    draft[at + 1] = jnp.where(top, temp[0, TILE:, :], temp[0, :TILE, :])
+    draft[at + (len(planes) + 1) // 2] = jnp.where(top, both[TILE:], both[:TILE])
+    write_temp_edge(top, temp, temp_edge, 0)
+
+
+def pack_flux_body(flux_at, draft, received, out):
+    far = [spot_of(received, flux_at, 1 + plane) for plane in HALO_FLUXES]
+    write_planes(far, out, out.shape[0] - (len(far) + 1) // 2)
 
 
 def edge_columns(fields, rows):
@@ -235,24 +246,13 @@
 HALO_FLUXES = (0, 1, 4)
 
 
-def pack_flux_body(flux_at, draft, received, out):
-    last = out.shape[0] - 2
-    planes = []
-    for plane in HALO_FLUXES:
-        spot = flux_at * 2 + 1 + plane
-        planes.append(received[spot // 2, :, (spot % 2) * LANES : (spot % 2 + 1) * LANES])
-    out[last] = jnp.concatenate(planes[:2], axis=1)
-    out[last + 1] = jnp.concatenate([planes[2], planes[2]], axis=1)
-
-
 def pass_body(first, second, out):
     out[0] = first[0]
 
 
 def pack_third_body(flux_at, received, out):
     for place, plane in enumerate(HALO_FLUXES):
-        spot = flux_at * 2 + 1 + plane
-        out[place] = received[spot // 2, :, (spot % 2) * LANES : (spot % 2 + 1) * LANES]
+        out[place] = spot_of(received, flux_at, 1 + plane)
 
 
 def unpack_rows(top, packed, level):
@@ -261,12 +261,11 @@
 
 
 def near_lanes(width):
-    north = lax.rem(lax.axis_index("lat"), 2) == 0
-    return (row_ids(TILE, width) < HALF) == north
-
-
-def unpack_first_body(temp_at, got_a, halo, edges):
-    levels, _, width = halo.shape
+    return (row_ids(TILE, width) < HALF) == (lax.rem(lax.axis_index("lat"), 2) == 0)
+
+
+def unpack_near_body(temp_at, got_a, halo, edges):
+    levels = halo.shape[0]
     even = lax.rem(lax.axis_index("lat"), 2) == 0
     fields = []
     for level in range(levels):
@@ -338,7 +337,18 @@
 
 
 def forcing_halo_body(
-    flux_at, draft, got_a, got_b, got_c, own, edges, edges_near, ext, send_a, send_b, edges_halo
+    flux_at,
+    draft,
+    got_a,
+    got_b,
+    got_c,
+    own,
+    edges,
+    edges_near,
+    ext,
+    send_a,
+    send_b,
+    edges_halo,
 ):
     even = lax.rem(lax.axis_index("lat"), 2) == 0
     rows, width = 2 * TILE, ext.shape[2]
@@ -352,13 +362,12 @@
         halos.append(roll_rows(jnp.where(sub < HALF, south, north), HALF))
     for place in range(4):
         ext[place, rows:, :] = halos[place]
-    last = got_b.shape[0] - 2
-    far_b = [got_b[last, :, :LANES], got_b[last, :, LANES:], got_b[last + 1, :, :LANES]]
     tables = {}
+    far_at = got_b.shape[0] - (len(HALO_FLUXES) + 1) // 2
     for place, plane in enumerate(HALO_FLUXES):
         one, two = spot_of(got_a, flux_at, 1 + plane), spot_of(got_b, flux_at, 1 + plane)
         north, south = by_side(even, one, two)
-        far_north, far_south = by_side(even, got_c[place], far_b[place])
+        far_north, far_south = by_side(even, got_c[place], spot_of(got_b, far_at, place))
         tables[plane] = [far_south, south, own[plane], north, far_north]
     sub_one = row_ids(TILE)
     north, south = by_side(even, spot_of(got_a, flux_at, 0), spot_of(got_b, flux_at, 0))
@@ -389,10 +398,8 @@
         edge = LANES - 3 * place
         to_east = jnp.where((lane >= edge - 3) & (lane < edge), high, to_east)
     near = near_lanes(LANES)
-    at = got_b.shape[0] - 4
     for place in range(2):
-        far = got_b[at, :, place * LANES : (place + 1) * LANES]
-        edges_halo[place] = jnp.where(near, edges_near[place], far)
+        edges_halo[place] = jnp.where(near, edges_near[place], spot_of(got_b, far_at - 1, place))
     lon_even = lax.rem(lax.axis_index("lon"), 2) == 0
     send_a[0] = jnp.where(lon_even, to_east, to_west)
     send_b[0] = jnp.where(lon_even, to_west, to_east)
@@ -406,81 +413,113 @@
     return counts * scale + counts * (counts - 1.0) * (scale / levels)
 
 
-def level_tendency(level, temp_level, halo_level, ends_temp, ends_lap, limits, speeds):
-    rows, width = temp_level.shape
-    whole = jnp.concatenate([temp_level, halo_level], axis=0)
+def sideways(array, ends):
+    rows, width = array.shape
+    lane = lane_ids(rows)
+    parts = [array[:, at : at + LANES] for at in range(0, width, LANES)]
+    right = [roll_lanes(part, -1) for part in parts] + [ends]
+    left = [ends] + [roll_lanes(part, 1) for part in parts]
+    east = [jnp.where(lane == LANES - 1, b, a) for a, b in zip(right, right[1:])]
+    west = [jnp.where(lane == 0, a, b) for a, b in zip(left, left[1:])]
+    return jnp.concatenate(east, axis=1), jnp.concatenate(west, axis=1)
+
+
+def turned(ends, level):
+    return pltpu.roll(ends, lax.rem(2 * LANES - 2 * level, LANES), 1)
+
+
+LEVELS_AT_ONCE = 6
+
+
+def before_body(ext, light, temp, halo_near, got_b, base, laps, halo):
+    levels, rows, width = temp.shape
+    counts = ext[3]
+    own_counts = counts[:rows]
+    lane = lane_ids(3 * TILE, width)
+    limit_east = jnp.where(lane == width - 1, 0.0, jnp.minimum(counts, roll_lanes(counts, -1)))
+    limit_north = jnp.minimum(counts, roll_rows(counts, -1))
+    limits = (limit_east, roll_lanes(limit_east, 1), limit_north, roll_rows(limit_north, 1))
+    step = math.gcd(levels, LEVELS_AT_ONCE)
+    odd = lax.rem(lax.axis_index("lat"), 2) == 1
+    near = near_lanes(width)
+    for level in range(levels):
+        rows_far = unpack_rows(odd, got_b[level // 4], level)
+        halo[level] = jnp.where(near, halo_near[level], rows_far)
+
+    def group(at, down_before):
+        for inner in range(step):
+            level = at * step + inner
+            level_f = level.astype(f32)
+            own = temp[level]
+            whole = jnp.concatenate([own, halo[level]], axis=0)
+            east, west = sideways(whole, whole[:, :LANES])
+            lap = -4.0 * whole
+            for around, limit in zip(
+                (east, west, roll_rows(whole, -1), roll_rows(whole, 1)), limits
+            ):
+                lap = lap + jnp.where(level_f < limit, around, whole)
+            laps[level] = lap
+            beneath = temp[jnp.minimum(level + 1, levels - 1)]
+            down = jnp.where(level_f + 1.0 < own_counts, beneath - own, 0.0)
+            absorb = jnp.exp(jnp.full(own.shape, -1.0 / light_decay, f32) * level_f)
+            absorb = absorb * (light_gain * (1.0 - math.exp(-1.0 / light_decay)))
+            source = absorb * light[1] + jnp.where(level == 0, heat_gain, 0.0) * light[0]
+            change = diapycnal_diffusion * (down - down_before) + source
+            base[level] = own + jnp.where(level_f < own_counts, change, 0.0)
+            down_before = down
+        return down_before
+
+    lax.fori_loop(0, levels // step, group, jnp.zeros((rows, width), f32))
+
+
+def finish_level(level, own, halo_level, base, lap, ends, limits, speeds):
+    rows, width = own.shape
+    level_f = level.astype(f32)
     lane = lane_ids(3 * TILE)
-    turn = lax.rem(2 * LANES - 2 * level, LANES)
-    level_f = level.astype(f32)
-
-    def beside(array, ends):
-        ends = pltpu.roll(ends, turn, 1)
-        lanes = lane[: array.shape[0]]
-        parts = [array[:, at : at + LANES] for at in range(0, width, LANES)]
-        right = [roll_lanes(part, -1) for part in parts] + [ends]
-        left = [ends] + [roll_lanes(part, 1) for part in parts]
-        east = [jnp.where(lanes == LANES - 1, b, a) for a, b in zip(right, right[1:])]
-        west = [jnp.where(lanes == 0, a, b) for a, b in zip(left, left[1:])]
-        return jnp.concatenate(east, axis=1), jnp.concatenate(west, axis=1)
-
-    east, west = beside(whole, ends_temp)
-    north, south = roll_rows(whole, -1), roll_rows(whole, 1)
-    opens = [level_f < limit for limit in limits]
-    lap = -4.0 * whole
-    for around, is_open in zip((east, west, north, south), opens):
-        lap = lap + jnp.where(is_open, around, whole)
-    own = whole[:rows]
+    side = turned(ends[2], level)
+    parts = [lap[:, at : at + LANES] for at in range(0, width, LANES)]
+    parts[0] = parts[0] + jnp.where(lane == 0, side, 0.0)
+    parts[-1] = parts[-1] + jnp.where(lane == LANES - 1, side, 0.0)
+    lap = jnp.concatenate(parts, axis=1)
+    whole = jnp.concatenate([own, halo_level], axis=0)
     own_lap = lap[:rows]
-    lap_east, lap_west = beside(own_lap, ends_lap)
-    lap_north, lap_south = roll_rows(lap, -1)[:rows], roll_rows(lap, 1)[:rows]
-    opens = [is_open[:rows] for is_open in opens]
-    mixing = -4.0 * own_lap
-    for around, is_open in zip((lap_east, lap_west, lap_north, lap_south), opens):
-        mixing = mixing + jnp.where(is_open, around, own_lap)
-    carried = [
-        jnp.where(is_open, speed * (around[:rows] + own), 0.0)
-        for around, is_open, speed in zip((east, west, north, south), opens, speeds)
-    ]
-    advect = carried[0] - carried[1] + carried[2] - carried[3]
-    return -advect_coef * advect - mixing_fourth * mixing
-
-
-def level_update(level, own, lateral, down, down_before, counts, solar, heat):
-    level_f = level.astype(f32)
-    absorb = jnp.exp(jnp.full(own.shape, -1.0 / light_decay, f32) * level_f)
-    absorb = absorb * (light_gain * (1.0 - math.exp(-1.0 / light_decay)))
-    source = absorb * solar + jnp.where(level == 0, heat_gain, 0.0) * heat
-    change = diapycnal_diffusion * (down - down_before) + lateral + source
-    return own + jnp.where(level_f < counts, change, 0.0)
+    around_temp = sideways(own, turned(ends[0][:rows], level))
+    around_temp += (roll_rows(whole, -1)[:rows], roll_rows(whole, 1)[:rows])
+    around_lap = sideways(own_lap, turned(ends[1][:rows], level))
+    around_lap += (roll_rows(lap, -1)[:rows], roll_rows(lap, 1)[:rows])
+    change = jnp.zeros((rows, width), f32)
+    for place, limit in enumerate(limits):
+        moved = mixing_fourth * (own_lap - around_lap[place])
+        moved = moved - speeds[place] * (around_temp[place] + own)
+        change = change + jnp.where(level_f < limit, moved, 0.0)
+    return base + change
 
 
 def hot_body(points, hot):
     links, rows, width = points.shape
     blocks = width // LANES
-    lane = lane_ids(LANES)
-    lines = [
-        points[k, :, b * LANES : (b + 1) * LANES] for k in range(links) for b in range(blocks)
-    ]
-    held = []
-    for at in range(0, len(lines) * rows, LANES):
-        group = lines[at // rows : (at + LANES) // rows]
-        held.append(jnp.transpose(jnp.concatenate(group, axis=0).astype(f32)).astype(i32))
-    for at in range(links * blocks * rows):
-        column = held[at // LANES][:, at % LANES : at % LANES + 1]
-        hot[at] = (column == lane).astype(f32).astype(jnp.bfloat16)
+    cells = row_ids(LANES).astype(f32).astype(jnp.bfloat16)
+    one, none = jnp.bfloat16(1.0), jnp.bfloat16(0.0)
+    for k in range(links):
+        for b in range(blocks):
+            for row in range(rows):
+                line = points[k, row : row + 1, b * LANES : (b + 1) * LANES]
+                line = jnp.broadcast_to(line.astype(f32), (2 * TILE, LANES)).astype(jnp.bfloat16)
+                line = jnp.concatenate([line] * (LANES // (2 * TILE)), axis=0)
+                hot[(k * blocks + b) * rows + row] = jnp.transpose(jnp.where(line == cells, one, none))
 
 
 def subcycle_body(
     levels,
     ext,
-    light,
     edges_own,
     edges_halo,
     got_a,
     got_b,
     temp,
-    halo_near,
-    lat_b,
+    halo,
+    base,
+    laps,
     hot,
     weights,
     tile_hbm,
@@ -556,13 +595,13 @@
     limit_north = jnp.minimum(counts, north_of(counts))
     limit_west, limit_south = west_of(limit_east), south_of(limit_north)
     limits = [
-        limit[:, :width] for limit in (limit_east, limit_west, limit_north, limit_south)
+        limit[:rows, :width] for limit in (limit_east, limit_west, limit_north, limit_south)
     ]
-    speed_east = 0.5 * zonal / jnp.maximum(east_depth, depth_floor)
-    speed_north = 0.5 * merid / jnp.maximum(north_depth, depth_floor)
+    speed_east = 0.5 * advect_coef * zonal / jnp.maximum(east_depth, depth_floor)
+    speed_north = 0.5 * advect_coef * merid / jnp.maximum(north_depth, depth_floor)
     speeds = [
         speed[:rows, :width]
-        for speed in (speed_east, west_of(speed_east), speed_north, south_of(speed_north))
+        for speed in (speed_east, -west_of(speed_east), speed_north, -south_of(speed_north))
     ]
     for place in range(4):
         limits_out[place] = limits[place]
@@ -597,24 +636,18 @@
     lap_east = edge_lap(
         far_east, roll_lanes(far_east, -1), roll_lanes(edges[1], -1), width, width - 1
     )
-    ends_temp = roll_lanes(jnp.where(odd_lane, far_west, far_east), -1)
-    ends_lap = roll_lanes(jnp.where(odd_lane, lap_west, lap_east), -1)
-    ends_out[0] = ends_temp
-    ends_out[1] = ends_lap
-
-    own_counts = counts[:rows, :width]
+    side_west = far_west - roll_lanes(edges[0], 1)
+    side_west = jnp.where(lane_level < column(limit_east, total_lanes - 1), side_west, 0.0)
+    side_east = far_east - roll_lanes(edges[1], -1)
+    side_east = jnp.where(lane_level < column(limit_east, width - 1), side_east, 0.0)
+    ends = []
+    for west, east in ((far_west, far_east), (lap_west, lap_east), (side_west, side_east)):
+        ends.append(roll_lanes(jnp.where(odd_lane, west, east), -1))
+    for place in range(3):
+        ends_out[place] = ends[place]
+
     zero = jnp.zeros((), i32)
-    top_halo = jnp.where(near_lanes(width), halo_near[0], lat_b[lat_b.shape[0] - 3])
-    lateral = level_tendency(
-        zero, temp[0], top_halo, ends_temp, ends_lap[:rows], limits, speeds
-    )
-    if levels > 1:
-        down = jnp.where(own_counts > 1.0, temp[1] - temp[0], 0.0)
-    else:
-        down = jnp.zeros((rows, width), f32)
-    top = level_update(
-        zero, temp[0], lateral, down, jnp.zeros_like(down), own_counts, light[1], light[0]
-    )
+    top = finish_level(zero, temp[0], halo[0], base[0], laps[0], ends, limits, speeds)
     own_wet = wet[:rows, :width]
     thick = jnp.maximum(depth[:rows, :width], depth_floor)
     surface = [
@@ -657,62 +690,42 @@
         sums_b[place] = jnp.where(even, south, north)
 
 
-LEVELS_AT_ONCE = 6
-
-
-def run_levels(first, count, temp, halo, limits, speeds, ends, light, state, out, done=None):
-    levels, rows, width = temp.shape
-    own_counts = state[3]
+def run_levels(first, count, temp, halo, base, laps, limits, speeds, ends, out, done=None):
     step = math.gcd(count, LEVELS_AT_ONCE)
 
-    def falls(level):
-        beneath = temp[jnp.minimum(level + 1, levels - 1)]
-        return jnp.where((level + 1).astype(f32) < own_counts, beneath - temp[level], 0.0)
-
-    def group(at, down_before):
+    def group(at, carry):
         for inner in range(step):
             level = first + at * step + inner
-            own = temp[level]
-            lateral = level_tendency(
+            out[at * step + inner] = finish_level(
                 level,
-                own,
+                temp[level],
                 halo[level],
-                ends[0],
-                ends[1, :rows],
+                base[level],
+                laps[level],
+                [ends[place] for place in range(3)],
                 [limits[place] for place in range(4)],
                 [speeds[place] for place in range(4)],
             )
-            down = falls(level)
-            out[at * step + inner] = level_update(
-                level, own, lateral, down, down_before, own_counts, light[1], light[0]
-            )
-            down_before = down
         if done is not None:
             done(at, step)
-        return down_before
-
-    start = falls(jnp.int32(first - 1)) if first else jnp.zeros((rows, width), f32)
-    lax.fori_loop(0, count // step, group, start)
-
-
-def upper_body(count, temp, halo_near, limits, speeds, ends, light, state, got_b, out, halo):
-    even = lax.rem(lax.axis_index("lat"), 2) == 0
-    near = near_lanes(temp.shape[2])
-    for level in range(temp.shape[0]):
-        rows = unpack_rows(jnp.logical_not(even), got_b[level // 4], level)
-        halo[level] = jnp.where(near, halo_near[level], rows)
-    run_levels(0, count, temp, halo, limits, speeds, ends, light, state, out)
+        return carry
+
+    lax.fori_loop(0, count // step, group, 0)
+
+
+def upper_body(count, temp, halo, base, laps, limits, speeds, ends, out):
+    run_levels(0, count, temp, halo, base, laps, limits, speeds, ends, out)
 
 
 def lower_body(
     first,
     temp,
     halo,
+    base,
+    laps,
     limits,
     speeds,
     ends,
-    light,
-    state,
     upper,
     height,
     zonal,
@@ -764,11 +777,11 @@
         count,
         temp,
         halo,
+        base,
+        laps,
         limits,
         speeds,
         ends,
-        light,
-        state,
         lower,
         lambda at, step: level_copy(at, step).start(),
     )
@@ -799,7 +812,8 @@
     nsums = 5
     fields = 4 + 2 * links
     flux_at = fields // 2
-    temp_at = flux_at + (nflux + 1) // 2
+    flux_tiles = (nflux + 2) // 2
+    temp_at = flux_at + flux_tiles
     groups = pl.cdiv(levels, 4)
     tile_lines = jnp.swapaxes(donor_tile_number, 1, 2)
     edge_a, own, state, points, weights, flags, temp = call(
@@ -826,7 +840,7 @@
             thermal_field,
         ),
         "load",
-        1.5,
+        1.6,
         scratch=[
             pltpu.VMEM((rows, width), i32),
             pltpu.VMEM((links, blocks, rows), i32),
@@ -836,10 +850,11 @@
         hbm=range(10),
     )
     got_a = swap(edge_a, "lat", 0, False)
+    edge_tiles = temp_at + 1 + (len(HALO_FLUXES) + 1) // 2
     draft_b, temp_b, edges = call(
         pack_second_body,
         [
-            shape(temp_at + 4, TILE, width),
+            shape(edge_tiles, TILE, width),
             shape(groups, TILE, width),
             shape(2, rows, LANES),
         ],
@@ -849,10 +864,10 @@
     )
     (edge_b,) = call(
         functools.partial(pack_flux_body, flux_at),
-        [shape(temp_at + 4, TILE, width)],
+        [shape(edge_tiles, TILE, width)],
         (draft_b, got_a),
-        "pack_b_flux",
-        0.02,
+        "pack_flux",
+        0.0,
         aliases={0: 0},
     )
     got_b = swap(edge_b, "lat", 1, False)
@@ -865,7 +880,7 @@
         [shape(len(HALO_FLUXES), TILE, LANES)],
         (got_b,),
         "pack_c",
-        0.02,
+        LATE,
     )
     got_c = swap(edge_c, "lat", 0, False)
     draft_ext, light = call(
@@ -876,11 +891,11 @@
         0.4,
     )
     halo_near, edges_near = call(
-        functools.partial(unpack_first_body, temp_at),
+        functools.partial(unpack_near_body, temp_at),
         [shape(levels, TILE, width), shape(2, TILE, LANES)],
         (got_a,),
         "unpack_a",
-        0.2,
+        0.0,
     )
     ext, send_a, send_b, edges_halo = call(
         functools.partial(forcing_halo_body, flux_at),
@@ -905,7 +920,19 @@
         [shape(links * blocks * rows, LANES, LANES, dtype=jnp.bfloat16)],
         (points,),
         "hot",
-        2.5,
+        0.0,
+    )
+    base, laps, halo = call(
+        before_body,
+        [
+            shape(levels, rows, width),
+            shape(levels, 3 * TILE, width),
+            shape(levels, TILE, width),
+        ],
+        (ext, light, temp, halo_near, got_temp_b),
+        "before",
+        0.0,
+        aliases={3: 2},
     )
     (
         advanced_elevation,
@@ -920,18 +947,18 @@
     ) = call(
         functools.partial(subcycle_body, levels),
         [shape(rows, width)] * 3
-        + [shape(4, 3 * TILE, width), shape(4, rows, width), shape(2, 3 * TILE, LANES)]
+        + [shape(4, rows, width), shape(4, rows, width), shape(3, 3 * TILE, LANES)]
         + [shape(nsums, TILE, LANES)] * 3,
         (
             ext,
-            light,
             edges,
             edges_halo,
             lon_a,
             lon_b,
             temp,
-            halo_near,
-            got_b,
+            halo,
+            base,
+            laps,
             hot,
             weights,
             tile_lines,
@@ -951,17 +978,15 @@
         pass_body, [shape(nsums, TILE, LANES)], (sums_a, sums_b), "pass_sums", LATE, aliases={0: 0}
     )
     back_a = swap(sums_a, "lat", 0, False)
-    first = levels // 10 * 6
-    tracer = (temp, halo_near, limits, speeds, ends, light, state)
-    upper, halo = call(
+    first = levels // 10 * 9
+    tracer = (temp, halo, base, laps, limits, speeds, ends)
+    (upper,) = call(
         functools.partial(upper_body, first),
-        [shape(first, rows, width), shape(levels, TILE, width)],
-        tracer + (got_temp_b,),
+        [shape(first, rows, width)],
+        tracer,
         "tracer_upper",
         2.3,
-        aliases={1: 1},
-    )
-    tracer = (temp, halo, limits, speeds, ends, light, state)
+    )
     return call(
         functools.partial(lower_body, first),
         [

time: 32.9 us -> 31.5 us (0.957)
  the two profiles are of different devices: /device:TPU:1 before, /device:TPU:0 now
where the time goes in v3:
time: 31.5 us; the launch traced here: 31.3 us
  starting transfers between devices  17.1 us (54%)
  Pallas kernels  12 us (38%)
  waiting for transfers between devices  1.39 us (4%)
  between operations  0.76 us (2%)
    ppermute x8, starting transfers between devices, swap(): lax.ppermute(array, axis, swap_pairs(lax.axis_size(axis), first, periodic))  17.1 us
    pallas_call x15, Pallas kernels, call(): pl.pallas_call(body, out_shape=outs, in_specs=specs, out_specs=[pl.BlockS...  12 us
    ppermute x8, waiting for transfers between devices, swap(): lax.ppermute(array, axis, swap_pairs(lax.axis_size(axis), first, periodic))  1.39 us
  transfers between devices with their start and end apart: 8, of which 3 were waited for; matrix products, arithmetic and copies ran while one was open for 0% of the time, Pallas kernels for 21%

profile of v3, /device:TPU:0, one launch (start us, length us, event | category | flops | bytes accessed | tf_op | source)
XLA Modules:
  0.0 31.3 jit_solution(8153293015076378148)
XLA Ops:
  0.6 1.5 %load.1 = (f32[24,8,256]{2,1,0:T(8,128)S(1)}, f32[7,8,128]{2,1,0:T(8,128)S(1)}, f32[4,16,256]{2,1,0:T(8,128)S(1)}, s32[4,16,256]{2,1,0:T(8,128)S(1)}, f32[4,16,2...) custom-call(f32[16,256]{1,0:T(8,128)} %height.1, f32[16,256]{1,0:T(8,128)} %zonal.1, ...), custom_call_target="tpu_custom_call" | custom-call | flops 1840000000 | bytes 1024 | tf_op jit(solution)/shard_map/load/pallas_call | solution.py:80
  2.2 0.5 %collective-permute-start = (f32[24,8,256]{2,1,0:T(8,128)S(1)}, f32[24,8,256]{2,1,0:T(8,128)S(1)}, u32[]{:S(2)}, u32[]{:S(2)}) collective-permute-start(f32[24,8,256]{2,1,0:T(8,128)S(1)} %get-tuple-element.36), channel_id=1, source_target_pairs={{0,1},{1,0},{2,3},{3,2},{4,5},{5,4},{6,7},{7,6},{8,9},{9,8},{10,11... | collective-permute-start | bytes 589832 | tf_op jit(solution)/shard_map/ppermute | solution.py:50
  2.7 0.3 pack_b.1
  3.0 0.8 %collective-permute-done.received.got_a = f32[24,8,256]{2,1,0:T(8,128)S(1)} collective-permute-done((f32[24,8,256]{2,1,0:T(8,128)S(1)}, f32[24,8,256]{2,1,0:T(8,128)S(1)}, u32[]{:S(2)}, u32[]{:S(2)}) %collective-permute-start) | collective-permute-done | bytes 196640 | tf_op jit(solution)/shard_map/ppermute | solution.py:50
  3.8 0.7 %collective-permute-start.1 = (f32[12,8,256]{2,1,0:T(8,128)S(1)}, f32[12,8,256]{2,1,0:T(8,128)S(1)}, u32[]{:S(2)}, u32[]{:S(2)}) collective-permute-start(f32[12,8,256]{2,1,0:T(8,128)S(1)} %pack_flux.1.second), channel_id=1, source_target_pairs={{1,2},{2,1},{3,4},{4,3},{5,6},{6,5},{9,10},{10,9},{11,12},{12,11},... | collective-permute-start | bytes 294920 | tf_op jit(solution)/shard_map/ppermute | solution.py:50
  4.4 0.7 %collective-permute-start.3 = (f32[15,8,256]{2,1,0:T(8,128)S(1)}, f32[15,8,256]{2,1,0:T(8,128)S(1)}, u32[]{:S(2)}, u32[]{:S(2)}) collective-permute-start(f32[15,8,256]{2,1,0:T(8,128)S(1)} %pass_temp.1), channel_id=1, source_target_pairs={{1,2},{2,1},{3,4},{4,3},{5,6},{6,5},{9,10},{10,9},{11,12},{12,11},... | collective-permute-start | bytes 368648 | tf_op jit(solution)/shard_map/ppermute | solution.py:50
  5.1 0.2 unpack_a.1
  5.3 0.0 collective-permute-done.1.got_b.received
  5.3 5.8 %collective-permute-start.2 = (f32[3,8,128]{2,1,0:T(8,128)S(1)}, f32[3,8,128]{2,1,0:T(8,128)S(1)}, u32[]{:S(2)}, u32[]{:S(2)}) collective-permute-start(f32[3,8,128]{2,1,0:T(8,128)S(1)} %pack_c.1), channel_id=1, source_target_pairs={{0,1},{1,0},{2,3},{3,2},{4,5},{5,4},{6,7},{7,6},{8,9},{9,8},{10,11... | collective-permute-start | bytes 36872 | tf_op jit(solution)/shard_map/ppermute | solution.py:50
  11.1 0.4 %forcing.1 = (f32[7,24,256]{2,1,0:T(8,128)S(1)}, f32[2,16,256]{2,1,0:T(8,128)S(1)}) custom-call(f32[24,8,256]{2,1,0:T(8,128)S(1)} %collective-permute-done.received.got_a, f32[12,8,256]{2,1,0:T(8,128)S(1)} %collective-permute-done.1.got_b.received, f32[7,8,128]{2,1,0:T(8,128)S(1)} %get-tuple-element.37.own, f32[4,16,256]{2,1,0:T(8,128)S(1)} %get-tuple-element.38.state, ...), custom_call_target="tpu_custom_call" | custom-call | flops 460000000 | bytes 1024 | tf_op jit(solution)/shard_map/forcing/pallas_call | solution.py:80
  11.5 0.5 %collective-permute-done.2.got_c = f32[3,8,128]{2,1,0:T(8,128)S(1)} collective-permute-done((f32[3,8,128]{2,1,0:T(8,128)S(1)}, f32[3,8,128]{2,1,0:T(8,128)S(1)}, u32[]{:S(2)}, u32[]{:S(2)}) %collective-permute-start.2) | collective-permute-done | bytes 12320 | tf_op jit(solution)/shard_map/ppermute | solution.py:50
  11.9 0.3 forcing_halo.1
  12.2 2.2 %collective-permute-start.4 = (f32[2,24,128]{2,1,0:T(8,128)S(1)}, f32[2,24,128]{2,1,0:T(8,128)S(1)}, u32[]{:S(2)}, u32[]{:S(2)}) collective-permute-start(f32[2,24,128]{2,1,0:T(8,128)S(1)} %pass_lon.1), channel_id=1, source_target_pairs={{0,8},{8,0},{16,24},{24,16},{1,9},{9,1},{17,25},{25,17},{2,10},{10... | collective-permute-start | bytes 73736 | tf_op jit(solution)/shard_map/ppermute | solution.py:50
  14.4 2.5 %collective-permute-start.5 = (f32[2,24,128]{2,1,0:T(8,128)S(1)}, f32[2,24,128]{2,1,0:T(8,128)S(1)}, u32[]{:S(2)}, u32[]{:S(2)}) collective-permute-start(f32[2,24,128]{2,1,0:T(8,128)S(1)} %get-tuple-element.54.second), channel_id=1, source_target_pairs={{8,16},{16,8},{24,0},{0,24},{9,17},{17,9},{25,1},{1,25},{10,18},{1... | collective-permute-start | bytes 73736 | tf_op jit(solution)/shard_map/ppermute | solution.py:50
  16.9 1.1 %hot.1 = bf16[128,128,128]{2,1,0:T(8,128)(2,1)S(1)} custom-call(s32[4,16,256]{2,1,0:T(8,128)S(1)} %get-tuple-element.39.points), custom_call_target="tpu_custom_call" | custom-call | bytes 1024 | tf_op jit(solution)/shard_map/hot/pallas_call | solution.py:80
  18.0 0.0 collective-permute-done.3.got_b
  18.1 1.8 %before.1 = (f32[60,16,256]{2,1,0:T(8,128)S(1)}, f32[60,24,256]{2,1,0:T(8,128)S(1)}, f32[60,8,256]{2,1,0:T(8,128)S(1)}) custom-call(f32[7,24,256]{2,1,0:T(8,128)S(1)} %get-tuple-element.45.ext, f32[2,16,256]{2,1,0:T(8,128)S(1)} %get-tuple-element.46.light, f32[60,16,256]{2,1,0:T(8,128)S(1)} %get-tuple-element.35.temp, ...), custom_call_target="tpu_custom_call", output_to_operand_aliasing={{2}: (3, {})} | custom-call | bytes 1024 | tf_op jit(solution)/shard_map/before/pallas_call | solution.py:80
  19.9 0.0 collective-permute-done.4.got_a
  19.9 0.1 collective-permute-done.5.got_b
  20.1 2.6 %subcycles.1 = (f32[16,256]{1,0:T(8,128)S(1)}, f32[16,256]{1,0:T(8,128)S(1)}, f32[16,256]{1,0:T(8,128)S(1)}, f32[4,16,256]{2,1,0:T(8,128)S(1)}, f32[4,16,256]{2,...) custom-call(f32[7,24,256]{2,1,0:T(8,128)S(1)} %get-tuple-element.45., ...), custom_call_target="tpu_custom_call" | custom-call | flops 2990000128 | bytes 1024 | tf_op jit(solution)/shard_map/subcycles/pallas_call | solution.py:80
  22.6 0.7 %collective-permute-start.7 = (f32[5,8,128]{2,1,0:T(8,128)S(1)}, f32[5,8,128]{2,1,0:T(8,128)S(1)}, u32[]{:S(2)}, u32[]{:S(2)}) collective-permute-start(f32[5,8,128]{2,1,0:T(8,128)S(1)} %get-tuple-element.63.second), channel_id=1, source_target_pairs={{1,2},{2,1},{3,4},{4,3},{5,6},{6,5},{9,10},{10,9},{11,12},{12,11},... | collective-permute-start | bytes 61448 | tf_op jit(solution)/shard_map/ppermute | solution.py:50
  23.3 4.1 %collective-permute-start.6 = (f32[5,8,128]{2,1,0:T(8,128)S(1)}, f32[5,8,128]{2,1,0:T(8,128)S(1)}, u32[]{:S(2)}, u32[]{:S(2)}) collective-permute-start(f32[5,8,128]{2,1,0:T(8,128)S(1)} %pass_sums.1), channel_id=1, source_target_pairs={{0,1},{1,0},{2,3},{3,2},{4,5},{5,4},{6,7},{7,6},{8,9},{9,8},{10,11... | collective-permute-start | bytes 61448 | tf_op jit(solution)/shard_map/ppermute | solution.py:50
  27.4 2.5 %tracer_upper.1.upper = f32[54,16,256]{2,1,0:T(8,128)S(1)} custom-call(f32[60,16,256]{2,1,0:T(8,128)S(1)} %get-tuple-element.35.temp, f32[60,8,256]{2,1,0:T(8,128)S(1)} %get-tuple-element.49.halo, f32[60,16,256]{2,1,0:T(8,128)S(1)} %get-tuple-element.50.base, f32[60,24,256]{2,1,0:T(8,128)S(1)} %get-tuple-element.51.laps, ...), custom_call_target="tpu_custom_call" | custom-call | flops 2644999936 | bytes 1024 | tf_op jit(solution)/shard_map/tracer_upper/pallas_call | solution.py:80
  30.0 0.0 collective-permute-done.6.got_a
  30.0 0.0 collective-permute-done.7.got_b
  30.0 1.3 %tracer_lower.1 = (f32[16,256]{1,0:T(8,128)}, f32[16,256]{1,0:T(8,128)}, f32[16,256]{1,0:T(8,128)}, f32[60,16,256]{2,1,0:T(8,128)}, f32[4,8,128]{2,1,0:T(8,128)}) custom-call(f32[60,16,256]{2,1,0:T(8,128)S(1)} %get-tuple-element.35.temp, f32[60,8,256]{2,1,0:T(8,128)S(1)} %get-tuple-element.49.halo, f32[60,16,256]{2,1,0:T(8,128)S(1)} %get-tuple-element.50.base, ...), custom_call_target="tpu_custom_call" | custom-call | flops 2760000000 | bytes 1024 | tf_op jit(solution)/shard_map/tracer_lower/pallas_call | solution.py:80
  (5 shorter events, 0.0 us)
Async XLA Ops:
  2.2 1.6 %collective-permute-start = (f32[24,8,256]{2,1,0:T(8,128)S(1)}, f32[24,8,256]{2,1,0:T(8,128)S(1)}, u32[]{:S(2)}, u32[]{:S(2)}) collective-permute-start(f32[24,8,256]{2,1,0:T(8,128)S(1)} %get-tuple-element.36), channel_id=1, source_target_pairs={{0,1},{1,0},{2,3},{3,2},{4,5},{5,4},{6,7},{7,6},{8,9},{9,8},{10,11... | collective-permute-start | bytes 589832 | tf_op jit(solution)/shard_map/ppermute | solution.py:50
  3.8 1.6 %collective-permute-start.1 = (f32[12,8,256]{2,1,0:T(8,128)S(1)}, f32[12,8,256]{2,1,0:T(8,128)S(1)}, u32[]{:S(2)}, u32[]{:S(2)}) collective-permute-start(f32[12,8,256]{2,1,0:T(8,128)S(1)} %pack_flux.1.second), channel_id=1, source_target_pairs={{1,2},{2,1},{3,4},{4,3},{5,6},{6,5},{9,10},{10,9},{11,12},{12,11},... | collective-permute-start | bytes 294920 | tf_op jit(solution)/shard_map/ppermute | solution.py:50
  4.4 13.6 %collective-permute-start.3 = (f32[15,8,256]{2,1,0:T(8,128)S(1)}, f32[15,8,256]{2,1,0:T(8,128)S(1)}, u32[]{:S(2)}, u32[]{:S(2)}) collective-permute-start(f32[15,8,256]{2,1,0:T(8,128)S(1)} %pass_temp.1), channel_id=1, source_target_pairs={{1,2},{2,1},{3,4},{4,3},{5,6},{6,5},{9,10},{10,9},{11,12},{12,11},... | collective-permute-start | bytes 368648 | tf_op jit(solution)/shard_map/ppermute | solution.py:50
  5.3 6.6 %collective-permute-start.2 = (f32[3,8,128]{2,1,0:T(8,128)S(1)}, f32[3,8,128]{2,1,0:T(8,128)S(1)}, u32[]{:S(2)}, u32[]{:S(2)}) collective-permute-start(f32[3,8,128]{2,1,0:T(8,128)S(1)} %pack_c.1), channel_id=1, source_target_pairs={{0,1},{1,0},{2,3},{3,2},{4,5},{5,4},{6,7},{7,6},{8,9},{9,8},{10,11... | collective-permute-start | bytes 36872 | tf_op jit(solution)/shard_map/ppermute | solution.py:50
  12.2 7.7 %collective-permute-start.4 = (f32[2,24,128]{2,1,0:T(8,128)S(1)}, f32[2,24,128]{2,1,0:T(8,128)S(1)}, u32[]{:S(2)}, u32[]{:S(2)}) collective-permute-start(f32[2,24,128]{2,1,0:T(8,128)S(1)} %pass_lon.1), channel_id=1, source_target_pairs={{0,8},{8,0},{16,24},{24,16},{1,9},{9,1},{17,25},{25,17},{2,10},{10... | collective-permute-start | bytes 73736 | tf_op jit(solution)/shard_map/ppermute | solution.py:50
  14.4 5.6 %collective-permute-start.5 = (f32[2,24,128]{2,1,0:T(8,128)S(1)}, f32[2,24,128]{2,1,0:T(8,128)S(1)}, u32[]{:S(2)}, u32[]{:S(2)}) collective-permute-start(f32[2,24,128]{2,1,0:T(8,128)S(1)} %get-tuple-element.54.second), channel_id=1, source_target_pairs={{8,16},{16,8},{24,0},{0,24},{9,17},{17,9},{25,1},{1,25},{10,18},{1... | collective-permute-start | bytes 73736 | tf_op jit(solution)/shard_map/ppermute | solution.py:50
  22.6 7.4 %collective-permute-start.7 = (f32[5,8,128]{2,1,0:T(8,128)S(1)}, f32[5,8,128]{2,1,0:T(8,128)S(1)}, u32[]{:S(2)}, u32[]{:S(2)}) collective-permute-start(f32[5,8,128]{2,1,0:T(8,128)S(1)} %get-tuple-element.63.second), channel_id=1, source_target_pairs={{1,2},{2,1},{3,4},{4,3},{5,6},{6,5},{9,10},{10,9},{11,12},{12,11},... | collective-permute-start | bytes 61448 | tf_op jit(solution)/shard_map/ppermute | solution.py:50
  23.3 6.7 %collective-permute-start.6 = (f32[5,8,128]{2,1,0:T(8,128)S(1)}, f32[5,8,128]{2,1,0:T(8,128)S(1)}, u32[]{:S(2)}, u32[]{:S(2)}) collective-permute-start(f32[5,8,128]{2,1,0:T(8,128)S(1)} %pass_sums.1), channel_id=1, source_target_pairs={{0,1},{1,0},{2,3},{3,2},{4,5},{5,4},{6,7},{7,6},{8,9},{9,8},{10,11... | collective-permute-start | bytes 61448 | tf_op jit(solution)/shard_map/ppermute | solution.py:50

commit v4 on v3

--- a/solution.py
+++ b/solution.py
@@ -506,7 +506,9 @@
                 line = points[k, row : row + 1, b * LANES : (b + 1) * LANES]
                 line = jnp.broadcast_to(line.astype(f32), (2 * TILE, LANES)).astype(jnp.bfloat16)
                 line = jnp.concatenate([line] * (LANES // (2 * TILE)), axis=0)
-                hot[(k * blocks + b) * rows + row] = jnp.transpose(jnp.where(line == cells, one, none))
+                hot[k * rows + row, :, b * LANES : (b + 1) * LANES] = jnp.transpose(
+                    jnp.where(line == cells, one, none)
+                )
 
 
 def subcycle_body(
@@ -532,6 +534,7 @@
     sums_a,
     sums_b,
     sums_mid,
+    whole,
     values,
     table,
     tile,
@@ -673,15 +676,14 @@
             upper = shares.astype(jnp.bfloat16)
             lower = (shares - upper.astype(f32)).astype(jnp.bfloat16)
             both = jnp.concatenate([upper, lower], axis=0)
+            stacked = jnp.concatenate(
+                [both[:, b * LANES : (b + 1) * LANES] for b in range(blocks)], axis=0
+            )
+            found = jnp.dot(stacked, hot[k * rows + row], preferred_element_type=f32)
             for b in range(blocks):
-                cols = slice(b * LANES, (b + 1) * LANES)
-                found = jnp.dot(
-                    both[:, cols],
-                    hot[(k * blocks + b) * rows + row],
-                    preferred_element_type=f32,
-                )
                 target = tile[k, b, row]
-                table[target] = table[target] + found
+                mine = found[b * 2 * TILE : (b + 1) * 2 * TILE, b * LANES : (b + 1) * LANES]
+                table[target] = table[target] + mine
     for place in range(nsums):
         total = table[:, place, :] + table[:, TILE + place, :]
         south, middle, north = total[:TILE], total[TILE : 2 * TILE], total[2 * TILE :]
@@ -689,14 +691,41 @@
         sums_a[place] = jnp.where(even, north, south)
         sums_b[place] = jnp.where(even, south, north)
 
-
-def run_levels(first, count, temp, halo, base, laps, limits, speeds, ends, out, done=None):
-    step = math.gcd(count, LEVELS_AT_ONCE)
+    run_levels(
+        0,
+        early_groups(levels),
+        temp,
+        halo,
+        base,
+        laps,
+        limits_out,
+        speeds_out,
+        ends_out,
+        whole,
+    )
+
+
+def level_step(levels):
+    return math.gcd(levels, LEVELS_AT_ONCE)
+
+
+def early_groups(levels):
+    groups = levels // level_step(levels)
+    place = lax.axis_index("lat")
+    inner = jnp.where(lax.rem(place, 2) == 1, groups // 5, 0)
+    return jnp.where(place == 0, groups // 2, inner)
+
+
+LAST_GROUPS = 2
+
+
+def run_levels(start, stop, temp, halo, base, laps, limits, speeds, ends, out, done=None):
+    step = level_step(temp.shape[0])
 
     def group(at, carry):
         for inner in range(step):
-            level = first + at * step + inner
-            out[at * step + inner] = finish_level(
+            level = jnp.int32(at * step + inner)
+            out[level] = finish_level(
                 level,
                 temp[level],
                 halo[level],
@@ -707,18 +736,13 @@
                 [speeds[place] for place in range(4)],
             )
         if done is not None:
-            done(at, step)
+            done(at)
         return carry
 
-    lax.fori_loop(0, count // step, group, 0)
-
-
-def upper_body(count, temp, halo, base, laps, limits, speeds, ends, out):
-    run_levels(0, count, temp, halo, base, laps, limits, speeds, ends, out)
-
-
-def lower_body(
-    first,
+    lax.fori_loop(start, stop, group, 0)
+
+
+def tracer_body(
     temp,
     halo,
     base,
@@ -726,70 +750,67 @@
     limits,
     speeds,
     ends,
-    upper,
+    draft,
     height,
     zonal,
     merid,
-    mid,
-    got_a,
-    got_b,
-    flags,
     out_height,
     out_zonal,
     out_merid,
     out,
-    out_surface,
-    lower,
-    surface,
+    whole,
     sems,
     level_sems,
 ):
-    open_sea = (1 - flags[...]).astype(f32)
-    nsurf = surface.shape[0]
-    area = mid[nsurf] + got_a[nsurf] + got_b[nsurf]
-    scale = open_sea / jnp.maximum(area, area_floor)
-    for place in range(nsurf):
-        surface[place] = (mid[place] + got_a[place] + got_b[place]) * scale
-    pairs = [
-        (surface, out_surface),
-        (upper, out.at[pl.ds(0, first)]),
-        (height, out_height),
-        (zonal, out_zonal),
-        (merid, out_merid),
-    ]
+    levels = temp.shape[0]
+    step = level_step(levels)
+    groups = levels // step
+    pairs = [(height, out_height), (zonal, out_zonal), (merid, out_merid)]
     copies = [
         pltpu.make_async_copy(source, target, sems.at[place])
         for place, (source, target) in enumerate(pairs)
     ]
     for copy in copies:
         copy.start()
-    count = temp.shape[0] - first
-
-    def level_copy(at, step):
-        return pltpu.make_async_copy(
-            lower.at[pl.ds(at * step, step)],
-            out.at[pl.ds(first + at * step, step)],
-            level_sems.at[at],
-        )
-
-    run_levels(
-        first,
-        count,
-        temp,
-        halo,
-        base,
-        laps,
-        limits,
-        speeds,
-        ends,
-        lower,
-        lambda at, step: level_copy(at, step).start(),
-    )
-    step = math.gcd(count, LEVELS_AT_ONCE)
-    for at in range(count // step):
-        level_copy(at, step).wait()
+
+    def level_copy(at):
+        part = pl.ds(at * step, step)
+        return pltpu.make_async_copy(whole.at[part], out.at[part], level_sems.at[at])
+
+    early = early_groups(levels)
+
+    def start(at, carry):
+        level_copy(at).start()
+        return carry
+
+    lax.fori_loop(0, early, start, 0)
+    inside = max(groups - LAST_GROUPS, 0)
+    refs = (temp, halo, base, laps, limits, speeds, ends, whole)
+    run_levels(early, inside, *refs, lambda at: level_copy(at).start())
+    run_levels(inside, groups, *refs)
+    for at in range(inside):
+        level_copy(at).wait()
     for copy in copies:
         copy.wait()
+
+
+def merge_body(mid, got_a, got_b, flags, whole, draft, out, out_temp, surface, sems):
+    levels = whole.shape[0]
+    step = level_step(levels)
+    first = step * max(levels // step - LAST_GROUPS, 0)
+    part = pl.ds(first, levels - first)
+    rest = pltpu.make_async_copy(whole.at[part], out_temp.at[part], sems.at[0])
+    rest.start()
+    open_sea = (1 - flags[...]).astype(f32)
+    nsurf = out.shape[0]
+    area = mid[nsurf] + got_a[nsurf] + got_b[nsurf]
+    scale = open_sea / jnp.maximum(area, area_floor)
+    for place in range(nsurf):
+        surface[place] = (mid[place] + got_a[place] + got_b[place]) * scale
+    copy = pltpu.make_async_copy(surface, out, sems.at[1])
+    copy.start()
+    copy.wait()
+    rest.wait()
 
 
 def shards(
@@ -917,7 +938,7 @@
     lon_a = swap(send_a, "lon", 0, True)
     (hot,) = call(
         hot_body,
-        [shape(links * blocks * rows, LANES, LANES, dtype=jnp.bfloat16)],
+        [shape(links * rows, LANES, blocks * LANES, dtype=jnp.bfloat16)],
         (points,),
         "hot",
         0.0,
@@ -944,11 +965,13 @@
         sums_a,
         sums_b,
         sums_mid,
+        draft,
     ) = call(
         functools.partial(subcycle_body, levels),
         [shape(rows, width)] * 3
         + [shape(4, rows, width), shape(4, rows, width), shape(3, 3 * TILE, LANES)]
-        + [shape(nsums, TILE, LANES)] * 3,
+        + [shape(nsums, TILE, LANES)] * 3
+        + [shape(levels, rows, width)],
         (
             ext,
             edges,
@@ -978,43 +1001,58 @@
         pass_body, [shape(nsums, TILE, LANES)], (sums_a, sums_b), "pass_sums", LATE, aliases={0: 0}
     )
     back_a = swap(sums_a, "lat", 0, False)
-    first = levels // 10 * 9
-    tracer = (temp, halo, base, laps, limits, speeds, ends)
-    (upper,) = call(
-        functools.partial(upper_body, first),
-        [shape(first, rows, width)],
-        tracer,
-        "tracer_upper",
-        2.3,
-    )
-    return call(
-        functools.partial(lower_body, first),
+    advanced_elevation, transport_x_next, transport_y_next, draft_field, draft = call(
+        tracer_body,
         [
             pltpu.HBM((rows, width), f32),
             pltpu.HBM((rows, width), f32),
             pltpu.HBM((rows, width), f32),
             pltpu.HBM((levels, rows, width), f32),
-            pltpu.HBM((nsums - 1, band_rows, lanes), f32),
+            shape(levels, rows, width),
         ],
-        tracer
-        + (
-            upper,
+        (
+            temp,
+            halo,
+            base,
+            laps,
+            limits,
+            speeds,
+            ends,
+            draft,
             advanced_elevation,
             transport_x_next,
             transport_y_next,
-            sums_mid,
-            back_a,
-            back_b,
-            flags,
         ),
-        "tracer_lower",
-        2.4,
+        "tracer",
+        2.5,
+        aliases={7: 4},
         scratch=[
-            pltpu.VMEM((levels - first, rows, width), f32),
+            pltpu.SemaphoreType.DMA((3,)),
+            pltpu.SemaphoreType.DMA((levels // level_step(levels),)),
+        ],
+    )
+    marine_skin_condition, advanced_thermal_field = call(
+        merge_body,
+        [
+            pltpu.HBM((nsums - 1, band_rows, lanes), f32),
+            pltpu.HBM((levels, rows, width), f32),
+        ],
+        (sums_mid, back_a, back_b, flags, draft, draft_field),
+        "merge",
+        0.1,
+        aliases={5: 1},
+        hbm=(5,),
+        scratch=[
             pltpu.VMEM((nsums - 1, band_rows, lanes), f32),
-            pltpu.SemaphoreType.DMA((5,)),
-            pltpu.SemaphoreType.DMA((levels - first,)),
+            pltpu.SemaphoreType.DMA((2,)),
         ],
+    )
+    return (
+        advanced_elevation,
+        transport_x_next,
+        transport_y_next,
+        advanced_thermal_field,
+        marine_skin_condition,
     )
 
 

time: 31.5 us -> 29.4 us (0.933)
  the two profiles are of different devices: /device:TPU:0 before, /device:TPU:1 now
where the time goes in v4:
time: 29.4 us; the launch traced here: 29.2 us
  starting transfers between devices  15.3 us (52%)
  Pallas kernels  11 us (37%)
  waiting for transfers between devices  2.21 us (8%)
  between operations  0.77 us (3%)
    ppermute x8, starting transfers between devices, swap(): lax.ppermute(array, axis, swap_pairs(lax.axis_size(axis), first, periodic))  15.3 us
    pallas_call x15, Pallas kernels, call(): pl.pallas_call(body, out_shape=outs, in_specs=specs, out_specs=[pl.BlockS...  11 us
    ppermute x8, waiting for transfers between devices, swap(): lax.ppermute(array, axis, swap_pairs(lax.axis_size(axis), first, periodic))  2.21 us
  transfers between devices with their start and end apart: 8, of which 3 were waited for; matrix products, arithmetic and copies ran while one was open for 0% of the time, Pallas kernels for 23%

profile of v4, /device:TPU:1, one launch (start us, length us, event | category | flops | bytes accessed | tf_op | source)
XLA Modules:
  0.0 29.2 jit_solution(674125753107434240)
XLA Ops:
  0.6 1.5 %load.1 = (f32[24,8,256]{2,1,0:T(8,128)S(1)}, f32[7,8,128]{2,1,0:T(8,128)S(1)}, f32[4,16,256]{2,1,0:T(8,128)S(1)}, s32[4,16,256]{2,1,0:T(8,128)S(1)}, f32[4,16,2...) custom-call(f32[16,256]{1,0:T(8,128)} %height.1, f32[16,256]{1,0:T(8,128)} %zonal.1, ...), custom_call_target="tpu_custom_call" | custom-call | flops 1840000000 | bytes 1024 | tf_op jit(solution)/shard_map/load/pallas_call | solution.py:80
  2.2 0.1 collective-permute-start
  2.3 0.3 pack_b.1
  2.6 1.1 %collective-permute-done.received.got_a = f32[24,8,256]{2,1,0:T(8,128)S(1)} collective-permute-done((f32[24,8,256]{2,1,0:T(8,128)S(1)}, f32[24,8,256]{2,1,0:T(8,128)S(1)}, u32[]{:S(2)}, u32[]{:S(2)}) %collective-permute-start) | collective-permute-done | bytes 196640 | tf_op jit(solution)/shard_map/ppermute | solution.py:50
  3.7 4.5 %collective-permute-start.1 = (f32[12,8,256]{2,1,0:T(8,128)S(1)}, f32[12,8,256]{2,1,0:T(8,128)S(1)}, u32[]{:S(2)}, u32[]{:S(2)}) collective-permute-start(f32[12,8,256]{2,1,0:T(8,128)S(1)} %pack_flux.1.second), channel_id=1, source_target_pairs={{1,2},{2,1},{3,4},{4,3},{5,6},{6,5},{9,10},{10,9},{11,12},{12,11},... | collective-permute-start | bytes 294920 | tf_op jit(solution)/shard_map/ppermute | solution.py:50
  8.2 1.9 %collective-permute-start.3 = (f32[15,8,256]{2,1,0:T(8,128)S(1)}, f32[15,8,256]{2,1,0:T(8,128)S(1)}, u32[]{:S(2)}, u32[]{:S(2)}) collective-permute-start(f32[15,8,256]{2,1,0:T(8,128)S(1)} %pass_temp.1), channel_id=1, source_target_pairs={{1,2},{2,1},{3,4},{4,3},{5,6},{6,5},{9,10},{10,9},{11,12},{12,11},... | collective-permute-start | bytes 368648 | tf_op jit(solution)/shard_map/ppermute | solution.py:50
  10.1 0.2 unpack_a.1
  10.3 0.3 %collective-permute-done.1.got_b.received = f32[12,8,256]{2,1,0:T(8,128)S(1)} collective-permute-done((f32[12,8,256]{2,1,0:T(8,128)S(1)}, f32[12,8,256]{2,1,0:T(8,128)S(1)}, u32[]{:S(2)}, u32[]{:S(2)}) %collective-permute-start.1) | collective-permute-done | bytes 98336 | tf_op jit(solution)/shard_map/ppermute | solution.py:50
  10.6 0.0 collective-permute-start.2
  10.7 0.4 %forcing.1 = (f32[7,24,256]{2,1,0:T(8,128)S(1)}, f32[2,16,256]{2,1,0:T(8,128)S(1)}) custom-call(f32[24,8,256]{2,1,0:T(8,128)S(1)} %collective-permute-done.received.got_a, f32[12,8,256]{2,1,0:T(8,128)S(1)} %collective-permute-done.1.got_b.received, f32[7,8,128]{2,1,0:T(8,128)S(1)} %get-tuple-element.45.own, f32[4,16,256]{2,1,0:T(8,128)S(1)} %get-tuple-element.46.state, ...), custom_call_target="tpu_custom_call" | custom-call | flops 460000000 | bytes 1024 | tf_op jit(solution)/shard_map/forcing/pallas_call | solution.py:80
  11.0 0.8 %collective-permute-done.2.got_c = f32[3,8,128]{2,1,0:T(8,128)S(1)} collective-permute-done((f32[3,8,128]{2,1,0:T(8,128)S(1)}, f32[3,8,128]{2,1,0:T(8,128)S(1)}, u32[]{:S(2)}, u32[]{:S(2)}) %collective-permute-start.2) | collective-permute-done | bytes 12320 | tf_op jit(solution)/shard_map/ppermute | solution.py:50
  11.8 0.3 forcing_halo.1
  12.1 1.9 %collective-permute-start.4 = (f32[2,24,128]{2,1,0:T(8,128)S(1)}, f32[2,24,128]{2,1,0:T(8,128)S(1)}, u32[]{:S(2)}, u32[]{:S(2)}) collective-permute-start(f32[2,24,128]{2,1,0:T(8,128)S(1)} %pass_lon.1), channel_id=1, source_target_pairs={{0,8},{8,0},{16,24},{24,16},{1,9},{9,1},{17,25},{25,17},{2,10},{10... | collective-permute-start | bytes 73736 | tf_op jit(solution)/shard_map/ppermute | solution.py:50
  14.0 2.2 %collective-permute-start.5 = (f32[2,24,128]{2,1,0:T(8,128)S(1)}, f32[2,24,128]{2,1,0:T(8,128)S(1)}, u32[]{:S(2)}, u32[]{:S(2)}) collective-permute-start(f32[2,24,128]{2,1,0:T(8,128)S(1)} %get-tuple-element.62.second), channel_id=1, source_target_pairs={{8,16},{16,8},{24,0},{0,24},{9,17},{17,9},{25,1},{1,25},{10,18},{1... | collective-permute-start | bytes 73736 | tf_op jit(solution)/shard_map/ppermute | solution.py:50
  16.2 1.1 %hot.1 = bf16[64,128,256]{2,1,0:T(8,128)(2,1)S(1)} custom-call(s32[4,16,256]{2,1,0:T(8,128)S(1)} %get-tuple-element.47.points), custom_call_target="tpu_custom_call" | custom-call | bytes 1024 | tf_op jit(solution)/shard_map/hot/pallas_call | solution.py:80
  17.4 0.0 collective-permute-done.3.got_b
  17.4 1.9 %before.1 = (f32[60,16,256]{2,1,0:T(8,128)S(1)}, f32[60,24,256]{2,1,0:T(8,128)S(1)}, f32[60,8,256]{2,1,0:T(8,128)S(1)}) custom-call(f32[7,24,256]{2,1,0:T(8,128)S(1)} %get-tuple-element.53.ext, f32[2,16,256]{2,1,0:T(8,128)S(1)} %get-tuple-element.54.light, f32[60,16,256]{2,1,0:T(8,128)S(1)} %get-tuple-element.43.temp, ...), custom_call_target="tpu_custom_call", output_to_operand_aliasing={{2}: (3, {})} | custom-call | bytes 1024 | tf_op jit(solution)/shard_map/before/pallas_call | solution.py:80
  19.3 0.0 collective-permute-done.4.got_a
  19.3 0.0 collective-permute-done.5.got_b
  19.3 2.2 %subcycles.1 = (f32[16,256]{1,0:T(8,128)S(1)}, f32[16,256]{1,0:T(8,128)S(1)}, f32[16,256]{1,0:T(8,128)S(1)}, f32[4,16,256]{2,1,0:T(8,128)S(1)}, f32[4,16,256]{2,...) custom-call(f32[7,24,256]{2,1,0:T(8,128)S(1)} %get-tuple-element.53., ...), custom_call_target="tpu_custom_call" | custom-call | flops 2990000128 | bytes 1024 | tf_op jit(solution)/shard_map/subcycles/pallas_call | solution.py:80
  21.4 4.5 %collective-permute-start.7 = (f32[5,8,128]{2,1,0:T(8,128)S(1)}, f32[5,8,128]{2,1,0:T(8,128)S(1)}, u32[]{:S(2)}, u32[]{:S(2)}) collective-permute-start(f32[5,8,128]{2,1,0:T(8,128)S(1)} %get-tuple-element.75.second), channel_id=1, source_target_pairs={{1,2},{2,1},{3,4},{4,3},{5,6},{6,5},{9,10},{10,9},{11,12},{12,11},... | collective-permute-start | bytes 61448 | tf_op jit(solution)/shard_map/ppermute | solution.py:50
  26.0 0.1 collective-permute-start.6
  26.1 2.4 %tracer.1 = (f32[16,256]{1,0:T(8,128)}, f32[16,256]{1,0:T(8,128)}, f32[16,256]{1,0:T(8,128)}, f32[60,16,256]{2,1,0:T(8,128)}, f32[60,16,256]{2,1,0:T(8,128)S(1)}) custom-call(f32[60,16,256]{2,1,0:T(8,128)S(1)} %get-tuple-element.43.temp, f32[60,8,256]{2,1,0:T(8,128)S(1)} %get-tuple-element.57.halo, ...), custom_call_target="tpu_custom_call", output_to_operand_aliasing={{4}: (7, {})} | custom-call | flops 2875000064 | bytes 1024 | tf_op jit(solution)/shard_map/tracer/pallas_call | solution.py:80
  28.5 0.0 collective-permute-done.6.got_a
  28.5 0.0 collective-permute-done.7.got_b
  28.5 0.7 %merge.1 = (f32[4,8,128]{2,1,0:T(8,128)}, f32[60,16,256]{2,1,0:T(8,128)}) custom-call(f32[5,8,128]{2,1,0:T(8,128)S(1)} %get-tuple-element.73.mid, f32[5,8,128]{2,1,0:T(8,128)S(1)} %collective-permute-done.6.got_a, f32[5,8,128]{2,1,0:T(8,128)S(1)} %collective-permute-done.7.got_b, ...), custom_call_target="tpu_custom_call", output_to_operand_aliasing={{1}: (5, {})} | custom-call | flops 115000000 | bytes 1024 | tf_op jit(solution)/shard_map/merge/pallas_call | solution.py:80
  (5 shorter events, 0.0 us)
Async XLA Ops:
  2.2 1.5 %collective-permute-start = (f32[24,8,256]{2,1,0:T(8,128)S(1)}, f32[24,8,256]{2,1,0:T(8,128)S(1)}, u32[]{:S(2)}, u32[]{:S(2)}) collective-permute-start(f32[24,8,256]{2,1,0:T(8,128)S(1)} %get-tuple-element.44), channel_id=1, source_target_pairs={{0,1},{1,0},{2,3},{3,2},{4,5},{5,4},{6,7},{7,6},{8,9},{9,8},{10,11... | collective-permute-start | bytes 589832 | tf_op jit(solution)/shard_map/ppermute | solution.py:50
  3.7 7.0 %collective-permute-start.1 = (f32[12,8,256]{2,1,0:T(8,128)S(1)}, f32[12,8,256]{2,1,0:T(8,128)S(1)}, u32[]{:S(2)}, u32[]{:S(2)}) collective-permute-start(f32[12,8,256]{2,1,0:T(8,128)S(1)} %pack_flux.1.second), channel_id=1, source_target_pairs={{1,2},{2,1},{3,4},{4,3},{5,6},{6,5},{9,10},{10,9},{11,12},{12,11},... | collective-permute-start | bytes 294920 | tf_op jit(solution)/shard_map/ppermute | solution.py:50
  8.2 9.2 %collective-permute-start.3 = (f32[15,8,256]{2,1,0:T(8,128)S(1)}, f32[15,8,256]{2,1,0:T(8,128)S(1)}, u32[]{:S(2)}, u32[]{:S(2)}) collective-permute-start(f32[15,8,256]{2,1,0:T(8,128)S(1)} %pass_temp.1), channel_id=1, source_target_pairs={{1,2},{2,1},{3,4},{4,3},{5,6},{6,5},{9,10},{10,9},{11,12},{12,11},... | collective-permute-start | bytes 368648 | tf_op jit(solution)/shard_map/ppermute | solution.py:50
  10.6 1.2 %collective-permute-start.2 = (f32[3,8,128]{2,1,0:T(8,128)S(1)}, f32[3,8,128]{2,1,0:T(8,128)S(1)}, u32[]{:S(2)}, u32[]{:S(2)}) collective-permute-start(f32[3,8,128]{2,1,0:T(8,128)S(1)} %pack_c.1), channel_id=1, source_target_pairs={{0,1},{1,0},{2,3},{3,2},{4,5},{5,4},{6,7},{7,6},{8,9},{9,8},{10,11... | collective-permute-start | bytes 36872 | tf_op jit(solution)/shard_map/ppermute | solution.py:50
  12.1 7.1 %collective-permute-start.4 = (f32[2,24,128]{2,1,0:T(8,128)S(1)}, f32[2,24,128]{2,1,0:T(8,128)S(1)}, u32[]{:S(2)}, u32[]{:S(2)}) collective-permute-start(f32[2,24,128]{2,1,0:T(8,128)S(1)} %pass_lon.1), channel_id=1, source_target_pairs={{0,8},{8,0},{16,24},{24,16},{1,9},{9,1},{17,25},{25,17},{2,10},{10... | collective-permute-start | bytes 73736 | tf_op jit(solution)/shard_map/ppermute | solution.py:50
  14.0 5.2 %collective-permute-start.5 = (f32[2,24,128]{2,1,0:T(8,128)S(1)}, f32[2,24,128]{2,1,0:T(8,128)S(1)}, u32[]{:S(2)}, u32[]{:S(2)}) collective-permute-start(f32[2,24,128]{2,1,0:T(8,128)S(1)} %get-tuple-element.62.second), channel_id=1, source_target_pairs={{8,16},{16,8},{24,0},{0,24},{9,17},{17,9},{25,1},{1,25},{10,18},{1... | collective-permute-start | bytes 73736 | tf_op jit(solution)/shard_map/ppermute | solution.py:50
  21.4 7.1 %collective-permute-start.7 = (f32[5,8,128]{2,1,0:T(8,128)S(1)}, f32[5,8,128]{2,1,0:T(8,128)S(1)}, u32[]{:S(2)}, u32[]{:S(2)}) collective-permute-start(f32[5,8,128]{2,1,0:T(8,128)S(1)} %get-tuple-element.75.second), channel_id=1, source_target_pairs={{1,2},{2,1},{3,4},{4,3},{5,6},{6,5},{9,10},{10,9},{11,12},{12,11},... | collective-permute-start | bytes 61448 | tf_op jit(solution)/shard_map/ppermute | solution.py:50
  26.0 2.5 %collective-permute-start.6 = (f32[5,8,128]{2,1,0:T(8,128)S(1)}, f32[5,8,128]{2,1,0:T(8,128)S(1)}, u32[]{:S(2)}, u32[]{:S(2)}) collective-permute-start(f32[5,8,128]{2,1,0:T(8,128)S(1)} %pass_sums.1), channel_id=1, source_target_pairs={{0,1},{1,0},{2,3},{3,2},{4,5},{5,4},{6,7},{7,6},{8,9},{9,8},{10,11... | collective-permute-start | bytes 61448 | tf_op jit(solution)/shard_map/ppermute | solution.py:50

commit v5 on v4

--- a/solution.py
+++ b/solution.py
@@ -84,7 +84,7 @@
         out_specs=[pl.BlockSpec(memory_space=leaf.memory_space) for leaf in outs],
         scratch_shapes=list(scratch),
         input_output_aliases=aliases or {},
-        compiler_params=pltpu.CompilerParams(vmem_limit_bytes=24 * 1024 * 1024),
+        compiler_params=pltpu.CompilerParams(vmem_limit_bytes=12 * 1024 * 1024),
         cost_estimate=pl.CostEstimate(
             flops=int(took * FLOPS_PER_US), bytes_accessed=1024, transcendentals=0
         ),
@@ -151,14 +151,12 @@
     weights,
     flux,
     flags,
-    temp,
     edge,
     own,
     state_out,
     points_out,
     weights_out,
     flags_out,
-    temp_out,
     counts_in,
     tile_in,
     flux_in,
@@ -174,7 +172,6 @@
         (merid, state_out.at[2]),
         (points, points_out),
         (weights, weights_out),
-        (temp, temp_out),
     ]
     copies = [
         pltpu.make_async_copy(source, target, sems.at[place])
@@ -182,7 +179,7 @@
     ]
     for copy in copies:
         copy.start()
-    for copy in copies[:-1]:
+    for copy in copies:
         copy.wait()
     state_out[3] = counts_in[...].astype(f32)
     links, blocks, rows = tile.shape
@@ -203,32 +200,34 @@
     top = goes_north(0)
     fields = edge_fields(state_out, points_out, weights_out)
     write_edge(top, fields, edge)
-    planes = flux_planes(top, own)
-    at = len(fields) // 2
-    write_planes(planes, edge, at)
-    copies[-1].wait()
-    write_temp_edge(top, temp_out, edge, at + (len(planes) + 1) // 2)
-
-
-def pack_second_body(own, state, points, weights, temp, draft, temp_edge, edges):
+    write_planes(flux_planes(top, own), edge, len(fields) // 2)
+
+
+def pack_second_body(own, state, points, weights, temp, draft, edges):
     top = goes_north(1)
     fields = edge_fields(state, points, weights)
     write_edge(top, fields, draft)
-    planes = flux_planes(top, own)
-    at = len(fields) // 2
-    write_planes(planes, draft, at)
+    write_planes(flux_planes(top, own), draft, len(fields) // 2)
     levels, rows, _ = temp.shape
-    columns = edge_columns([temp[level] for level in range(levels)], rows)
-    for place in range(2):
-        edges[place] = columns[place]
-    both = jnp.concatenate(columns, axis=1)
-    draft[at + (len(planes) + 1) // 2] = jnp.where(top, both[TILE:], both[:TILE])
-    write_temp_edge(top, temp, temp_edge, 0)
-
-
-def pack_flux_body(flux_at, draft, received, out):
-    far = [spot_of(received, flux_at, 1 + plane) for plane in HALO_FLUXES]
-    write_planes(far, out, out.shape[0] - (len(far) + 1) // 2)
+    for place, columns in enumerate(edge_columns([temp[level] for level in range(levels)], rows)):
+        edges[place] = columns
+
+
+def corner_plane(top, edges):
+    west = jnp.where(top, edges[0, TILE:, :], edges[0, :TILE, :])
+    east = jnp.where(top, edges[1, TILE:, :], edges[1, :TILE, :])
+    return jnp.where((row_ids(TILE) >= HALF) == top, west, roll_rows(east, HALF))
+
+
+def far_planes(flux_at, received):
+    return [spot_of(received, flux_at, 1 + plane) for plane in HALO_FLUXES]
+
+
+def pack_flux_body(flux_at, draft, received, edges, out):
+    planes = far_planes(flux_at, received) + [corner_plane(goes_north(1), edges)]
+    at = out.shape[0] - len(planes) // 2
+    out[:at] = draft[:at]
+    write_planes(planes, out, at)
 
 
 def edge_columns(fields, rows):
@@ -247,12 +246,15 @@
 
 
 def pass_body(first, second, out):
-    out[0] = first[0]
-
-
-def pack_third_body(flux_at, received, out):
-    for place, plane in enumerate(HALO_FLUXES):
-        out[place] = spot_of(received, flux_at, 1 + plane)
+    out[...] = first[...]
+
+
+def pack_temp_body(first, temp, other, out):
+    write_temp_edge(goes_north(first), temp, out, 0)
+
+
+def pack_third_body(flux_at, received, edges, out):
+    write_planes(far_planes(flux_at, received) + [corner_plane(goes_north(0), edges)], out, 0)
 
 
 def unpack_rows(top, packed, level):
@@ -262,18 +264,6 @@
 
 def near_lanes(width):
     return (row_ids(TILE, width) < HALF) == (lax.rem(lax.axis_index("lat"), 2) == 0)
-
-
-def unpack_near_body(temp_at, got_a, halo, edges):
-    levels = halo.shape[0]
-    even = lax.rem(lax.axis_index("lat"), 2) == 0
-    fields = []
-    for level in range(levels):
-        rows = unpack_rows(even, got_a[temp_at + level // 4], level)
-        halo[level] = rows
-        fields.append(rows)
-    for place, columns in enumerate(edge_columns(fields, TILE)):
-        edges[place] = columns
 
 
 def pick(array, rows):
@@ -336,6 +326,15 @@
                     light[plane - 2, here, cols] = totals[plane]
 
 
+def both_fields(even, near, far):
+    north, south = by_side(even, near, far)
+    sub = row_ids(*near.shape)
+    return [
+        jnp.where(sub < HALF, north, south),
+        roll_rows(jnp.where(sub < HALF, south, north), HALF),
+    ]
+
+
 def forcing_halo_body(
     flux_at,
     draft,
@@ -344,7 +343,6 @@
     got_c,
     own,
     edges,
-    edges_near,
     ext,
     send_a,
     send_b,
@@ -354,12 +352,10 @@
     rows, width = 2 * TILE, ext.shape[2]
     blocks = width // LANES
     links = flux_at - 2
-    sub = row_ids(TILE, width)
     halos = []
     for place in range(flux_at):
-        north, south = by_side(even, got_a[place], got_b[place])
-        halos.append(jnp.where(sub < HALF, north, south))
-        halos.append(roll_rows(jnp.where(sub < HALF, south, north), HALF))
+        halos += both_fields(even, got_a[place], got_b[place])
+    ext[:, :rows, :] = draft[:, :rows, :]
     for place in range(4):
         ext[place, rows:, :] = halos[place]
     tables = {}
@@ -367,7 +363,9 @@
     for place, plane in enumerate(HALO_FLUXES):
         one, two = spot_of(got_a, flux_at, 1 + plane), spot_of(got_b, flux_at, 1 + plane)
         north, south = by_side(even, one, two)
-        far_north, far_south = by_side(even, got_c[place], spot_of(got_b, far_at, place))
+        far_north, far_south = by_side(
+            even, spot_of(got_c, 0, place), spot_of(got_b, far_at, place)
+        )
         tables[plane] = [far_south, south, own[plane], north, far_north]
     sub_one = row_ids(TILE)
     north, south = by_side(even, spot_of(got_a, flux_at, 0), spot_of(got_b, flux_at, 0))
@@ -397,9 +395,10 @@
         to_west = jnp.where((lane >= 3 * place) & (lane < 3 * place + 3), low, to_west)
         edge = LANES - 3 * place
         to_east = jnp.where((lane >= edge - 3) & (lane < edge), high, to_east)
-    near = near_lanes(LANES)
+    corner = len(HALO_FLUXES)
+    corners = both_fields(even, spot_of(got_c, 0, corner), spot_of(got_b, far_at, corner))
     for place in range(2):
-        edges_halo[place] = jnp.where(near, edges_near[place], spot_of(got_b, far_at - 1, place))
+        edges_halo[place] = corners[place]
     lon_even = lax.rem(lax.axis_index("lon"), 2) == 0
     send_a[0] = jnp.where(lon_even, to_east, to_west)
     send_b[0] = jnp.where(lon_even, to_west, to_east)
@@ -431,7 +430,7 @@
 LEVELS_AT_ONCE = 6
 
 
-def before_body(ext, light, temp, halo_near, got_b, base, laps, halo):
+def before_body(ext, light, temp, got_a, got_b, base, laps, halo):
     levels, rows, width = temp.shape
     counts = ext[3]
     own_counts = counts[:rows]
@@ -443,8 +442,9 @@
     odd = lax.rem(lax.axis_index("lat"), 2) == 1
     near = near_lanes(width)
     for level in range(levels):
+        rows_near = unpack_rows(jnp.logical_not(odd), got_a[level // 4], level)
         rows_far = unpack_rows(odd, got_b[level // 4], level)
-        halo[level] = jnp.where(near, halo_near[level], rows_far)
+        halo[level] = jnp.where(near, rows_near, rows_far)
 
     def group(at, down_before):
         for inner in range(step):
@@ -773,14 +773,14 @@
     for copy in copies:
         copy.start()
 
-    def level_copy(at):
+    def level_copy(at, source=whole):
         part = pl.ds(at * step, step)
-        return pltpu.make_async_copy(whole.at[part], out.at[part], level_sems.at[at])
+        return pltpu.make_async_copy(source.at[part], out.at[part], level_sems.at[at])
 
     early = early_groups(levels)
 
     def start(at, carry):
-        level_copy(at).start()
+        level_copy(at, draft).start()
         return carry
 
     lax.fori_loop(0, early, start, 0)
@@ -837,16 +837,16 @@
     temp_at = flux_at + flux_tiles
     groups = pl.cdiv(levels, 4)
     tile_lines = jnp.swapaxes(donor_tile_number, 1, 2)
-    edge_a, own, state, points, weights, flags, temp = call(
+    temp = thermal_field
+    edge_a, own, state, points, weights, flags = call(
         load_body,
         [
-            shape(temp_at + groups, TILE, width),
+            shape(temp_at, TILE, width),
             shape(nflux + 2, TILE, LANES),
             shape(4, rows, width),
             shape(links, rows, width, dtype=i32),
             shape(links, rows, width),
             shape(band_rows, lanes, dtype=i32),
-            shape(levels, rows, width),
         ],
         (
             free_elevation,
@@ -858,7 +858,6 @@
             pairing_coefficients,
             aerial_exchanges,
             aerial_terrain_flags,
-            thermal_field,
         ),
         "load",
         1.6,
@@ -866,17 +865,17 @@
             pltpu.VMEM((rows, width), i32),
             pltpu.VMEM((links, blocks, rows), i32),
             pltpu.VMEM((nflux, band_rows, lanes), f32),
-            pltpu.SemaphoreType.DMA((10,)),
+            pltpu.SemaphoreType.DMA((9,)),
         ],
-        hbm=range(10),
+        hbm=range(9),
     )
     got_a = swap(edge_a, "lat", 0, False)
-    edge_tiles = temp_at + 1 + (len(HALO_FLUXES) + 1) // 2
-    draft_b, temp_b, edges = call(
+    far_tiles = (len(HALO_FLUXES) + 1) // 2
+    edge_tiles = temp_at + far_tiles
+    draft_b, edges = call(
         pack_second_body,
         [
             shape(edge_tiles, TILE, width),
-            shape(groups, TILE, width),
             shape(2, rows, LANES),
         ],
         (own, state, points, weights, temp),
@@ -886,20 +885,31 @@
     (edge_b,) = call(
         functools.partial(pack_flux_body, flux_at),
         [shape(edge_tiles, TILE, width)],
-        (draft_b, got_a),
+        (draft_b, got_a, edges),
         "pack_flux",
         0.0,
-        aliases={0: 0},
     )
     got_b = swap(edge_b, "lat", 1, False)
     (temp_b,) = call(
-        pass_body, [shape(groups, TILE, width)], (temp_b, edge_b), "pass_temp", LATE, aliases={0: 0}
+        functools.partial(pack_temp_body, 1),
+        [shape(groups, TILE, width)],
+        (temp, edge_b),
+        "pack_temp_b",
+        LATE,
     )
     got_temp_b = swap(temp_b, "lat", 1, False)
+    (temp_a,) = call(
+        functools.partial(pack_temp_body, 0),
+        [shape(groups, TILE, width)],
+        (temp, temp_b),
+        "pack_temp_a",
+        0.0,
+    )
+    got_temp_a = swap(temp_a, "lat", 0, False)
     (edge_c,) = call(
         functools.partial(pack_third_body, flux_at),
-        [shape(len(HALO_FLUXES), TILE, LANES)],
-        (got_b,),
+        [shape(far_tiles, TILE, width)],
+        (got_b, edges),
         "pack_c",
         LATE,
     )
@@ -910,13 +920,6 @@
         (got_a, got_b, own, state, points, weights),
         "forcing",
         0.4,
-    )
-    halo_near, edges_near = call(
-        functools.partial(unpack_near_body, temp_at),
-        [shape(levels, TILE, width), shape(2, TILE, LANES)],
-        (got_a,),
-        "unpack_a",
-        0.0,
     )
     ext, send_a, send_b, edges_halo = call(
         functools.partial(forcing_halo_body, flux_at),
@@ -926,14 +929,13 @@
             shape(2, 3 * TILE, LANES),
             shape(2, TILE, LANES),
         ],
-        (draft_ext, got_a, got_b, got_c, own, edges, edges_near),
+        (draft_ext, got_a, got_b, got_c, own, edges),
         "forcing_halo",
         0.3,
-        aliases={0: 0},
     )
     lon_b = swap(send_b, "lon", 1, True)
     (send_a,) = call(
-        pass_body, [shape(2, 3 * TILE, LANES)], (send_a, send_b), "pass_lon", LATE, aliases={0: 0}
+        pass_body, [shape(2, 3 * TILE, LANES)], (send_a, send_b), "pass_lon", LATE
     )
     lon_a = swap(send_a, "lon", 0, True)
     (hot,) = call(
@@ -950,10 +952,9 @@
             shape(levels, 3 * TILE, width),
             shape(levels, TILE, width),
         ],
-        (ext, light, temp, halo_near, got_temp_b),
+        (ext, light, temp, got_temp_a, got_temp_b),
         "before",
         0.0,
-        aliases={3: 2},
     )
     (
         advanced_elevation,
@@ -998,7 +999,7 @@
     )
     back_b = swap(sums_b, "lat", 1, False)
     (sums_a,) = call(
-        pass_body, [shape(nsums, TILE, LANES)], (sums_a, sums_b), "pass_sums", LATE, aliases={0: 0}
+        pass_body, [shape(nsums, TILE, LANES)], (sums_a, sums_b), "pass_sums", LATE
     )
     back_a = swap(sums_a, "lat", 0, False)
     advanced_elevation, transport_x_next, transport_y_next, draft_field, draft = call(
@@ -1025,7 +1026,6 @@
         ),
         "tracer",
         2.5,
-        aliases={7: 4},
         scratch=[
             pltpu.SemaphoreType.DMA((3,)),
             pltpu.SemaphoreType.DMA((levels // level_step(levels),)),

time: 29.4 us -> 28.8 us (0.980)
  waiting for transfers between devices: 2.21 us -> 1.52 us
  Pallas kernels: 11 us -> 10.6 us
  starting transfers between devices: 15.3 us -> 15.7 us
    ppermute x8 -> x9, waiting for transfers between devices: 2.21 us -> 1.52 us  [swap(): lax.ppermute(array, axis, swap_pairs(lax.axis_size(axis), first, periodic))]
    ppermute x8 -> x9, starting transfers between devices: 15.3 us -> 15.7 us  [swap(): lax.ppermute(array, axis, swap_pairs(lax.axis_size(axis), first, periodic))]
    pallas_call x15, Pallas kernels: 11 us -> 10.6 us  [call(): pl.pallas_call(body, out_shape=outs, in_specs=specs, out_specs=[pl.BlockS...]
  transfers between devices with their start and end apart: 8 -> 9, of which waited for: 3 -> 3; matrix products, arithmetic and copies ran while one was open for 0% -> 0% of each run, Pallas kernels for 23% -> 23%
where the time goes in v5:
time: 28.8 us; the launch traced here: 28.6 us
  starting transfers between devices  15.7 us (55%)
  Pallas kernels  10.6 us (37%)
  waiting for transfers between devices  1.52 us (5%)
  between operations  0.81 us (3%)
    ppermute x9, starting transfers between devices, swap(): lax.ppermute(array, axis, swap_pairs(lax.axis_size(axis), first, periodic))  15.7 us
    pallas_call x15, Pallas kernels, call(): pl.pallas_call(body, out_shape=outs, in_specs=specs, out_specs=[pl.BlockS...  10.6 us
    ppermute x9, waiting for transfers between devices, swap(): lax.ppermute(array, axis, swap_pairs(lax.axis_size(axis), first, periodic))  1.52 us
  transfers between devices with their start and end apart: 9, of which 3 were waited for; matrix products, arithmetic and copies ran while one was open for 0% of the time, Pallas kernels for 23%

profile of v5, /device:TPU:1, one launch (start us, length us, event | category | flops | bytes accessed | tf_op | source)
XLA Modules:
  0.0 28.6 jit_solution(4897821411109076883)
XLA Ops:
  0.6 0.0 copy-start
  0.6 1.3 %load.1 = (f32[9,8,256]{2,1,0:T(8,128)S(1)}, f32[7,8,128]{2,1,0:T(8,128)S(1)}, f32[4,16,256]{2,1,0:T(8,128)S(1)}, s32[4,16,256]{2,1,0:T(8,128)S(1)}, f32[4,16,256]{2,1,0:T(8,128)S(1)}, /*index=5*/s32[8,128]{1,0:T(8,128)S(1)}) custom-call(f32[16,256]{1,0:T(8,128)} %height.1, f32[16,256]{1,0:T(8,128)} %zonal.1, f32[16,256]{1,0:T(8,128)} %merid.1, ...), custom_call_target="tpu_custom_call" | custom-call | flops 1840000000 | bytes 1024 | tf_op jit(solution)/shard_map/load/pallas_call | solution.py:80
  1.9 0.1 collective-permute-start
  2.0 0.0 copy-done
  2.0 0.3 pack_b.1
  2.3 0.9 %collective-permute-done.received.got_a = f32[9,8,256]{2,1,0:T(8,128)S(1)} collective-permute-done((f32[9,8,256]{2,1,0:T(8,128)S(1)}, f32[9,8,256]{2,1,0:T(8,128)S(1)}, u32[]{:S(2)}, u32[]{:S(2)}) %collective-permute-start) | collective-permute-done | bytes 73760 | tf_op jit(solution)/shard_map/ppermute | solution.py:50
  3.3 4.5 %collective-permute-start.1 = (f32[11,8,256]{2,1,0:T(8,128)S(1)}, f32[11,8,256]{2,1,0:T(8,128)S(1)}, u32[]{:S(2)}, u32[]{:S(2)}) collective-permute-start(f32[11,8,256]{2,1,0:T(8,128)S(1)} %pack_flux.1.other), channel_id=1, source_target_pairs={{1,2},{2,1},{3,4},{4,3},{5,6},{6,5},{9,10},{10,9},{11,12},{12,11},... | collective-permute-start | bytes 270344 | tf_op jit(solution)/shard_map/ppermute | solution.py:50
  7.8 0.1 pack_temp_b.1.other
  7.9 0.1 pack_temp_a.1
  7.9 1.9 %collective-permute-start.4 = (f32[15,8,256]{2,1,0:T(8,128)S(1)}, f32[15,8,256]{2,1,0:T(8,128)S(1)}, u32[]{:S(2)}, u32[]{:S(2)}) collective-permute-start(f32[15,8,256]{2,1,0:T(8,128)S(1)} %pack_temp_b.1.other), channel_id=1, source_target_pairs={{1,2},{2,1},{3,4},{4,3},{5,6},{6,5},{9,10},{10,9},{11,12},{12,11},... | collective-permute-start | bytes 368648 | tf_op jit(solution)/shard_map/ppermute | solution.py:50
  9.9 0.1 collective-permute-start.3
  9.9 0.1 collective-permute-done.1.got_b.received
  10.1 0.5 %collective-permute-start.2 = (f32[2,8,256]{2,1,0:T(8,128)S(1)}, f32[2,8,256]{2,1,0:T(8,128)S(1)}, u32[]{:S(2)}, u32[]{:S(2)}) collective-permute-start(f32[2,8,256]{2,1,0:T(8,128)S(1)} %pack_c.1), channel_id=1, source_target_pairs={{0,1},{1,0},{2,3},{3,2},{4,5},{5,4},{6,7},{7,6},{8,9},{9,8},{10,11... | collective-permute-start | bytes 49160 | tf_op jit(solution)/shard_map/ppermute | solution.py:50
  10.5 0.4 %forcing.1 = (f32[7,24,256]{2,1,0:T(8,128)S(1)}, f32[2,16,256]{2,1,0:T(8,128)S(1)}) custom-call(f32[9,8,256]{2,1,0:T(8,128)S(1)} %collective-permute-done.received.got_a, f32[11,8,256]{2,1,0:T(8,128)S(1)} %collective-permute-done.1.got_b.received, f32[7,8,128]{2,1,0:T(8,128)S(1)} %get-tuple-element.40.own, f32[4,16,256]{2,1,0:T(8,128)S(1)} %get-tuple-element.41.state, ...), custom_call_target="tpu_custom_call" | custom-call | flops 460000000 | bytes 1024 | tf_op jit(solution)/shard_map/forcing/pallas_call | solution.py:80
  10.9 0.5 %collective-permute-done.2.got_c = f32[2,8,256]{2,1,0:T(8,128)S(1)} collective-permute-done((f32[2,8,256]{2,1,0:T(8,128)S(1)}, f32[2,8,256]{2,1,0:T(8,128)S(1)}, u32[]{:S(2)}, u32[]{:S(2)}) %collective-permute-start.2) | collective-permute-done | bytes 16416 | tf_op jit(solution)/shard_map/ppermute | solution.py:50
  11.4 0.3 forcing_halo.1
  11.6 1.9 %collective-permute-start.5 = (f32[2,24,128]{2,1,0:T(8,128)S(1)}, f32[2,24,128]{2,1,0:T(8,128)S(1)}, u32[]{:S(2)}, u32[]{:S(2)}) collective-permute-start(f32[2,24,128]{2,1,0:T(8,128)S(1)} %pass_lon.1), channel_id=1, source_target_pairs={{0,8},{8,0},{16,24},{24,16},{1,9},{9,1},{17,25},{25,17},{2,10},{10... | collective-permute-start | bytes 73736 | tf_op jit(solution)/shard_map/ppermute | solution.py:50
  13.5 2.2 %collective-permute-start.6 = (f32[2,24,128]{2,1,0:T(8,128)S(1)}, f32[2,24,128]{2,1,0:T(8,128)S(1)}, u32[]{:S(2)}, u32[]{:S(2)}) collective-permute-start(f32[2,24,128]{2,1,0:T(8,128)S(1)} %get-tuple-element.54.second), channel_id=1, source_target_pairs={{8,16},{16,8},{24,0},{0,24},{9,17},{17,9},{25,1},{1,25},{10,18},{1... | collective-permute-start | bytes 73736 | tf_op jit(solution)/shard_map/ppermute | solution.py:50
  15.7 1.1 %hot.1 = bf16[64,128,256]{2,1,0:T(8,128)(2,1)S(1)} custom-call(s32[4,16,256]{2,1,0:T(8,128)S(1)} %get-tuple-element.42.points), custom_call_target="tpu_custom_call" | custom-call | bytes 1024 | tf_op jit(solution)/shard_map/hot/pallas_call | solution.py:80
  16.8 0.0 collective-permute-done.3.got_a
  16.8 0.0 collective-permute-done.4.got_b
  16.8 1.8 %before.1 = (f32[60,16,256]{2,1,0:T(8,128)S(1)}, f32[60,24,256]{2,1,0:T(8,128)S(1)}, f32[60,8,256]{2,1,0:T(8,128)S(1)}) custom-call(f32[7,24,256]{2,1,0:T(8,128)S(1)} %get-tuple-element.47.ext, f32[2,16,256]{2,1,0:T(8,128)S(1)} %get-tuple-element.48.light, f32[60,16,256]{2,1,0:T(8,128)S(1)} %copy-done, f32[15,8,256]{2,1,0:T(8,128)S(1)} %collective-permute-done.3.got_a, ...), custom_call_target="tpu_custom_call" | custom-call | bytes 1024 | tf_op jit(solution)/shard_map/before/pallas_call | solution.py:80
  18.7 0.0 collective-permute-done.5.got_a
  18.7 0.0 collective-permute-done.6.got_b
  18.7 2.2 %subcycles.1 = (f32[16,256]{1,0:T(8,128)S(1)}, f32[16,256]{1,0:T(8,128)S(1)}, f32[16,256]{1,0:T(8,128)S(1)}, f32[4,16,256]{2,1,0:T(8,128)S(1)}, f32[4,16,256]{2,...) custom-call(f32[7,24,256]{2,1,0:T(8,128)S(1)} %get-tuple-element.47., ...), custom_call_target="tpu_custom_call" | custom-call | flops 2990000128 | bytes 1024 | tf_op jit(solution)/shard_map/subcycles/pallas_call | solution.py:80
  20.9 4.5 %collective-permute-start.8 = (f32[5,8,128]{2,1,0:T(8,128)S(1)}, f32[5,8,128]{2,1,0:T(8,128)S(1)}, u32[]{:S(2)}, u32[]{:S(2)}) collective-permute-start(f32[5,8,128]{2,1,0:T(8,128)S(1)} %get-tuple-element.67.second), channel_id=1, source_target_pairs={{1,2},{2,1},{3,4},{4,3},{5,6},{6,5},{9,10},{10,9},{11,12},{12,11},... | collective-permute-start | bytes 61448 | tf_op jit(solution)/shard_map/ppermute | solution.py:50
  25.4 0.1 collective-permute-start.7
  25.5 2.4 %tracer.1 = (f32[16,256]{1,0:T(8,128)}, f32[16,256]{1,0:T(8,128)}, f32[16,256]{1,0:T(8,128)}, f32[60,16,256]{2,1,0:T(8,128)}, f32[60,16,256]{2,1,0:T(8,128)S(1)}) custom-call(f32[60,16,256]{2,1,0:T(8,128)S(1)} %copy-done, f32[60,8,256]{2,1,0:T(8,128)S(1)} %get-tuple-element.49.halo, f32[60,16,256]{2,1,0:T(8,128)S(1)} %get-tuple-element.50.base, ...), custom_call_target="tpu_custom_call" | custom-call | flops 2875000064 | bytes 1024 | tf_op jit(solution)/shard_map/tracer/pallas_call | solution.py:80
  27.9 0.0 collective-permute-done.7.got_a
  27.9 0.0 collective-permute-done.8.got_b
  27.9 0.7 %merge.1 = (f32[4,8,128]{2,1,0:T(8,128)}, f32[60,16,256]{2,1,0:T(8,128)}) custom-call(f32[5,8,128]{2,1,0:T(8,128)S(1)} %get-tuple-element.65.mid, f32[5,8,128]{2,1,0:T(8,128)S(1)} %collective-permute-done.7.got_a, f32[5,8,128]{2,1,0:T(8,128)S(1)} %collective-permute-done.8.got_b, ...), custom_call_target="tpu_custom_call", output_to_operand_aliasing={{1}: (5, {})} | custom-call | flops 115000000 | bytes 1024 | tf_op jit(solution)/shard_map/merge/pallas_call | solution.py:80
  (4 shorter events, 0.0 us)
Async XLA Ops:
  0.6 1.4 %copy-start = (f32[60,16,256]{2,1,0:T(8,128)S(1)}, f32[60,16,256]{2,1,0:T(8,128)}, u32[]{:S(2)}) copy-start(f32[60,16,256]{2,1,0:T(8,128)} %temp.11) | copy-start | bytes 2949124
  1.9 1.3 %collective-permute-start = (f32[9,8,256]{2,1,0:T(8,128)S(1)}, f32[9,8,256]{2,1,0:T(8,128)S(1)}, u32[]{:S(2)}, u32[]{:S(2)}) collective-permute-start(f32[9,8,256]{2,1,0:T(8,128)S(1)} %get-tuple-element.39), channel_id=1, source_target_pairs={{0,1},{1,0},{2,3},{3,2},{4,5},{5,4},{6,7},{7,6},{8,9},{9,8},{10,11... | collective-permute-start | bytes 221192 | tf_op jit(solution)/shard_map/ppermute | solution.py:50
  3.3 6.8 %collective-permute-start.1 = (f32[11,8,256]{2,1,0:T(8,128)S(1)}, f32[11,8,256]{2,1,0:T(8,128)S(1)}, u32[]{:S(2)}, u32[]{:S(2)}) collective-permute-start(f32[11,8,256]{2,1,0:T(8,128)S(1)} %pack_flux.1.other), channel_id=1, source_target_pairs={{1,2},{2,1},{3,4},{4,3},{5,6},{6,5},{9,10},{10,9},{11,12},{12,11},... | collective-permute-start | bytes 270344 | tf_op jit(solution)/shard_map/ppermute | solution.py:50
  7.9 8.9 %collective-permute-start.4 = (f32[15,8,256]{2,1,0:T(8,128)S(1)}, f32[15,8,256]{2,1,0:T(8,128)S(1)}, u32[]{:S(2)}, u32[]{:S(2)}) collective-permute-start(f32[15,8,256]{2,1,0:T(8,128)S(1)} %pack_temp_b.1.other), channel_id=1, source_target_pairs={{1,2},{2,1},{3,4},{4,3},{5,6},{6,5},{9,10},{10,9},{11,12},{12,11},... | collective-permute-start | bytes 368648 | tf_op jit(solution)/shard_map/ppermute | solution.py:50
  9.9 7.0 %collective-permute-start.3 = (f32[15,8,256]{2,1,0:T(8,128)S(1)}, f32[15,8,256]{2,1,0:T(8,128)S(1)}, u32[]{:S(2)}, u32[]{:S(2)}) collective-permute-start(f32[15,8,256]{2,1,0:T(8,128)S(1)} %pack_temp_a.1), channel_id=1, source_target_pairs={{0,1},{1,0},{2,3},{3,2},{4,5},{5,4},{6,7},{7,6},{8,9},{9,8},{10,11... | collective-permute-start | bytes 368648 | tf_op jit(solution)/shard_map/ppermute | solution.py:50
  10.1 1.3 %collective-permute-start.2 = (f32[2,8,256]{2,1,0:T(8,128)S(1)}, f32[2,8,256]{2,1,0:T(8,128)S(1)}, u32[]{:S(2)}, u32[]{:S(2)}) collective-permute-start(f32[2,8,256]{2,1,0:T(8,128)S(1)} %pack_c.1), channel_id=1, source_target_pairs={{0,1},{1,0},{2,3},{3,2},{4,5},{5,4},{6,7},{7,6},{8,9},{9,8},{10,11... | collective-permute-start | bytes 49160 | tf_op jit(solution)/shard_map/ppermute | solution.py:50
  11.6 7.0 %collective-permute-start.5 = (f32[2,24,128]{2,1,0:T(8,128)S(1)}, f32[2,24,128]{2,1,0:T(8,128)S(1)}, u32[]{:S(2)}, u32[]{:S(2)}) collective-permute-start(f32[2,24,128]{2,1,0:T(8,128)S(1)} %pass_lon.1), channel_id=1, source_target_pairs={{0,8},{8,0},{16,24},{24,16},{1,9},{9,1},{17,25},{25,17},{2,10},{10... | collective-permute-start | bytes 73736 | tf_op jit(solution)/shard_map/ppermute | solution.py:50
  13.5 5.2 %collective-permute-start.6 = (f32[2,24,128]{2,1,0:T(8,128)S(1)}, f32[2,24,128]{2,1,0:T(8,128)S(1)}, u32[]{:S(2)}, u32[]{:S(2)}) collective-permute-start(f32[2,24,128]{2,1,0:T(8,128)S(1)} %get-tuple-element.54.second), channel_id=1, source_target_pairs={{8,16},{16,8},{24,0},{0,24},{9,17},{17,9},{25,1},{1,25},{10,18},{1... | collective-permute-start | bytes 73736 | tf_op jit(solution)/shard_map/ppermute | solution.py:50
  20.9 7.1 %collective-permute-start.8 = (f32[5,8,128]{2,1,0:T(8,128)S(1)}, f32[5,8,128]{2,1,0:T(8,128)S(1)}, u32[]{:S(2)}, u32[]{:S(2)}) collective-permute-start(f32[5,8,128]{2,1,0:T(8,128)S(1)} %get-tuple-element.67.second), channel_id=1, source_target_pairs={{1,2},{2,1},{3,4},{4,3},{5,6},{6,5},{9,10},{10,9},{11,12},{12,11},... | collective-permute-start | bytes 61448 | tf_op jit(solution)/shard_map/ppermute | solution.py:50
  25.4 2.5 %collective-permute-start.7 = (f32[5,8,128]{2,1,0:T(8,128)S(1)}, f32[5,8,128]{2,1,0:T(8,128)S(1)}, u32[]{:S(2)}, u32[]{:S(2)}) collective-permute-start(f32[5,8,128]{2,1,0:T(8,128)S(1)} %pass_sums.1), channel_id=1, source_target_pairs={{0,1},{1,0},{2,3},{3,2},{4,5},{5,4},{6,7},{7,6},{8,9},{9,8},{10,11... | collective-permute-start | bytes 61448 | tf_op jit(solution)/shard_map/ppermute | solution.py:50

commit v6 on v5

--- a/solution.py
+++ b/solution.py
@@ -111,9 +111,8 @@
         out_ref[at + place] = jnp.concatenate(planes[2 * place : 2 * place + 2], axis=1)
 
 
-def flux_planes(top, own):
-    nflux = own.shape[0] - 2
-    return [jnp.where(top, own[nflux + 1], own[nflux])] + [own[plane] for plane in range(nflux)]
+def edge_numbers(top, numbers):
+    return jnp.where(top, numbers[1], numbers[0])
 
 
 def write_temp_edge(top, temp_ref, out_ref, at):
@@ -157,15 +156,15 @@
     points_out,
     weights_out,
     flags_out,
+    tile_out,
     counts_in,
-    tile_in,
     flux_in,
     sems,
 ):
     pairs = [
         (flux, flux_in),
         (flags, flags_out),
-        (tile, tile_in),
+        (tile, tile_out),
         (counts, counts_in),
         (height, state_out.at[0]),
         (zonal, state_out.at[1]),
@@ -182,32 +181,33 @@
     for copy in copies:
         copy.wait()
     state_out[3] = counts_in[...].astype(f32)
-    links, blocks, rows = tile.shape
     open_sea = (1 - flags_out[...]).astype(f32)
     masked = [flux_in[plane] * open_sea for plane in range(flux.shape[0])]
+    for plane, values in enumerate(masked):
+        own[plane] = values
+    top = goes_north(0)
+    fields = edge_fields(state_out, points_out, weights_out)
+    write_edge(top, fields, edge)
+    write_planes(masked[:1] + masked, edge, len(fields) // 2)
+
+
+def pack_second_body(own, state, points, weights, tile, temp, draft, edges, numbers):
+    top = goes_north(1)
+    fields = edge_fields(state, points, weights)
+    write_edge(top, fields, draft)
+    links, blocks, rows = tile.shape
     lane = lane_ids(rows)
     diagonal = row_ids(rows, rows) == lane_ids(rows, rows)
     tiles = jnp.zeros((rows, LANES), f32)
     for k in range(links):
         for b in range(blocks):
-            line = jnp.broadcast_to(tile_in[k, b : b + 1, :].astype(f32), (rows, rows))
+            line = jnp.broadcast_to(tile[k, b : b + 1, :].astype(f32), (rows, rows))
             upright = jnp.sum(jnp.where(diagonal, line, 0.0), axis=1, keepdims=True)
             tiles = jnp.where(lane == k * blocks + b, upright, tiles)
-    for plane, values in enumerate(masked):
-        own[plane] = values
-    own[len(masked)] = tiles[:TILE]
-    own[len(masked) + 1] = tiles[TILE:]
-    top = goes_north(0)
-    fields = edge_fields(state_out, points_out, weights_out)
-    write_edge(top, fields, edge)
-    write_planes(flux_planes(top, own), edge, len(fields) // 2)
-
-
-def pack_second_body(own, state, points, weights, temp, draft, edges):
-    top = goes_north(1)
-    fields = edge_fields(state, points, weights)
-    write_edge(top, fields, draft)
-    write_planes(flux_planes(top, own), draft, len(fields) // 2)
+    numbers[0] = tiles[:TILE]
+    numbers[1] = tiles[TILE:]
+    masked = [own[plane] for plane in range(own.shape[0])]
+    write_planes([edge_numbers(top, numbers)] + masked, draft, len(fields) // 2)
     levels, rows, _ = temp.shape
     for place, columns in enumerate(edge_columns([temp[level] for level in range(levels)], rows)):
         edges[place] = columns
@@ -253,8 +253,10 @@
     write_temp_edge(goes_north(first), temp, out, 0)
 
 
-def pack_third_body(flux_at, received, edges, out):
-    write_planes(far_planes(flux_at, received) + [corner_plane(goes_north(0), edges)], out, 0)
+def pack_third_body(flux_at, received, edges, numbers, out):
+    top = goes_north(0)
+    planes = far_planes(flux_at, received)
+    write_planes(planes + [corner_plane(top, edges), edge_numbers(top, numbers)], out, 0)
 
 
 def unpack_rows(top, packed, level):
@@ -290,11 +292,11 @@
 FORCING_AT = {0: 4, 1: 5, 4: 6}
 
 
-def forcing_body(flux_at, got_a, got_b, own, state, points, weights, ext, light):
+def forcing_body(flux_at, got_a, got_b, own, numbers, state, points, weights, ext, light):
     even = lax.rem(lax.axis_index("lat"), 2) == 0
     links, rows, width = points.shape
     blocks = width // LANES
-    nflux = own.shape[0] - 2
+    nflux = own.shape[0]
     ext[:4, :rows, :] = state[...]
     north, south = [], []
     for plane in range(nflux):
@@ -309,7 +311,7 @@
             cols = slice(b * LANES, (b + 1) * LANES)
             totals = [jnp.zeros((TILE, LANES), f32) for _ in range(nflux)]
             for k in range(links):
-                within, band = row_numbers(own[nflux + row_tile], k * blocks + b)
+                within, band = row_numbers(numbers[row_tile], k * blocks + b)
                 lanes = points[k, here, cols]
                 weight = weights[k, here, cols]
                 for plane in range(nflux):
@@ -368,7 +370,9 @@
         )
         tables[plane] = [far_south, south, own[plane], north, far_north]
     sub_one = row_ids(TILE)
-    north, south = by_side(even, spot_of(got_a, flux_at, 0), spot_of(got_b, flux_at, 0))
+    north, south = by_side(
+        even, spot_of(got_c, 0, len(HALO_FLUXES) + 1), spot_of(got_b, flux_at, 0)
+    )
     numbers = jnp.where(sub_one < HALF, north, south)
     for b in range(blocks):
         cols = slice(b * LANES, (b + 1) * LANES)
@@ -713,7 +717,7 @@
     groups = levels // level_step(levels)
     place = lax.axis_index("lat")
     inner = jnp.where(lax.rem(place, 2) == 1, groups // 5, 0)
-    return jnp.where(place == 0, groups // 2, inner)
+    return jnp.where(place == 0, groups // 2, jnp.where(place == 1, groups * 2 // 5, inner))
 
 
 LAST_GROUPS = 2
@@ -838,15 +842,16 @@
     groups = pl.cdiv(levels, 4)
     tile_lines = jnp.swapaxes(donor_tile_number, 1, 2)
     temp = thermal_field
-    edge_a, own, state, points, weights, flags = call(
+    edge_a, own, state, points, weights, flags, tile = call(
         load_body,
         [
             shape(temp_at, TILE, width),
-            shape(nflux + 2, TILE, LANES),
+            shape(nflux, TILE, LANES),
             shape(4, rows, width),
             shape(links, rows, width, dtype=i32),
             shape(links, rows, width),
             shape(band_rows, lanes, dtype=i32),
+            shape(links, blocks, rows, dtype=i32),
         ],
         (
             free_elevation,
@@ -863,7 +868,6 @@
         1.6,
         scratch=[
             pltpu.VMEM((rows, width), i32),
-            pltpu.VMEM((links, blocks, rows), i32),
             pltpu.VMEM((nflux, band_rows, lanes), f32),
             pltpu.SemaphoreType.DMA((9,)),
         ],
@@ -872,13 +876,14 @@
     got_a = swap(edge_a, "lat", 0, False)
     far_tiles = (len(HALO_FLUXES) + 1) // 2
     edge_tiles = temp_at + far_tiles
-    draft_b, edges = call(
+    draft_b, edges, numbers = call(
         pack_second_body,
         [
             shape(edge_tiles, TILE, width),
             shape(2, rows, LANES),
+            shape(2, TILE, LANES),
         ],
-        (own, state, points, weights, temp),
+        (own, state, points, weights, tile, temp),
         "pack_b",
         0.3,
     )
@@ -908,8 +913,8 @@
     got_temp_a = swap(temp_a, "lat", 0, False)
     (edge_c,) = call(
         functools.partial(pack_third_body, flux_at),
-        [shape(far_tiles, TILE, width)],
-        (got_b, edges),
+        [shape((len(HALO_FLUXES) + 3) // 2, TILE, width)],
+        (got_b, edges, numbers),
         "pack_c",
         LATE,
     )
@@ -917,7 +922,7 @@
     draft_ext, light = call(
         functools.partial(forcing_body, flux_at),
         [shape(7, 3 * TILE, width), shape(2, rows, width)],
-        (got_a, got_b, own, state, points, weights),
+        (got_a, got_b, own, numbers, state, points, weights),
         "forcing",
         0.4,
     )

time: 28.8 us -> 28.4 us (0.986)
  starting transfers between devices: 15.7 us -> 15.2 us
    ppermute x9, starting transfers between devices: 15.7 us -> 15.2 us  [swap(): lax.ppermute(array, axis, swap_pairs(lax.axis_size(axis), first, periodic))]
  transfers between devices with their start and end apart: 9 -> 9, of which waited for: 3 -> 3; matrix products, arithmetic and copies ran while one was open for 0% -> 0% of each run, Pallas kernels for 23% -> 21%
where the time goes in v6:
time: 28.4 us; the launch traced here: 28.1 us
  starting transfers between devices  15.2 us (54%)
  Pallas kernels  10.5 us (37%)
  waiting for transfers between devices  1.45 us (5%)
  between operations  0.81 us (3%)
    ppermute x9, starting transfers between devices, swap(): lax.ppermute(array, axis, swap_pairs(lax.axis_size(axis), first, periodic))  15.2 us
    pallas_call x15, Pallas kernels, call(): pl.pallas_call(body, out_shape=outs, in_specs=specs, out_specs=[pl.BlockS...  10.5 us
    ppermute x9, waiting for transfers between devices, swap(): lax.ppermute(array, axis, swap_pairs(lax.axis_size(axis), first, periodic))  1.45 us
  transfers between devices with their start and end apart: 9, of which 3 were waited for; matrix products, arithmetic and copies ran while one was open for 0% of the time, Pallas kernels for 21%

profile of v6, /device:TPU:1, one launch (start us, length us, event | category | flops | bytes accessed | tf_op | source)
XLA Modules:
  0.0 28.1 jit_solution(3763452001914880361)
XLA Ops:
  0.6 0.0 copy-start
  0.6 1.2 %load.1 = (f32[9,8,256]{2,1,0:T(8,128)S(1)}, f32[5,8,128]{2,1,0:T(8,128)S(1)}, f32[4,16,256]{2,1,0:T(8,128)S(1)}, s32[4,16,256]{2,1,0:T(8,128)S(1)}, f32[4,16,25...) custom-call(f32[16,256]{1,0:T(8,128)} %height.1, f32[16,256]{1,0:T(8,128)} %zonal.1, ...), custom_call_target="tpu_custom_call" | custom-call | flops 1840000000 | bytes 1024 | tf_op jit(solution)/shard_map/load/pallas_call | solution.py:80
  1.8 0.1 collective-permute-start
  1.9 0.1 copy-done
  2.0 0.3 %pack_b.1 = (f32[11,8,256]{2,1,0:T(8,128)S(1)}, f32[2,16,128]{2,1,0:T(8,128)S(1)}, f32[2,8,128]{2,1,0:T(8,128)S(1)}) custom-call(f32[5,8,128]{2,1,0:T(8,128)S(1)} %get-tuple-element.42.own, f32[4,16,256]{2,1,0:T(8,128)S(1)} %get-tuple-element.43.state, s32[4,16,256]{2,1,0:T(8,128)S(1)} %get-tuple-element.44.points, ...), custom_call_target="tpu_custom_call" | custom-call | flops 345000000 | bytes 1024 | tf_op jit(solution)/shard_map/pack_b/pallas_call | solution.py:80
  2.3 0.8 %collective-permute-done.received.got_a = f32[9,8,256]{2,1,0:T(8,128)S(1)} collective-permute-done((f32[9,8,256]{2,1,0:T(8,128)S(1)}, f32[9,8,256]{2,1,0:T(8,128)S(1)}, u32[]{:S(2)}, u32[]{:S(2)}) %collective-permute-start) | collective-permute-done | bytes 73760 | tf_op jit(solution)/shard_map/ppermute | solution.py:50
  3.2 4.5 %collective-permute-start.1 = (f32[11,8,256]{2,1,0:T(8,128)S(1)}, f32[11,8,256]{2,1,0:T(8,128)S(1)}, u32[]{:S(2)}, u32[]{:S(2)}) collective-permute-start(f32[11,8,256]{2,1,0:T(8,128)S(1)} %pack_flux.1.other), channel_id=1, source_target_pairs={{1,2},{2,1},{3,4},{4,3},{5,6},{6,5},{9,10},{10,9},{11,12},{12,11},... | collective-permute-start | bytes 270344 | tf_op jit(solution)/shard_map/ppermute | solution.py:50
  7.7 0.1 pack_temp_b.1.other
  7.8 0.1 pack_temp_a.1
  7.8 1.9 %collective-permute-start.4 = (f32[15,8,256]{2,1,0:T(8,128)S(1)}, f32[15,8,256]{2,1,0:T(8,128)S(1)}, u32[]{:S(2)}, u32[]{:S(2)}) collective-permute-start(f32[15,8,256]{2,1,0:T(8,128)S(1)} %pack_temp_b.1.other), channel_id=1, source_target_pairs={{1,2},{2,1},{3,4},{4,3},{5,6},{6,5},{9,10},{10,9},{11,12},{12,11},... | collective-permute-start | bytes 368648 | tf_op jit(solution)/shard_map/ppermute | solution.py:50
  9.8 0.1 collective-permute-start.3
  9.8 0.1 collective-permute-done.1.got_b.received
  10.0 0.5 %collective-permute-start.2 = (f32[3,8,256]{2,1,0:T(8,128)S(1)}, f32[3,8,256]{2,1,0:T(8,128)S(1)}, u32[]{:S(2)}, u32[]{:S(2)}) collective-permute-start(f32[3,8,256]{2,1,0:T(8,128)S(1)} %pack_c.1), channel_id=1, source_target_pairs={{0,1},{1,0},{2,3},{3,2},{4,5},{5,4},{6,7},{7,6},{8,9},{9,8},{10,11... | collective-permute-start | bytes 73736 | tf_op jit(solution)/shard_map/ppermute | solution.py:50
  10.4 0.4 %forcing.1 = (f32[7,24,256]{2,1,0:T(8,128)S(1)}, f32[2,16,256]{2,1,0:T(8,128)S(1)}) custom-call(f32[9,8,256]{2,1,0:T(8,128)S(1)} %collective-permute-done.received.got_a, f32[11,8,256]{2,1,0:T(8,128)S(1)} %collective-permute-done.1.got_b.received, f32[5,8,128]{2,1,0:T(8,128)S(1)} %get-tuple-element.42.own, f32[2,8,128]{2,1,0:T(8,128)S(1)} %get-tuple-element.49.numbers, ...), custom_call_target="tpu_custom_call" | custom-call | flops 460000000 | bytes 1024 | tf_op jit(solution)/shard_map/forcing/pallas_call | solution.py:80
  10.8 0.5 %collective-permute-done.2.got_c = f32[3,8,256]{2,1,0:T(8,128)S(1)} collective-permute-done((f32[3,8,256]{2,1,0:T(8,128)S(1)}, f32[3,8,256]{2,1,0:T(8,128)S(1)}, u32[]{:S(2)}, u32[]{:S(2)}) %collective-permute-start.2) | collective-permute-done | bytes 24608 | tf_op jit(solution)/shard_map/ppermute | solution.py:50
  11.3 0.3 forcing_halo.1
  11.6 1.9 %collective-permute-start.5 = (f32[2,24,128]{2,1,0:T(8,128)S(1)}, f32[2,24,128]{2,1,0:T(8,128)S(1)}, u32[]{:S(2)}, u32[]{:S(2)}) collective-permute-start(f32[2,24,128]{2,1,0:T(8,128)S(1)} %pass_lon.1), channel_id=1, source_target_pairs={{0,8},{8,0},{16,24},{24,16},{1,9},{9,1},{17,25},{25,17},{2,10},{10... | collective-permute-start | bytes 73736 | tf_op jit(solution)/shard_map/ppermute | solution.py:50
  13.5 2.2 %collective-permute-start.6 = (f32[2,24,128]{2,1,0:T(8,128)S(1)}, f32[2,24,128]{2,1,0:T(8,128)S(1)}, u32[]{:S(2)}, u32[]{:S(2)}) collective-permute-start(f32[2,24,128]{2,1,0:T(8,128)S(1)} %get-tuple-element.58.second), channel_id=1, source_target_pairs={{8,16},{16,8},{24,0},{0,24},{9,17},{17,9},{25,1},{1,25},{10,18},{1... | collective-permute-start | bytes 73736 | tf_op jit(solution)/shard_map/ppermute | solution.py:50
  15.7 1.1 %hot.1 = bf16[64,128,256]{2,1,0:T(8,128)(2,1)S(1)} custom-call(s32[4,16,256]{2,1,0:T(8,128)S(1)} %get-tuple-element.44.points), custom_call_target="tpu_custom_call" | custom-call | bytes 1024 | tf_op jit(solution)/shard_map/hot/pallas_call | solution.py:80
  16.8 0.0 collective-permute-done.3.got_a
  16.8 0.0 collective-permute-done.4.got_b
  16.8 1.8 %before.1 = (f32[60,16,256]{2,1,0:T(8,128)S(1)}, f32[60,24,256]{2,1,0:T(8,128)S(1)}, f32[60,8,256]{2,1,0:T(8,128)S(1)}) custom-call(f32[7,24,256]{2,1,0:T(8,128)S(1)} %get-tuple-element.51.ext, f32[2,16,256]{2,1,0:T(8,128)S(1)} %get-tuple-element.52.light, f32[60,16,256]{2,1,0:T(8,128)S(1)} %copy-done, f32[15,8,256]{2,1,0:T(8,128)S(1)} %collective-permute-done.3.got_a, ...), custom_call_target="tpu_custom_call" | custom-call | bytes 1024 | tf_op jit(solution)/shard_map/before/pallas_call | solution.py:80
  18.7 0.0 collective-permute-done.5.got_a
  18.7 0.0 collective-permute-done.6.got_b
  18.7 2.7 %subcycles.1 = (f32[16,256]{1,0:T(8,128)S(1)}, f32[16,256]{1,0:T(8,128)S(1)}, f32[16,256]{1,0:T(8,128)S(1)}, f32[4,16,256]{2,1,0:T(8,128)S(1)}, f32[4,16,256]{2,...) custom-call(f32[7,24,256]{2,1,0:T(8,128)S(1)} %get-tuple-element.51., ...), custom_call_target="tpu_custom_call" | custom-call | flops 2990000128 | bytes 1024 | tf_op jit(solution)/shard_map/subcycles/pallas_call | solution.py:80
  21.4 4.0 %collective-permute-start.8 = (f32[5,8,128]{2,1,0:T(8,128)S(1)}, f32[5,8,128]{2,1,0:T(8,128)S(1)}, u32[]{:S(2)}, u32[]{:S(2)}) collective-permute-start(f32[5,8,128]{2,1,0:T(8,128)S(1)} %get-tuple-element.71.second), channel_id=1, source_target_pairs={{1,2},{2,1},{3,4},{4,3},{5,6},{6,5},{9,10},{10,9},{11,12},{12,11},... | collective-permute-start | bytes 61448 | tf_op jit(solution)/shard_map/ppermute | solution.py:50
  25.4 0.1 collective-permute-start.7
  25.5 1.9 %tracer.1 = (f32[16,256]{1,0:T(8,128)}, f32[16,256]{1,0:T(8,128)}, f32[16,256]{1,0:T(8,128)}, f32[60,16,256]{2,1,0:T(8,128)}, f32[60,16,256]{2,1,0:T(8,128)S(1)}) custom-call(f32[60,16,256]{2,1,0:T(8,128)S(1)} %copy-done, f32[60,8,256]{2,1,0:T(8,128)S(1)} %get-tuple-element.53.halo, f32[60,16,256]{2,1,0:T(8,128)S(1)} %get-tuple-element.54.base, ...), custom_call_target="tpu_custom_call" | custom-call | flops 2875000064 | bytes 1024 | tf_op jit(solution)/shard_map/tracer/pallas_call | solution.py:80
  27.4 0.0 collective-permute-done.7.got_a
  27.4 0.0 collective-permute-done.8.got_b
  27.4 0.7 %merge.1 = (f32[4,8,128]{2,1,0:T(8,128)}, f32[60,16,256]{2,1,0:T(8,128)}) custom-call(f32[5,8,128]{2,1,0:T(8,128)S(1)} %get-tuple-element.69.mid, f32[5,8,128]{2,1,0:T(8,128)S(1)} %collective-permute-done.7.got_a, f32[5,8,128]{2,1,0:T(8,128)S(1)} %collective-permute-done.8.got_b, ...), custom_call_target="tpu_custom_call", output_to_operand_aliasing={{1}: (5, {})} | custom-call | flops 115000000 | bytes 1024 | tf_op jit(solution)/shard_map/merge/pallas_call | solution.py:80
  (4 shorter events, 0.0 us)
Async XLA Ops:
  0.6 1.4 %copy-start = (f32[60,16,256]{2,1,0:T(8,128)S(1)}, f32[60,16,256]{2,1,0:T(8,128)}, u32[]{:S(2)}) copy-start(f32[60,16,256]{2,1,0:T(8,128)} %temp.11) | copy-start | bytes 2949124
  1.8 1.3 %collective-permute-start = (f32[9,8,256]{2,1,0:T(8,128)S(1)}, f32[9,8,256]{2,1,0:T(8,128)S(1)}, u32[]{:S(2)}, u32[]{:S(2)}) collective-permute-start(f32[9,8,256]{2,1,0:T(8,128)S(1)} %get-tuple-element.41), channel_id=1, source_target_pairs={{0,1},{1,0},{2,3},{3,2},{4,5},{5,4},{6,7},{7,6},{8,9},{9,8},{10,11... | collective-permute-start | bytes 221192 | tf_op jit(solution)/shard_map/ppermute | solution.py:50
  3.2 6.8 %collective-permute-start.1 = (f32[11,8,256]{2,1,0:T(8,128)S(1)}, f32[11,8,256]{2,1,0:T(8,128)S(1)}, u32[]{:S(2)}, u32[]{:S(2)}) collective-permute-start(f32[11,8,256]{2,1,0:T(8,128)S(1)} %pack_flux.1.other), channel_id=1, source_target_pairs={{1,2},{2,1},{3,4},{4,3},{5,6},{6,5},{9,10},{10,9},{11,12},{12,11},... | collective-permute-start | bytes 270344 | tf_op jit(solution)/shard_map/ppermute | solution.py:50
  7.8 9.0 %collective-permute-start.4 = (f32[15,8,256]{2,1,0:T(8,128)S(1)}, f32[15,8,256]{2,1,0:T(8,128)S(1)}, u32[]{:S(2)}, u32[]{:S(2)}) collective-permute-start(f32[15,8,256]{2,1,0:T(8,128)S(1)} %pack_temp_b.1.other), channel_id=1, source_target_pairs={{1,2},{2,1},{3,4},{4,3},{5,6},{6,5},{9,10},{10,9},{11,12},{12,11},... | collective-permute-start | bytes 368648 | tf_op jit(solution)/shard_map/ppermute | solution.py:50
  9.8 7.0 %collective-permute-start.3 = (f32[15,8,256]{2,1,0:T(8,128)S(1)}, f32[15,8,256]{2,1,0:T(8,128)S(1)}, u32[]{:S(2)}, u32[]{:S(2)}) collective-permute-start(f32[15,8,256]{2,1,0:T(8,128)S(1)} %pack_temp_a.1), channel_id=1, source_target_pairs={{0,1},{1,0},{2,3},{3,2},{4,5},{5,4},{6,7},{7,6},{8,9},{9,8},{10,11... | collective-permute-start | bytes 368648 | tf_op jit(solution)/shard_map/ppermute | solution.py:50
  10.0 1.3 %collective-permute-start.2 = (f32[3,8,256]{2,1,0:T(8,128)S(1)}, f32[3,8,256]{2,1,0:T(8,128)S(1)}, u32[]{:S(2)}, u32[]{:S(2)}) collective-permute-start(f32[3,8,256]{2,1,0:T(8,128)S(1)} %pack_c.1), channel_id=1, source_target_pairs={{0,1},{1,0},{2,3},{3,2},{4,5},{5,4},{6,7},{7,6},{8,9},{9,8},{10,11... | collective-permute-start | bytes 73736 | tf_op jit(solution)/shard_map/ppermute | solution.py:50
  11.6 7.1 %collective-permute-start.5 = (f32[2,24,128]{2,1,0:T(8,128)S(1)}, f32[2,24,128]{2,1,0:T(8,128)S(1)}, u32[]{:S(2)}, u32[]{:S(2)}) collective-permute-start(f32[2,24,128]{2,1,0:T(8,128)S(1)} %pass_lon.1), channel_id=1, source_target_pairs={{0,8},{8,0},{16,24},{24,16},{1,9},{9,1},{17,25},{25,17},{2,10},{10... | collective-permute-start | bytes 73736 | tf_op jit(solution)/shard_map/ppermute | solution.py:50
  13.5 5.2 %collective-permute-start.6 = (f32[2,24,128]{2,1,0:T(8,128)S(1)}, f32[2,24,128]{2,1,0:T(8,128)S(1)}, u32[]{:S(2)}, u32[]{:S(2)}) collective-permute-start(f32[2,24,128]{2,1,0:T(8,128)S(1)} %get-tuple-element.58.second), channel_id=1, source_target_pairs={{8,16},{16,8},{24,0},{0,24},{9,17},{17,9},{25,1},{1,25},{10,18},{1... | collective-permute-start | bytes 73736 | tf_op jit(solution)/shard_map/ppermute | solution.py:50
  21.4 6.0 %collective-permute-start.8 = (f32[5,8,128]{2,1,0:T(8,128)S(1)}, f32[5,8,128]{2,1,0:T(8,128)S(1)}, u32[]{:S(2)}, u32[]{:S(2)}) collective-permute-start(f32[5,8,128]{2,1,0:T(8,128)S(1)} %get-tuple-element.71.second), channel_id=1, source_target_pairs={{1,2},{2,1},{3,4},{4,3},{5,6},{6,5},{9,10},{10,9},{11,12},{12,11},... | collective-permute-start | bytes 61448 | tf_op jit(solution)/shard_map/ppermute | solution.py:50
  25.4 2.0 %collective-permute-start.7 = (f32[5,8,128]{2,1,0:T(8,128)S(1)}, f32[5,8,128]{2,1,0:T(8,128)S(1)}, u32[]{:S(2)}, u32[]{:S(2)}) collective-permute-start(f32[5,8,128]{2,1,0:T(8,128)S(1)} %pass_sums.1), channel_id=1, source_target_pairs={{0,1},{1,0},{2,3},{3,2},{4,5},{5,4},{6,7},{7,6},{8,9},{9,8},{10,11... | collective-permute-start | bytes 61448 | tf_op jit(solution)/shard_map/ppermute | solution.py:50

commit v7 on v6

--- a/solution.py
+++ b/solution.py
@@ -432,6 +432,7 @@
 
 
 LEVELS_AT_ONCE = 6
+LEVELS_BEFORE = 10
 
 
 def before_body(ext, light, temp, got_a, got_b, base, laps, halo):
@@ -442,7 +443,7 @@
     limit_east = jnp.where(lane == width - 1, 0.0, jnp.minimum(counts, roll_lanes(counts, -1)))
     limit_north = jnp.minimum(counts, roll_rows(counts, -1))
     limits = (limit_east, roll_lanes(limit_east, 1), limit_north, roll_rows(limit_north, 1))
-    step = math.gcd(levels, LEVELS_AT_ONCE)
+    step = math.gcd(levels, LEVELS_BEFORE)
     odd = lax.rem(lax.axis_index("lat"), 2) == 1
     near = near_lanes(width)
     for level in range(levels):

time: 28.4 us -> 28.4 us (level)
  no operation moved by 1% of the time
where the time goes in v7:
time: 28.4 us; the launch traced here: 28.1 us
  starting transfers between devices  15.4 us (54%)
  Pallas kernels  10.4 us (37%)
  waiting for transfers between devices  1.45 us (5%)
  between operations  0.81 us (3%)
    ppermute x9, starting transfers between devices, swap(): lax.ppermute(array, axis, swap_pairs(lax.axis_size(axis), first, periodic))  15.4 us
    pallas_call x15, Pallas kernels, call(): pl.pallas_call(body, out_shape=outs, in_specs=specs, out_specs=[pl.BlockS...  10.4 us
    ppermute x9, waiting for transfers between devices, swap(): lax.ppermute(array, axis, swap_pairs(lax.axis_size(axis), first, periodic))  1.45 us
  transfers between devices with their start and end apart: 9, of which 3 were waited for; matrix products, arithmetic and copies ran while one was open for 0% of the time, Pallas kernels for 21%

profile of v7, /device:TPU:1, one launch (start us, length us, event | category | flops | bytes accessed | tf_op | source)
XLA Modules:
  0.0 28.1 jit_solution(9785698795109585873)
XLA Ops:
  0.6 0.0 copy-start
  0.6 1.2 %load.1 = (f32[9,8,256]{2,1,0:T(8,128)S(1)}, f32[5,8,128]{2,1,0:T(8,128)S(1)}, f32[4,16,256]{2,1,0:T(8,128)S(1)}, s32[4,16,256]{2,1,0:T(8,128)S(1)}, f32[4,16,25...) custom-call(f32[16,256]{1,0:T(8,128)} %height.1, f32[16,256]{1,0:T(8,128)} %zonal.1, ...), custom_call_target="tpu_custom_call" | custom-call | flops 1840000000 | bytes 1024 | tf_op jit(solution)/shard_map/load/pallas_call | solution.py:80
  1.8 0.1 collective-permute-start
  1.9 0.1 copy-done
  2.0 0.3 %pack_b.1 = (f32[11,8,256]{2,1,0:T(8,128)S(1)}, f32[2,16,128]{2,1,0:T(8,128)S(1)}, f32[2,8,128]{2,1,0:T(8,128)S(1)}) custom-call(f32[5,8,128]{2,1,0:T(8,128)S(1)} %get-tuple-element.42.own, f32[4,16,256]{2,1,0:T(8,128)S(1)} %get-tuple-element.43.state, s32[4,16,256]{2,1,0:T(8,128)S(1)} %get-tuple-element.44.points, ...), custom_call_target="tpu_custom_call" | custom-call | flops 345000000 | bytes 1024 | tf_op jit(solution)/shard_map/pack_b/pallas_call | solution.py:80
  2.3 0.8 %collective-permute-done.received.got_a = f32[9,8,256]{2,1,0:T(8,128)S(1)} collective-permute-done((f32[9,8,256]{2,1,0:T(8,128)S(1)}, f32[9,8,256]{2,1,0:T(8,128)S(1)}, u32[]{:S(2)}, u32[]{:S(2)}) %collective-permute-start) | collective-permute-done | bytes 73760 | tf_op jit(solution)/shard_map/ppermute | solution.py:50
  3.2 4.5 %collective-permute-start.1 = (f32[11,8,256]{2,1,0:T(8,128)S(1)}, f32[11,8,256]{2,1,0:T(8,128)S(1)}, u32[]{:S(2)}, u32[]{:S(2)}) collective-permute-start(f32[11,8,256]{2,1,0:T(8,128)S(1)} %pack_flux.1.other), channel_id=1, source_target_pairs={{1,2},{2,1},{3,4},{4,3},{5,6},{6,5},{9,10},{10,9},{11,12},{12,11},... | collective-permute-start | bytes 270344 | tf_op jit(solution)/shard_map/ppermute | solution.py:50
  7.7 0.1 pack_temp_b.1.other
  7.8 0.1 pack_temp_a.1
  7.8 1.9 %collective-permute-start.4 = (f32[15,8,256]{2,1,0:T(8,128)S(1)}, f32[15,8,256]{2,1,0:T(8,128)S(1)}, u32[]{:S(2)}, u32[]{:S(2)}) collective-permute-start(f32[15,8,256]{2,1,0:T(8,128)S(1)} %pack_temp_b.1.other), channel_id=1, source_target_pairs={{1,2},{2,1},{3,4},{4,3},{5,6},{6,5},{9,10},{10,9},{11,12},{12,11},... | collective-permute-start | bytes 368648 | tf_op jit(solution)/shard_map/ppermute | solution.py:50
  9.8 0.1 collective-permute-start.3
  9.8 0.1 collective-permute-done.1.got_b.received
  10.0 0.5 %collective-permute-start.2 = (f32[3,8,256]{2,1,0:T(8,128)S(1)}, f32[3,8,256]{2,1,0:T(8,128)S(1)}, u32[]{:S(2)}, u32[]{:S(2)}) collective-permute-start(f32[3,8,256]{2,1,0:T(8,128)S(1)} %pack_c.1), channel_id=1, source_target_pairs={{0,1},{1,0},{2,3},{3,2},{4,5},{5,4},{6,7},{7,6},{8,9},{9,8},{10,11... | collective-permute-start | bytes 73736 | tf_op jit(solution)/shard_map/ppermute | solution.py:50
  10.4 0.4 %forcing.1 = (f32[7,24,256]{2,1,0:T(8,128)S(1)}, f32[2,16,256]{2,1,0:T(8,128)S(1)}) custom-call(f32[9,8,256]{2,1,0:T(8,128)S(1)} %collective-permute-done.received.got_a, f32[11,8,256]{2,1,0:T(8,128)S(1)} %collective-permute-done.1.got_b.received, f32[5,8,128]{2,1,0:T(8,128)S(1)} %get-tuple-element.42.own, f32[2,8,128]{2,1,0:T(8,128)S(1)} %get-tuple-element.49.numbers, ...), custom_call_target="tpu_custom_call" | custom-call | flops 460000000 | bytes 1024 | tf_op jit(solution)/shard_map/forcing/pallas_call | solution.py:80
  10.8 0.5 %collective-permute-done.2.got_c = f32[3,8,256]{2,1,0:T(8,128)S(1)} collective-permute-done((f32[3,8,256]{2,1,0:T(8,128)S(1)}, f32[3,8,256]{2,1,0:T(8,128)S(1)}, u32[]{:S(2)}, u32[]{:S(2)}) %collective-permute-start.2) | collective-permute-done | bytes 24608 | tf_op jit(solution)/shard_map/ppermute | solution.py:50
  11.3 0.3 forcing_halo.1
  11.6 1.9 %collective-permute-start.5 = (f32[2,24,128]{2,1,0:T(8,128)S(1)}, f32[2,24,128]{2,1,0:T(8,128)S(1)}, u32[]{:S(2)}, u32[]{:S(2)}) collective-permute-start(f32[2,24,128]{2,1,0:T(8,128)S(1)} %pass_lon.1), channel_id=1, source_target_pairs={{0,8},{8,0},{16,24},{24,16},{1,9},{9,1},{17,25},{25,17},{2,10},{10... | collective-permute-start | bytes 73736 | tf_op jit(solution)/shard_map/ppermute | solution.py:50
  13.5 2.2 %collective-permute-start.6 = (f32[2,24,128]{2,1,0:T(8,128)S(1)}, f32[2,24,128]{2,1,0:T(8,128)S(1)}, u32[]{:S(2)}, u32[]{:S(2)}) collective-permute-start(f32[2,24,128]{2,1,0:T(8,128)S(1)} %get-tuple-element.58.second), channel_id=1, source_target_pairs={{8,16},{16,8},{24,0},{0,24},{9,17},{17,9},{25,1},{1,25},{10,18},{1... | collective-permute-start | bytes 73736 | tf_op jit(solution)/shard_map/ppermute | solution.py:50
  15.7 1.1 %hot.1 = bf16[64,128,256]{2,1,0:T(8,128)(2,1)S(1)} custom-call(s32[4,16,256]{2,1,0:T(8,128)S(1)} %get-tuple-element.44.points), custom_call_target="tpu_custom_call" | custom-call | bytes 1024 | tf_op jit(solution)/shard_map/hot/pallas_call | solution.py:80
  16.8 0.0 collective-permute-done.3.got_a
  16.8 0.0 collective-permute-done.4.got_b
  16.8 1.7 %before.1 = (f32[60,16,256]{2,1,0:T(8,128)S(1)}, f32[60,24,256]{2,1,0:T(8,128)S(1)}, f32[60,8,256]{2,1,0:T(8,128)S(1)}) custom-call(f32[7,24,256]{2,1,0:T(8,128)S(1)} %get-tuple-element.51.ext, f32[2,16,256]{2,1,0:T(8,128)S(1)} %get-tuple-element.52.light, f32[60,16,256]{2,1,0:T(8,128)S(1)} %copy-done, f32[15,8,256]{2,1,0:T(8,128)S(1)} %collective-permute-done.3.got_a, ...), custom_call_target="tpu_custom_call" | custom-call | bytes 1024 | tf_op jit(solution)/shard_map/before/pallas_call | solution.py:80
  18.5 0.0 collective-permute-done.5.got_a
  18.5 0.0 collective-permute-done.6.got_b
  18.5 2.7 %subcycles.1 = (f32[16,256]{1,0:T(8,128)S(1)}, f32[16,256]{1,0:T(8,128)S(1)}, f32[16,256]{1,0:T(8,128)S(1)}, f32[4,16,256]{2,1,0:T(8,128)S(1)}, f32[4,16,256]{2,...) custom-call(f32[7,24,256]{2,1,0:T(8,128)S(1)} %get-tuple-element.51., ...), custom_call_target="tpu_custom_call" | custom-call | flops 2990000128 | bytes 1024 | tf_op jit(solution)/shard_map/subcycles/pallas_call | solution.py:80
  21.2 4.1 %collective-permute-start.8 = (f32[5,8,128]{2,1,0:T(8,128)S(1)}, f32[5,8,128]{2,1,0:T(8,128)S(1)}, u32[]{:S(2)}, u32[]{:S(2)}) collective-permute-start(f32[5,8,128]{2,1,0:T(8,128)S(1)} %get-tuple-element.71.second), channel_id=1, source_target_pairs={{1,2},{2,1},{3,4},{4,3},{5,6},{6,5},{9,10},{10,9},{11,12},{12,11},... | collective-permute-start | bytes 61448 | tf_op jit(solution)/shard_map/ppermute | solution.py:50
  25.4 0.1 collective-permute-start.7
  25.5 1.9 %tracer.1 = (f32[16,256]{1,0:T(8,128)}, f32[16,256]{1,0:T(8,128)}, f32[16,256]{1,0:T(8,128)}, f32[60,16,256]{2,1,0:T(8,128)}, f32[60,16,256]{2,1,0:T(8,128)S(1)}) custom-call(f32[60,16,256]{2,1,0:T(8,128)S(1)} %copy-done, f32[60,8,256]{2,1,0:T(8,128)S(1)} %get-tuple-element.53.halo, f32[60,16,256]{2,1,0:T(8,128)S(1)} %get-tuple-element.54.base, ...), custom_call_target="tpu_custom_call" | custom-call | flops 2875000064 | bytes 1024 | tf_op jit(solution)/shard_map/tracer/pallas_call | solution.py:80
  27.3 0.0 collective-permute-done.7.got_a
  27.4 0.0 collective-permute-done.8.got_b
  27.4 0.7 %merge.1 = (f32[4,8,128]{2,1,0:T(8,128)}, f32[60,16,256]{2,1,0:T(8,128)}) custom-call(f32[5,8,128]{2,1,0:T(8,128)S(1)} %get-tuple-element.69.mid, f32[5,8,128]{2,1,0:T(8,128)S(1)} %collective-permute-done.7.got_a, f32[5,8,128]{2,1,0:T(8,128)S(1)} %collective-permute-done.8.got_b, ...), custom_call_target="tpu_custom_call", output_to_operand_aliasing={{1}: (5, {})} | custom-call | flops 115000000 | bytes 1024 | tf_op jit(solution)/shard_map/merge/pallas_call | solution.py:80
  (4 shorter events, 0.0 us)
Async XLA Ops:
  0.6 1.4 %copy-start = (f32[60,16,256]{2,1,0:T(8,128)S(1)}, f32[60,16,256]{2,1,0:T(8,128)}, u32[]{:S(2)}) copy-start(f32[60,16,256]{2,1,0:T(8,128)} %temp.11) | copy-start | bytes 2949124
  1.8 1.3 %collective-permute-start = (f32[9,8,256]{2,1,0:T(8,128)S(1)}, f32[9,8,256]{2,1,0:T(8,128)S(1)}, u32[]{:S(2)}, u32[]{:S(2)}) collective-permute-start(f32[9,8,256]{2,1,0:T(8,128)S(1)} %get-tuple-element.41), channel_id=1, source_target_pairs={{0,1},{1,0},{2,3},{3,2},{4,5},{5,4},{6,7},{7,6},{8,9},{9,8},{10,11... | collective-permute-start | bytes 221192 | tf_op jit(solution)/shard_map/ppermute | solution.py:50
  3.2 6.8 %collective-permute-start.1 = (f32[11,8,256]{2,1,0:T(8,128)S(1)}, f32[11,8,256]{2,1,0:T(8,128)S(1)}, u32[]{:S(2)}, u32[]{:S(2)}) collective-permute-start(f32[11,8,256]{2,1,0:T(8,128)S(1)} %pack_flux.1.other), channel_id=1, source_target_pairs={{1,2},{2,1},{3,4},{4,3},{5,6},{6,5},{9,10},{10,9},{11,12},{12,11},... | collective-permute-start | bytes 270344 | tf_op jit(solution)/shard_map/ppermute | solution.py:50
  7.8 9.0 %collective-permute-start.4 = (f32[15,8,256]{2,1,0:T(8,128)S(1)}, f32[15,8,256]{2,1,0:T(8,128)S(1)}, u32[]{:S(2)}, u32[]{:S(2)}) collective-permute-start(f32[15,8,256]{2,1,0:T(8,128)S(1)} %pack_temp_b.1.other), channel_id=1, source_target_pairs={{1,2},{2,1},{3,4},{4,3},{5,6},{6,5},{9,10},{10,9},{11,12},{12,11},... | collective-permute-start | bytes 368648 | tf_op jit(solution)/shard_map/ppermute | solution.py:50
  9.8 7.0 %collective-permute-start.3 = (f32[15,8,256]{2,1,0:T(8,128)S(1)}, f32[15,8,256]{2,1,0:T(8,128)S(1)}, u32[]{:S(2)}, u32[]{:S(2)}) collective-permute-start(f32[15,8,256]{2,1,0:T(8,128)S(1)} %pack_temp_a.1), channel_id=1, source_target_pairs={{0,1},{1,0},{2,3},{3,2},{4,5},{5,4},{6,7},{7,6},{8,9},{9,8},{10,11... | collective-permute-start | bytes 368648 | tf_op jit(solution)/shard_map/ppermute | solution.py:50
  10.0 1.3 %collective-permute-start.2 = (f32[3,8,256]{2,1,0:T(8,128)S(1)}, f32[3,8,256]{2,1,0:T(8,128)S(1)}, u32[]{:S(2)}, u32[]{:S(2)}) collective-permute-start(f32[3,8,256]{2,1,0:T(8,128)S(1)} %pack_c.1), channel_id=1, source_target_pairs={{0,1},{1,0},{2,3},{3,2},{4,5},{5,4},{6,7},{7,6},{8,9},{9,8},{10,11... | collective-permute-start | bytes 73736 | tf_op jit(solution)/shard_map/ppermute | solution.py:50
  11.6 7.0 %collective-permute-start.5 = (f32[2,24,128]{2,1,0:T(8,128)S(1)}, f32[2,24,128]{2,1,0:T(8,128)S(1)}, u32[]{:S(2)}, u32[]{:S(2)}) collective-permute-start(f32[2,24,128]{2,1,0:T(8,128)S(1)} %pass_lon.1), channel_id=1, source_target_pairs={{0,8},{8,0},{16,24},{24,16},{1,9},{9,1},{17,25},{25,17},{2,10},{10... | collective-permute-start | bytes 73736 | tf_op jit(solution)/shard_map/ppermute | solution.py:50
  13.5 5.0 %collective-permute-start.6 = (f32[2,24,128]{2,1,0:T(8,128)S(1)}, f32[2,24,128]{2,1,0:T(8,128)S(1)}, u32[]{:S(2)}, u32[]{:S(2)}) collective-permute-start(f32[2,24,128]{2,1,0:T(8,128)S(1)} %get-tuple-element.58.second), channel_id=1, source_target_pairs={{8,16},{16,8},{24,0},{0,24},{9,17},{17,9},{25,1},{1,25},{10,18},{1... | collective-permute-start | bytes 73736 | tf_op jit(solution)/shard_map/ppermute | solution.py:50
  21.2 6.1 %collective-permute-start.8 = (f32[5,8,128]{2,1,0:T(8,128)S(1)}, f32[5,8,128]{2,1,0:T(8,128)S(1)}, u32[]{:S(2)}, u32[]{:S(2)}) collective-permute-start(f32[5,8,128]{2,1,0:T(8,128)S(1)} %get-tuple-element.71.second), channel_id=1, source_target_pairs={{1,2},{2,1},{3,4},{4,3},{5,6},{6,5},{9,10},{10,9},{11,12},{12,11},... | collective-permute-start | bytes 61448 | tf_op jit(solution)/shard_map/ppermute | solution.py:50
  25.4 2.0 %collective-permute-start.7 = (f32[5,8,128]{2,1,0:T(8,128)S(1)}, f32[5,8,128]{2,1,0:T(8,128)S(1)}, u32[]{:S(2)}, u32[]{:S(2)}) collective-permute-start(f32[5,8,128]{2,1,0:T(8,128)S(1)} %pass_sums.1), channel_id=1, source_target_pairs={{0,1},{1,0},{2,3},{3,2},{4,5},{5,4},{6,7},{7,6},{8,9},{9,8},{10,11... | collective-permute-start | bytes 61448 | tf_op jit(solution)/shard_map/ppermute | solution.py:50

commit v8 on v7

--- a/solution.py
+++ b/solution.py
@@ -718,7 +718,7 @@
     groups = levels // level_step(levels)
     place = lax.axis_index("lat")
     inner = jnp.where(lax.rem(place, 2) == 1, groups // 5, 0)
-    return jnp.where(place == 0, groups // 2, jnp.where(place == 1, groups * 2 // 5, inner))
+    return jnp.where(place == 0, groups * 7 // 10, jnp.where(place == 1, groups // 2, inner))
 
 
 LAST_GROUPS = 2

time: 28.4 us -> 28.2 us (level)
  starting transfers between devices: 15.4 us -> 15.1 us
  transfers between devices with their start and end apart: 9 -> 9, of which waited for: 3 -> 3; matrix products, arithmetic and copies ran while one was open for 0% -> 0% of each run, Pallas kernels for 21% -> 20%
where the time goes in v8:
time: 28.2 us; the launch traced here: 27.8 us
  starting transfers between devices  15.1 us (54%)
  Pallas kernels  10.4 us (37%)
  waiting for transfers between devices  1.45 us (5%)
  between operations  0.81 us (3%)
    ppermute x9, starting transfers between devices, swap(): lax.ppermute(array, axis, swap_pairs(lax.axis_size(axis), first, periodic))  15.1 us
    pallas_call x15, Pallas kernels, call(): pl.pallas_call(body, out_shape=outs, in_specs=specs, out_specs=[pl.BlockS...  10.4 us
    ppermute x9, waiting for transfers between devices, swap(): lax.ppermute(array, axis, swap_pairs(lax.axis_size(axis), first, periodic))  1.45 us
  transfers between devices with their start and end apart: 9, of which 3 were waited for; matrix products, arithmetic and copies ran while one was open for 0% of the time, Pallas kernels for 20%

profile of v8, /device:TPU:1, one launch (start us, length us, event | category | flops | bytes accessed | tf_op | source)
XLA Modules:
  0.0 27.8 jit_solution(4944376286148555270)
XLA Ops:
  0.6 0.0 copy-start
  0.6 1.2 %load.1 = (f32[9,8,256]{2,1,0:T(8,128)S(1)}, f32[5,8,128]{2,1,0:T(8,128)S(1)}, f32[4,16,256]{2,1,0:T(8,128)S(1)}, s32[4,16,256]{2,1,0:T(8,128)S(1)}, f32[4,16,25...) custom-call(f32[16,256]{1,0:T(8,128)} %height.1, f32[16,256]{1,0:T(8,128)} %zonal.1, ...), custom_call_target="tpu_custom_call" | custom-call | flops 1840000000 | bytes 1024 | tf_op jit(solution)/shard_map/load/pallas_call | solution.py:80
  1.8 0.1 collective-permute-start
  1.9 0.1 copy-done
  2.0 0.3 %pack_b.1 = (f32[11,8,256]{2,1,0:T(8,128)S(1)}, f32[2,16,128]{2,1,0:T(8,128)S(1)}, f32[2,8,128]{2,1,0:T(8,128)S(1)}) custom-call(f32[5,8,128]{2,1,0:T(8,128)S(1)} %get-tuple-element.42.own, f32[4,16,256]{2,1,0:T(8,128)S(1)} %get-tuple-element.43.state, s32[4,16,256]{2,1,0:T(8,128)S(1)} %get-tuple-element.44.points, ...), custom_call_target="tpu_custom_call" | custom-call | flops 345000000 | bytes 1024 | tf_op jit(solution)/shard_map/pack_b/pallas_call | solution.py:80
  2.3 0.8 %collective-permute-done.received.got_a = f32[9,8,256]{2,1,0:T(8,128)S(1)} collective-permute-done((f32[9,8,256]{2,1,0:T(8,128)S(1)}, f32[9,8,256]{2,1,0:T(8,128)S(1)}, u32[]{:S(2)}, u32[]{:S(2)}) %collective-permute-start) | collective-permute-done | bytes 73760 | tf_op jit(solution)/shard_map/ppermute | solution.py:50
  3.2 4.5 %collective-permute-start.1 = (f32[11,8,256]{2,1,0:T(8,128)S(1)}, f32[11,8,256]{2,1,0:T(8,128)S(1)}, u32[]{:S(2)}, u32[]{:S(2)}) collective-permute-start(f32[11,8,256]{2,1,0:T(8,128)S(1)} %pack_flux.1.other), channel_id=1, source_target_pairs={{1,2},{2,1},{3,4},{4,3},{5,6},{6,5},{9,10},{10,9},{11,12},{12,11},... | collective-permute-start | bytes 270344 | tf_op jit(solution)/shard_map/ppermute | solution.py:50
  7.7 0.1 pack_temp_b.1.other
  7.8 0.1 pack_temp_a.1
  7.8 1.9 %collective-permute-start.4 = (f32[15,8,256]{2,1,0:T(8,128)S(1)}, f32[15,8,256]{2,1,0:T(8,128)S(1)}, u32[]{:S(2)}, u32[]{:S(2)}) collective-permute-start(f32[15,8,256]{2,1,0:T(8,128)S(1)} %pack_temp_b.1.other), channel_id=1, source_target_pairs={{1,2},{2,1},{3,4},{4,3},{5,6},{6,5},{9,10},{10,9},{11,12},{12,11},... | collective-permute-start | bytes 368648 | tf_op jit(solution)/shard_map/ppermute | solution.py:50
  9.8 0.1 collective-permute-start.3
  9.8 0.1 collective-permute-done.1.got_b.received
  10.0 0.5 %collective-permute-start.2 = (f32[3,8,256]{2,1,0:T(8,128)S(1)}, f32[3,8,256]{2,1,0:T(8,128)S(1)}, u32[]{:S(2)}, u32[]{:S(2)}) collective-permute-start(f32[3,8,256]{2,1,0:T(8,128)S(1)} %pack_c.1), channel_id=1, source_target_pairs={{0,1},{1,0},{2,3},{3,2},{4,5},{5,4},{6,7},{7,6},{8,9},{9,8},{10,11... | collective-permute-start | bytes 73736 | tf_op jit(solution)/shard_map/ppermute | solution.py:50
  10.4 0.4 %forcing.1 = (f32[7,24,256]{2,1,0:T(8,128)S(1)}, f32[2,16,256]{2,1,0:T(8,128)S(1)}) custom-call(f32[9,8,256]{2,1,0:T(8,128)S(1)} %collective-permute-done.received.got_a, f32[11,8,256]{2,1,0:T(8,128)S(1)} %collective-permute-done.1.got_b.received, f32[5,8,128]{2,1,0:T(8,128)S(1)} %get-tuple-element.42.own, f32[2,8,128]{2,1,0:T(8,128)S(1)} %get-tuple-element.49.numbers, ...), custom_call_target="tpu_custom_call" | custom-call | flops 460000000 | bytes 1024 | tf_op jit(solution)/shard_map/forcing/pallas_call | solution.py:80
  10.8 0.5 %collective-permute-done.2.got_c = f32[3,8,256]{2,1,0:T(8,128)S(1)} collective-permute-done((f32[3,8,256]{2,1,0:T(8,128)S(1)}, f32[3,8,256]{2,1,0:T(8,128)S(1)}, u32[]{:S(2)}, u32[]{:S(2)}) %collective-permute-start.2) | collective-permute-done | bytes 24608 | tf_op jit(solution)/shard_map/ppermute | solution.py:50
  11.3 0.3 forcing_halo.1
  11.6 1.9 %collective-permute-start.5 = (f32[2,24,128]{2,1,0:T(8,128)S(1)}, f32[2,24,128]{2,1,0:T(8,128)S(1)}, u32[]{:S(2)}, u32[]{:S(2)}) collective-permute-start(f32[2,24,128]{2,1,0:T(8,128)S(1)} %pass_lon.1), channel_id=1, source_target_pairs={{0,8},{8,0},{16,24},{24,16},{1,9},{9,1},{17,25},{25,17},{2,10},{10... | collective-permute-start | bytes 73736 | tf_op jit(solution)/shard_map/ppermute | solution.py:50
  13.5 2.2 %collective-permute-start.6 = (f32[2,24,128]{2,1,0:T(8,128)S(1)}, f32[2,24,128]{2,1,0:T(8,128)S(1)}, u32[]{:S(2)}, u32[]{:S(2)}) collective-permute-start(f32[2,24,128]{2,1,0:T(8,128)S(1)} %get-tuple-element.58.second), channel_id=1, source_target_pairs={{8,16},{16,8},{24,0},{0,24},{9,17},{17,9},{25,1},{1,25},{10,18},{1... | collective-permute-start | bytes 73736 | tf_op jit(solution)/shard_map/ppermute | solution.py:50
  15.7 1.1 %hot.1 = bf16[64,128,256]{2,1,0:T(8,128)(2,1)S(1)} custom-call(s32[4,16,256]{2,1,0:T(8,128)S(1)} %get-tuple-element.44.points), custom_call_target="tpu_custom_call" | custom-call | bytes 1024 | tf_op jit(solution)/shard_map/hot/pallas_call | solution.py:80
  16.8 0.0 collective-permute-done.3.got_a
  16.8 0.0 collective-permute-done.4.got_b
  16.8 1.7 %before.1 = (f32[60,16,256]{2,1,0:T(8,128)S(1)}, f32[60,24,256]{2,1,0:T(8,128)S(1)}, f32[60,8,256]{2,1,0:T(8,128)S(1)}) custom-call(f32[7,24,256]{2,1,0:T(8,128)S(1)} %get-tuple-element.51.ext, f32[2,16,256]{2,1,0:T(8,128)S(1)} %get-tuple-element.52.light, f32[60,16,256]{2,1,0:T(8,128)S(1)} %copy-done, f32[15,8,256]{2,1,0:T(8,128)S(1)} %collective-permute-done.3.got_a, ...), custom_call_target="tpu_custom_call" | custom-call | bytes 1024 | tf_op jit(solution)/shard_map/before/pallas_call | solution.py:80
  18.5 0.0 collective-permute-done.5.got_a
  18.5 0.0 collective-permute-done.6.got_b
  18.5 3.0 %subcycles.1 = (f32[16,256]{1,0:T(8,128)S(1)}, f32[16,256]{1,0:T(8,128)S(1)}, f32[16,256]{1,0:T(8,128)S(1)}, f32[4,16,256]{2,1,0:T(8,128)S(1)}, f32[4,16,256]{2,...) custom-call(f32[7,24,256]{2,1,0:T(8,128)S(1)} %get-tuple-element.51., ...), custom_call_target="tpu_custom_call" | custom-call | flops 2990000128 | bytes 1024 | tf_op jit(solution)/shard_map/subcycles/pallas_call | solution.py:80
  21.5 3.8 %collective-permute-start.8 = (f32[5,8,128]{2,1,0:T(8,128)S(1)}, f32[5,8,128]{2,1,0:T(8,128)S(1)}, u32[]{:S(2)}, u32[]{:S(2)}) collective-permute-start(f32[5,8,128]{2,1,0:T(8,128)S(1)} %get-tuple-element.71.second), channel_id=1, source_target_pairs={{1,2},{2,1},{3,4},{4,3},{5,6},{6,5},{9,10},{10,9},{11,12},{12,11},... | collective-permute-start | bytes 61448 | tf_op jit(solution)/shard_map/ppermute | solution.py:50
  25.4 0.1 collective-permute-start.7
  25.5 1.6 %tracer.1 = (f32[16,256]{1,0:T(8,128)}, f32[16,256]{1,0:T(8,128)}, f32[16,256]{1,0:T(8,128)}, f32[60,16,256]{2,1,0:T(8,128)}, f32[60,16,256]{2,1,0:T(8,128)S(1)}) custom-call(f32[60,16,256]{2,1,0:T(8,128)S(1)} %copy-done, f32[60,8,256]{2,1,0:T(8,128)S(1)} %get-tuple-element.53.halo, f32[60,16,256]{2,1,0:T(8,128)S(1)} %get-tuple-element.54.base, ...), custom_call_target="tpu_custom_call" | custom-call | flops 2875000064 | bytes 1024 | tf_op jit(solution)/shard_map/tracer/pallas_call | solution.py:80
  27.1 0.0 collective-permute-done.7.got_a
  27.1 0.0 collective-permute-done.8.got_b
  27.1 0.7 %merge.1 = (f32[4,8,128]{2,1,0:T(8,128)}, f32[60,16,256]{2,1,0:T(8,128)}) custom-call(f32[5,8,128]{2,1,0:T(8,128)S(1)} %get-tuple-element.69.mid, f32[5,8,128]{2,1,0:T(8,128)S(1)} %collective-permute-done.7.got_a, f32[5,8,128]{2,1,0:T(8,128)S(1)} %collective-permute-done.8.got_b, ...), custom_call_target="tpu_custom_call", output_to_operand_aliasing={{1}: (5, {})} | custom-call | flops 115000000 | bytes 1024 | tf_op jit(solution)/shard_map/merge/pallas_call | solution.py:80
  (4 shorter events, 0.0 us)
Async XLA Ops:
  0.6 1.4 %copy-start = (f32[60,16,256]{2,1,0:T(8,128)S(1)}, f32[60,16,256]{2,1,0:T(8,128)}, u32[]{:S(2)}) copy-start(f32[60,16,256]{2,1,0:T(8,128)} %temp.11) | copy-start | bytes 2949124
  1.8 1.3 %collective-permute-start = (f32[9,8,256]{2,1,0:T(8,128)S(1)}, f32[9,8,256]{2,1,0:T(8,128)S(1)}, u32[]{:S(2)}, u32[]{:S(2)}) collective-permute-start(f32[9,8,256]{2,1,0:T(8,128)S(1)} %get-tuple-element.41), channel_id=1, source_target_pairs={{0,1},{1,0},{2,3},{3,2},{4,5},{5,4},{6,7},{7,6},{8,9},{9,8},{10,11... | collective-permute-start | bytes 221192 | tf_op jit(solution)/shard_map/ppermute | solution.py:50
  3.2 6.8 %collective-permute-start.1 = (f32[11,8,256]{2,1,0:T(8,128)S(1)}, f32[11,8,256]{2,1,0:T(8,128)S(1)}, u32[]{:S(2)}, u32[]{:S(2)}) collective-permute-start(f32[11,8,256]{2,1,0:T(8,128)S(1)} %pack_flux.1.other), channel_id=1, source_target_pairs={{1,2},{2,1},{3,4},{4,3},{5,6},{6,5},{9,10},{10,9},{11,12},{12,11},... | collective-permute-start | bytes 270344 | tf_op jit(solution)/shard_map/ppermute | solution.py:50
  7.8 9.0 %collective-permute-start.4 = (f32[15,8,256]{2,1,0:T(8,128)S(1)}, f32[15,8,256]{2,1,0:T(8,128)S(1)}, u32[]{:S(2)}, u32[]{:S(2)}) collective-permute-start(f32[15,8,256]{2,1,0:T(8,128)S(1)} %pack_temp_b.1.other), channel_id=1, source_target_pairs={{1,2},{2,1},{3,4},{4,3},{5,6},{6,5},{9,10},{10,9},{11,12},{12,11},... | collective-permute-start | bytes 368648 | tf_op jit(solution)/shard_map/ppermute | solution.py:50
  9.8 7.0 %collective-permute-start.3 = (f32[15,8,256]{2,1,0:T(8,128)S(1)}, f32[15,8,256]{2,1,0:T(8,128)S(1)}, u32[]{:S(2)}, u32[]{:S(2)}) collective-permute-start(f32[15,8,256]{2,1,0:T(8,128)S(1)} %pack_temp_a.1), channel_id=1, source_target_pairs={{0,1},{1,0},{2,3},{3,2},{4,5},{5,4},{6,7},{7,6},{8,9},{9,8},{10,11... | collective-permute-start | bytes 368648 | tf_op jit(solution)/shard_map/ppermute | solution.py:50
  10.0 1.3 %collective-permute-start.2 = (f32[3,8,256]{2,1,0:T(8,128)S(1)}, f32[3,8,256]{2,1,0:T(8,128)S(1)}, u32[]{:S(2)}, u32[]{:S(2)}) collective-permute-start(f32[3,8,256]{2,1,0:T(8,128)S(1)} %pack_c.1), channel_id=1, source_target_pairs={{0,1},{1,0},{2,3},{3,2},{4,5},{5,4},{6,7},{7,6},{8,9},{9,8},{10,11... | collective-permute-start | bytes 73736 | tf_op jit(solution)/shard_map/ppermute | solution.py:50
  11.6 7.0 %collective-permute-start.5 = (f32[2,24,128]{2,1,0:T(8,128)S(1)}, f32[2,24,128]{2,1,0:T(8,128)S(1)}, u32[]{:S(2)}, u32[]{:S(2)}) collective-permute-start(f32[2,24,128]{2,1,0:T(8,128)S(1)} %pass_lon.1), channel_id=1, source_target_pairs={{0,8},{8,0},{16,24},{24,16},{1,9},{9,1},{17,25},{25,17},{2,10},{10... | collective-permute-start | bytes 73736 | tf_op jit(solution)/shard_map/ppermute | solution.py:50
  13.5 5.0 %collective-permute-start.6 = (f32[2,24,128]{2,1,0:T(8,128)S(1)}, f32[2,24,128]{2,1,0:T(8,128)S(1)}, u32[]{:S(2)}, u32[]{:S(2)}) collective-permute-start(f32[2,24,128]{2,1,0:T(8,128)S(1)} %get-tuple-element.58.second), channel_id=1, source_target_pairs={{8,16},{16,8},{24,0},{0,24},{9,17},{17,9},{25,1},{1,25},{10,18},{1... | collective-permute-start | bytes 73736 | tf_op jit(solution)/shard_map/ppermute | solution.py:50
  21.5 5.6 %collective-permute-start.8 = (f32[5,8,128]{2,1,0:T(8,128)S(1)}, f32[5,8,128]{2,1,0:T(8,128)S(1)}, u32[]{:S(2)}, u32[]{:S(2)}) collective-permute-start(f32[5,8,128]{2,1,0:T(8,128)S(1)} %get-tuple-element.71.second), channel_id=1, source_target_pairs={{1,2},{2,1},{3,4},{4,3},{5,6},{6,5},{9,10},{10,9},{11,12},{12,11},... | collective-permute-start | bytes 61448 | tf_op jit(solution)/shard_map/ppermute | solution.py:50
  25.4 1.7 %collective-permute-start.7 = (f32[5,8,128]{2,1,0:T(8,128)S(1)}, f32[5,8,128]{2,1,0:T(8,128)S(1)}, u32[]{:S(2)}, u32[]{:S(2)}) collective-permute-start(f32[5,8,128]{2,1,0:T(8,128)S(1)} %pass_sums.1), channel_id=1, source_target_pairs={{0,1},{1,0},{2,3},{3,2},{4,5},{5,4},{6,7},{7,6},{8,9},{9,8},{10,11... | collective-permute-start | bytes 61448 | tf_op jit(solution)/shard_map/ppermute | solution.py:50

commit v9 on v8

--- a/solution.py
+++ b/solution.py
@@ -718,6 +718,7 @@
     groups = levels // level_step(levels)
     place = lax.axis_index("lat")
     inner = jnp.where(lax.rem(place, 2) == 1, groups // 5, 0)
+    inner = jnp.where(place == 2, groups // 10, inner)
     return jnp.where(place == 0, groups * 7 // 10, jnp.where(place == 1, groups // 2, inner))
 
 

time: 28.2 us -> 28.3 us (level)
  starting transfers between devices: 15.1 us -> 15.4 us
where the time goes in v9:
time: 28.3 us; the launch traced here: 28.1 us
  starting transfers between devices  15.4 us (54%)
  Pallas kernels  10.4 us (37%)
  waiting for transfers between devices  1.45 us (5%)
  between operations  0.81 us (3%)
    ppermute x9, starting transfers between devices, swap(): lax.ppermute(array, axis, swap_pairs(lax.axis_size(axis), first, periodic))  15.4 us
    pallas_call x15, Pallas kernels, call(): pl.pallas_call(body, out_shape=outs, in_specs=specs, out_specs=[pl.BlockS...  10.4 us
    ppermute x9, waiting for transfers between devices, swap(): lax.ppermute(array, axis, swap_pairs(lax.axis_size(axis), first, periodic))  1.45 us
  transfers between devices with their start and end apart: 9, of which 3 were waited for; matrix products, arithmetic and copies ran while one was open for 0% of the time, Pallas kernels for 20%

profile of v9, /device:TPU:1, one launch (start us, length us, event | category | flops | bytes accessed | tf_op | source)
XLA Modules:
  0.0 28.1 jit_solution(8825438991773822298)
XLA Ops:
  0.6 0.0 copy-start
  0.6 1.2 %load.1 = (f32[9,8,256]{2,1,0:T(8,128)S(1)}, f32[5,8,128]{2,1,0:T(8,128)S(1)}, f32[4,16,256]{2,1,0:T(8,128)S(1)}, s32[4,16,256]{2,1,0:T(8,128)S(1)}, f32[4,16,25...) custom-call(f32[16,256]{1,0:T(8,128)} %height.1, f32[16,256]{1,0:T(8,128)} %zonal.1, ...), custom_call_target="tpu_custom_call" | custom-call | flops 1840000000 | bytes 1024 | tf_op jit(solution)/shard_map/load/pallas_call | solution.py:80
  1.8 0.1 collective-permute-start
  1.9 0.1 copy-done
  2.0 0.3 %pack_b.1 = (f32[11,8,256]{2,1,0:T(8,128)S(1)}, f32[2,16,128]{2,1,0:T(8,128)S(1)}, f32[2,8,128]{2,1,0:T(8,128)S(1)}) custom-call(f32[5,8,128]{2,1,0:T(8,128)S(1)} %get-tuple-element.42.own, f32[4,16,256]{2,1,0:T(8,128)S(1)} %get-tuple-element.43.state, s32[4,16,256]{2,1,0:T(8,128)S(1)} %get-tuple-element.44.points, ...), custom_call_target="tpu_custom_call" | custom-call | flops 345000000 | bytes 1024 | tf_op jit(solution)/shard_map/pack_b/pallas_call | solution.py:80
  2.3 0.8 %collective-permute-done.received.got_a = f32[9,8,256]{2,1,0:T(8,128)S(1)} collective-permute-done((f32[9,8,256]{2,1,0:T(8,128)S(1)}, f32[9,8,256]{2,1,0:T(8,128)S(1)}, u32[]{:S(2)}, u32[]{:S(2)}) %collective-permute-start) | collective-permute-done | bytes 73760 | tf_op jit(solution)/shard_map/ppermute | solution.py:50
  3.2 4.5 %collective-permute-start.1 = (f32[11,8,256]{2,1,0:T(8,128)S(1)}, f32[11,8,256]{2,1,0:T(8,128)S(1)}, u32[]{:S(2)}, u32[]{:S(2)}) collective-permute-start(f32[11,8,256]{2,1,0:T(8,128)S(1)} %pack_flux.1.other), channel_id=1, source_target_pairs={{1,2},{2,1},{3,4},{4,3},{5,6},{6,5},{9,10},{10,9},{11,12},{12,11},... | collective-permute-start | bytes 270344 | tf_op jit(solution)/shard_map/ppermute | solution.py:50
  7.7 0.1 pack_temp_b.1.other
  7.8 0.1 pack_temp_a.1
  7.8 1.9 %collective-permute-start.4 = (f32[15,8,256]{2,1,0:T(8,128)S(1)}, f32[15,8,256]{2,1,0:T(8,128)S(1)}, u32[]{:S(2)}, u32[]{:S(2)}) collective-permute-start(f32[15,8,256]{2,1,0:T(8,128)S(1)} %pack_temp_b.1.other), channel_id=1, source_target_pairs={{1,2},{2,1},{3,4},{4,3},{5,6},{6,5},{9,10},{10,9},{11,12},{12,11},... | collective-permute-start | bytes 368648 | tf_op jit(solution)/shard_map/ppermute | solution.py:50
  9.8 0.1 collective-permute-start.3
  9.8 0.1 collective-permute-done.1.got_b.received
  10.0 0.5 %collective-permute-start.2 = (f32[3,8,256]{2,1,0:T(8,128)S(1)}, f32[3,8,256]{2,1,0:T(8,128)S(1)}, u32[]{:S(2)}, u32[]{:S(2)}) collective-permute-start(f32[3,8,256]{2,1,0:T(8,128)S(1)} %pack_c.1), channel_id=1, source_target_pairs={{0,1},{1,0},{2,3},{3,2},{4,5},{5,4},{6,7},{7,6},{8,9},{9,8},{10,11... | collective-permute-start | bytes 73736 | tf_op jit(solution)/shard_map/ppermute | solution.py:50
  10.4 0.4 %forcing.1 = (f32[7,24,256]{2,1,0:T(8,128)S(1)}, f32[2,16,256]{2,1,0:T(8,128)S(1)}) custom-call(f32[9,8,256]{2,1,0:T(8,128)S(1)} %collective-permute-done.received.got_a, f32[11,8,256]{2,1,0:T(8,128)S(1)} %collective-permute-done.1.got_b.received, f32[5,8,128]{2,1,0:T(8,128)S(1)} %get-tuple-element.42.own, f32[2,8,128]{2,1,0:T(8,128)S(1)} %get-tuple-element.49.numbers, ...), custom_call_target="tpu_custom_call" | custom-call | flops 460000000 | bytes 1024 | tf_op jit(solution)/shard_map/forcing/pallas_call | solution.py:80
  10.8 0.5 %collective-permute-done.2.got_c = f32[3,8,256]{2,1,0:T(8,128)S(1)} collective-permute-done((f32[3,8,256]{2,1,0:T(8,128)S(1)}, f32[3,8,256]{2,1,0:T(8,128)S(1)}, u32[]{:S(2)}, u32[]{:S(2)}) %collective-permute-start.2) | collective-permute-done | bytes 24608 | tf_op jit(solution)/shard_map/ppermute | solution.py:50
  11.3 0.3 forcing_halo.1
  11.6 1.9 %collective-permute-start.5 = (f32[2,24,128]{2,1,0:T(8,128)S(1)}, f32[2,24,128]{2,1,0:T(8,128)S(1)}, u32[]{:S(2)}, u32[]{:S(2)}) collective-permute-start(f32[2,24,128]{2,1,0:T(8,128)S(1)} %pass_lon.1), channel_id=1, source_target_pairs={{0,8},{8,0},{16,24},{24,16},{1,9},{9,1},{17,25},{25,17},{2,10},{10... | collective-permute-start | bytes 73736 | tf_op jit(solution)/shard_map/ppermute | solution.py:50
  13.5 2.2 %collective-permute-start.6 = (f32[2,24,128]{2,1,0:T(8,128)S(1)}, f32[2,24,128]{2,1,0:T(8,128)S(1)}, u32[]{:S(2)}, u32[]{:S(2)}) collective-permute-start(f32[2,24,128]{2,1,0:T(8,128)S(1)} %get-tuple-element.58.second), channel_id=1, source_target_pairs={{8,16},{16,8},{24,0},{0,24},{9,17},{17,9},{25,1},{1,25},{10,18},{1... | collective-permute-start | bytes 73736 | tf_op jit(solution)/shard_map/ppermute | solution.py:50
  15.7 1.1 %hot.1 = bf16[64,128,256]{2,1,0:T(8,128)(2,1)S(1)} custom-call(s32[4,16,256]{2,1,0:T(8,128)S(1)} %get-tuple-element.44.points), custom_call_target="tpu_custom_call" | custom-call | bytes 1024 | tf_op jit(solution)/shard_map/hot/pallas_call | solution.py:80
  16.8 0.0 collective-permute-done.3.got_a
  16.8 0.0 collective-permute-done.4.got_b
  16.8 1.7 %before.1 = (f32[60,16,256]{2,1,0:T(8,128)S(1)}, f32[60,24,256]{2,1,0:T(8,128)S(1)}, f32[60,8,256]{2,1,0:T(8,128)S(1)}) custom-call(f32[7,24,256]{2,1,0:T(8,128)S(1)} %get-tuple-element.51.ext, f32[2,16,256]{2,1,0:T(8,128)S(1)} %get-tuple-element.52.light, f32[60,16,256]{2,1,0:T(8,128)S(1)} %copy-done, f32[15,8,256]{2,1,0:T(8,128)S(1)} %collective-permute-done.3.got_a, ...), custom_call_target="tpu_custom_call" | custom-call | bytes 1024 | tf_op jit(solution)/shard_map/before/pallas_call | solution.py:80
  18.5 0.0 collective-permute-done.5.got_a
  18.5 0.0 collective-permute-done.6.got_b
  18.5 3.0 %subcycles.1 = (f32[16,256]{1,0:T(8,128)S(1)}, f32[16,256]{1,0:T(8,128)S(1)}, f32[16,256]{1,0:T(8,128)S(1)}, f32[4,16,256]{2,1,0:T(8,128)S(1)}, f32[4,16,256]{2,...) custom-call(f32[7,24,256]{2,1,0:T(8,128)S(1)} %get-tuple-element.51., ...), custom_call_target="tpu_custom_call" | custom-call | flops 2990000128 | bytes 1024 | tf_op jit(solution)/shard_map/subcycles/pallas_call | solution.py:80
  21.5 4.1 %collective-permute-start.8 = (f32[5,8,128]{2,1,0:T(8,128)S(1)}, f32[5,8,128]{2,1,0:T(8,128)S(1)}, u32[]{:S(2)}, u32[]{:S(2)}) collective-permute-start(f32[5,8,128]{2,1,0:T(8,128)S(1)} %get-tuple-element.71.second), channel_id=1, source_target_pairs={{1,2},{2,1},{3,4},{4,3},{5,6},{6,5},{9,10},{10,9},{11,12},{12,11},... | collective-permute-start | bytes 61448 | tf_op jit(solution)/shard_map/ppermute | solution.py:50
  25.7 0.1 collective-permute-start.7
  25.7 1.6 %tracer.1 = (f32[16,256]{1,0:T(8,128)}, f32[16,256]{1,0:T(8,128)}, f32[16,256]{1,0:T(8,128)}, f32[60,16,256]{2,1,0:T(8,128)}, f32[60,16,256]{2,1,0:T(8,128)S(1)}) custom-call(f32[60,16,256]{2,1,0:T(8,128)S(1)} %copy-done, f32[60,8,256]{2,1,0:T(8,128)S(1)} %get-tuple-element.53.halo, f32[60,16,256]{2,1,0:T(8,128)S(1)} %get-tuple-element.54.base, ...), custom_call_target="tpu_custom_call" | custom-call | flops 2875000064 | bytes 1024 | tf_op jit(solution)/shard_map/tracer/pallas_call | solution.py:80
  27.4 0.0 collective-permute-done.7.got_a
  27.4 0.0 collective-permute-done.8.got_b
  27.4 0.7 %merge.1 = (f32[4,8,128]{2,1,0:T(8,128)}, f32[60,16,256]{2,1,0:T(8,128)}) custom-call(f32[5,8,128]{2,1,0:T(8,128)S(1)} %get-tuple-element.69.mid, f32[5,8,128]{2,1,0:T(8,128)S(1)} %collective-permute-done.7.got_a, f32[5,8,128]{2,1,0:T(8,128)S(1)} %collective-permute-done.8.got_b, ...), custom_call_target="tpu_custom_call", output_to_operand_aliasing={{1}: (5, {})} | custom-call | flops 115000000 | bytes 1024 | tf_op jit(solution)/shard_map/merge/pallas_call | solution.py:80
  (4 shorter events, 0.0 us)
Async XLA Ops:
  0.6 1.4 %copy-start = (f32[60,16,256]{2,1,0:T(8,128)S(1)}, f32[60,16,256]{2,1,0:T(8,128)}, u32[]{:S(2)}) copy-start(f32[60,16,256]{2,1,0:T(8,128)} %temp.11) | copy-start | bytes 2949124
  1.8 1.3 %collective-permute-start = (f32[9,8,256]{2,1,0:T(8,128)S(1)}, f32[9,8,256]{2,1,0:T(8,128)S(1)}, u32[]{:S(2)}, u32[]{:S(2)}) collective-permute-start(f32[9,8,256]{2,1,0:T(8,128)S(1)} %get-tuple-element.41), channel_id=1, source_target_pairs={{0,1},{1,0},{2,3},{3,2},{4,5},{5,4},{6,7},{7,6},{8,9},{9,8},{10,11... | collective-permute-start | bytes 221192 | tf_op jit(solution)/shard_map/ppermute | solution.py:50
  3.2 6.8 %collective-permute-start.1 = (f32[11,8,256]{2,1,0:T(8,128)S(1)}, f32[11,8,256]{2,1,0:T(8,128)S(1)}, u32[]{:S(2)}, u32[]{:S(2)}) collective-permute-start(f32[11,8,256]{2,1,0:T(8,128)S(1)} %pack_flux.1.other), channel_id=1, source_target_pairs={{1,2},{2,1},{3,4},{4,3},{5,6},{6,5},{9,10},{10,9},{11,12},{12,11},... | collective-permute-start | bytes 270344 | tf_op jit(solution)/shard_map/ppermute | solution.py:50
  7.8 9.0 %collective-permute-start.4 = (f32[15,8,256]{2,1,0:T(8,128)S(1)}, f32[15,8,256]{2,1,0:T(8,128)S(1)}, u32[]{:S(2)}, u32[]{:S(2)}) collective-permute-start(f32[15,8,256]{2,1,0:T(8,128)S(1)} %pack_temp_b.1.other), channel_id=1, source_target_pairs={{1,2},{2,1},{3,4},{4,3},{5,6},{6,5},{9,10},{10,9},{11,12},{12,11},... | collective-permute-start | bytes 368648 | tf_op jit(solution)/shard_map/ppermute | solution.py:50
  9.8 7.0 %collective-permute-start.3 = (f32[15,8,256]{2,1,0:T(8,128)S(1)}, f32[15,8,256]{2,1,0:T(8,128)S(1)}, u32[]{:S(2)}, u32[]{:S(2)}) collective-permute-start(f32[15,8,256]{2,1,0:T(8,128)S(1)} %pack_temp_a.1), channel_id=1, source_target_pairs={{0,1},{1,0},{2,3},{3,2},{4,5},{5,4},{6,7},{7,6},{8,9},{9,8},{10,11... | collective-permute-start | bytes 368648 | tf_op jit(solution)/shard_map/ppermute | solution.py:50
  10.0 1.3 %collective-permute-start.2 = (f32[3,8,256]{2,1,0:T(8,128)S(1)}, f32[3,8,256]{2,1,0:T(8,128)S(1)}, u32[]{:S(2)}, u32[]{:S(2)}) collective-permute-start(f32[3,8,256]{2,1,0:T(8,128)S(1)} %pack_c.1), channel_id=1, source_target_pairs={{0,1},{1,0},{2,3},{3,2},{4,5},{5,4},{6,7},{7,6},{8,9},{9,8},{10,11... | collective-permute-start | bytes 73736 | tf_op jit(solution)/shard_map/ppermute | solution.py:50
  11.6 7.0 %collective-permute-start.5 = (f32[2,24,128]{2,1,0:T(8,128)S(1)}, f32[2,24,128]{2,1,0:T(8,128)S(1)}, u32[]{:S(2)}, u32[]{:S(2)}) collective-permute-start(f32[2,24,128]{2,1,0:T(8,128)S(1)} %pass_lon.1), channel_id=1, source_target_pairs={{0,8},{8,0},{16,24},{24,16},{1,9},{9,1},{17,25},{25,17},{2,10},{10... | collective-permute-start | bytes 73736 | tf_op jit(solution)/shard_map/ppermute | solution.py:50
  13.5 5.0 %collective-permute-start.6 = (f32[2,24,128]{2,1,0:T(8,128)S(1)}, f32[2,24,128]{2,1,0:T(8,128)S(1)}, u32[]{:S(2)}, u32[]{:S(2)}) collective-permute-start(f32[2,24,128]{2,1,0:T(8,128)S(1)} %get-tuple-element.58.second), channel_id=1, source_target_pairs={{8,16},{16,8},{24,0},{0,24},{9,17},{17,9},{25,1},{1,25},{10,18},{1... | collective-permute-start | bytes 73736 | tf_op jit(solution)/shard_map/ppermute | solution.py:50
  21.5 5.9 %collective-permute-start.8 = (f32[5,8,128]{2,1,0:T(8,128)S(1)}, f32[5,8,128]{2,1,0:T(8,128)S(1)}, u32[]{:S(2)}, u32[]{:S(2)}) collective-permute-start(f32[5,8,128]{2,1,0:T(8,128)S(1)} %get-tuple-element.71.second), channel_id=1, source_target_pairs={{1,2},{2,1},{3,4},{4,3},{5,6},{6,5},{9,10},{10,9},{11,12},{12,11},... | collective-permute-start | bytes 61448 | tf_op jit(solution)/shard_map/ppermute | solution.py:50
  25.7 1.7 %collective-permute-start.7 = (f32[5,8,128]{2,1,0:T(8,128)S(1)}, f32[5,8,128]{2,1,0:T(8,128)S(1)}, u32[]{:S(2)}, u32[]{:S(2)}) collective-permute-start(f32[5,8,128]{2,1,0:T(8,128)S(1)} %pass_sums.1), channel_id=1, source_target_pairs={{0,1},{1,0},{2,3},{3,2},{4,5},{5,4},{6,7},{7,6},{8,9},{9,8},{10,11... | collective-permute-start | bytes 61448 | tf_op jit(solution)/shard_map/ppermute | solution.py:50
